TPU v7x, 32 devices: a whole 2x2x4 slice. The times are simulated.
32 devices in a mesh: blocks: 8 (over y, x, core), group: 4 (over z).
Axes of the slice: x: 2, y: 2, z: 4, core: 2. Of those that a mesh axis runs over, the one named last changes fastest.
Arguments:
- ocean_state: float32 [36, 4, 64, 512], P(None, None, 'blocks', 'group'), may hold values from -6 to 6
- surface_height: float32 [64, 512], P('blocks', 'group'), may hold values from -6 to 6
- surface_damping: float32 [64, 512], P('blocks', 'group'), may hold values from 0.05 to 1
- land_mask: int32 [64, 512], P('blocks', 'group'), may hold values from 0 to 1, as said below
Outputs:
- new_state: float32 [36, 4, 64, 512], P(None, None, 'blocks', 'group')
- surface: float32 [64, 512], P('blocks', 'group')
Inputs may be any that keep to these rules, and one draw needn't show every extreme that they name: `land_mask`: 1 marks an ocean cell.
All inputs are finite; a program needn't handle non-finite values.
Results may differ from a plain program's by a relative error of at most 0.0003.
Values sent between devices are 32-bit elements; how exact they have to be, the bound alone decides.
No kernel may reach another device: no remote copies, remote signals or barrier semaphores. Data moves between devices by JAX's collectives and lax.ppermute only.
A program may use at most 64 MiB of HBM per device.

v0:
```python
import jax
import jax.numpy as jnp
from jax import lax
from jax.sharding import PartitionSpec as P

ITERS = 3


time_step = 0.25
hyper_visc = 0.025
mixing = 0.2
gravity = 4.0
rotation = 0.2


def padded_2(shard, sides, width):
    for axis, dim in sides:
        count, length = (lax.axis_size(axis), shard.shape[dim])
        up = [(i, (i + 1) % count) for i in range(count - 1)]
        down = [(j, i) for i, j in up]
        last = lax.slice_in_dim(shard, length - width, length, axis=dim)
        initial = lax.slice_in_dim(shard, 0, width, axis=dim)
        before = lax.ppermute(last, axis, up)
        after = lax.ppermute(initial, axis, down)
        shard = jnp.concatenate([before, shard, after], axis=dim)
    return shard


def laplace(padded):
    return (
        padded[..., 2:, 1:-1]
        + padded[..., :-2, 1:-1]
        + padded[..., 1:-1, 2:]
        + padded[..., 1:-1, :-2]
        - 4.0 * padded[..., 1:-1, 1:-1]
    )


def on_device(ocean_state, surface_height, surface_damping, land_mask):
    sea_mask = land_mask.astype(jnp.float32)
    masked = ocean_state * sea_mask
    rows_dev, cols_dev = sea_mask.shape
    total_rows = rows_dev * lax.axis_size("blocks")
    total_cols = cols_dev * lax.axis_size("group")
    first_row = lax.axis_index("blocks") * rows_dev
    first_col = lax.axis_index("group") * cols_dev
    padded = padded_2(masked, (("blocks", 2), ("group", 3)), 2)
    lap_cycle = laplace(padded)
    row_pos = first_row - 1 + jnp.arange(rows_dev + 2, dtype=jnp.int32)
    col_pos = first_col - 1 + jnp.arange(cols_dev + 2, dtype=jnp.int32)
    inside = ((row_pos >= 0) & (row_pos < total_rows))[:, None] & (
        (col_pos >= 0) & (col_pos < total_cols)
    )[None, :]
    biharm = laplace(jnp.where(inside, lap_cycle, 0.0))
    near_cycle = padded[..., 1:-1, 1:-1]
    slope_east = 0.5 * (near_cycle[..., 2:, 1:-1] - near_cycle[..., :-2, 1:-1])
    slope_north = 0.5 * (near_cycle[..., 1:-1, 2:] - near_cycle[..., 1:-1, :-2])
    east_flow = masked[:, 2:3]
    north_flow = masked[:, 3:4]
    advect = east_flow * slope_east + north_flow * slope_north
    above_level = jnp.concatenate([masked[:1], masked[:-1]], axis=0)
    below_level = jnp.concatenate([masked[1:], masked[-1:]], axis=0)
    vertical = above_level + below_level - 2.0 * masked
    col_index = (first_col + jnp.arange(cols_dev, dtype=jnp.int32)).astype(jnp.float32)
    coriolis = rotation * (2.0 * (col_index + 0.5) / total_cols - 1.0)
    zeros_two = jnp.zeros_like(masked[:, 0:2])
    rotated = jnp.concatenate([zeros_two, coriolis * north_flow, -coriolis * east_flow], axis=1)
    updated = masked + time_step * (rotated - advect) - hyper_visc * biharm + mixing * vertical
    new_state = sea_mask * updated
    transport = jnp.sum(new_state[:, 2:4], axis=0) / new_state.shape[0]
    surface_pad = padded_2(transport, (("blocks", 1), ("group", 2)), 1)
    divergence = 0.5 * (
        surface_pad[0, 2:, 1:-1]
        - surface_pad[0, :-2, 1:-1]
        + surface_pad[1, 1:-1, 2:]
        - surface_pad[1, 1:-1, :-2]
    )
    right_side = sea_mask * (surface_damping * surface_height - gravity * divergence)
    solution = jnp.zeros_like(right_side)

    def global_total(value):
        part_sum = lax.psum(value, "blocks")
        return lax.psum(part_sum, "group")

    residual = right_side
    direction = right_side
    norm_now = global_total(jnp.sum(residual * residual))
    for iteration in range(ITERS):
        padded_field = padded_2(direction, (("blocks", 0), ("group", 1)), 1)
        beside = (
            padded_field[2:, 1:-1]
            + padded_field[:-2, 1:-1]
            + padded_field[1:-1, 2:]
            + padded_field[1:-1, :-2]
        )
        applied = sea_mask * ((4.0 + surface_damping) * direction - beside)
        step_size = norm_now / global_total(jnp.sum(direction * applied))
        solution = solution + step_size * direction
        if iteration + 1 < ITERS:
            residual = residual - step_size * applied
            norm_next = global_total(jnp.sum(residual * residual))
            direction = residual + norm_next / norm_now * direction
            norm_now = norm_next
    return (new_state, solution)


def solution(mesh):
    placed = (
        P(None, None, "blocks", "group"),
        P("blocks", "group"),
        P("blocks", "group"),
        P("blocks", "group"),
    )
    return jax.shard_map(
        on_device,
        mesh=mesh,
        in_specs=placed,
        out_specs=(P(None, None, "blocks", "group"), P("blocks", "group")),
        check_vma=False,
    )
```

profile of v0, /device:TPU:0, one launch (start us, length us, event | category | flops | bytes accessed | tf_op | source)
XLA Modules:
  0.0 218.8 jit_solution(13714373210834754403)
XLA Ops:
  1.3 1.4 copy_multiply_fusion
  2.8 1.3 collective-permute-start
  4.1 3.0 %collective-permute-start.1 = (f32[36,4,2,128]{3,0,2,1:T(8,128)S(1)}, f32[36,4,2,128]{3,0,2,1:T(8,128)S(1)}, u32[]{:S(2)}, u32[]{:S(2)}) collective-permute-start(f32[36,4,2,128]{3,0,2,1:T(8,128)S(1)} %get-tuple-element.25), channel_id=1, source_target_pairs={{0,4},{4,8},{8,12},{12,16},{16,20},{20,24},{24,28},{1,5},{5,9},{9,... | collective-permute-start | bytes 442376 | tf_op jit(solution)/shard_map/ppermute | solution.py:23
  10.2 4.9 %collective-permute-start.3 = (f32[36,4,12,2]{0,2,3,1:T(8,128)S(1)}, f32[36,4,12,2]{0,2,3,1:T(8,128)S(1)}, u32[]{:S(2)}, u32[]{:S(2)}) collective-permute-start(f32[36,4,12,2]{0,2,3,1:T(8,128)S(1)} %copy.9), channel_id=1, source_target_pairs={{0,1},{1,2},{2,3},{4,5},{5,6},{6,7},{8,9},{9,10},{10,11},{12,13},{... | collective-permute-start | bytes 41480 | tf_op jit(solution)/shard_map/ppermute | solution.py:23
  15.6 1.3 collective-permute-start.2
  17.8 4.7 %collective-permute-done.2 = f32[36,4,12,2]{0,2,3,1:T(8,128)S(1)} collective-permute-done((f32[36,4,12,2]{0,2,3,1:T(8,128)S(1)}, f32[36,4,12,2]{0,2,3,1:T(8,128)S(1)}, u32[]{:S(2)}, u32[]{:S(2)}) %collective-permute-start.2) | collective-permute-done | bytes 13856 | tf_op jit(solution)/shard_map/ppermute | solution.py:24
  23.8 1.8 fusion.1
  25.7 2.3 %fusion.8 = f32[36,4,8,128]{3,0,2,1:T(8,128)S(1)} fusion(f32[36,4,10,130]{3,0,2,1:T(8,128)S(1)} %fusion.1, f32[36,4,8,128]{3,0,2,1:T(8,128)S(1)} %copy_multiply_fusion, f32[36,4,12,2]{3,0,2,1:T(8,128)S(1)} %copy.10, f32[36,4,2,128]{3,0,2,1:T(8,128)S(1)} %collective-permute-done, f32[36,4,2,128]{3,0,2,1:T(8,128)} %copy-done.2, f32[36,4,12,2]{3,0,2,1:T(8,128)S(1)} %copy.8, ...), kind=kLoop, calls=%fused_computation.19 | loop fusion | flops 4866048 | bytes 6224912 | tf_op jit(solution)/shard_map/mul | solution.py:69
  28.1 1.3 collective-permute-start.4
  29.4 3.0 %collective-permute-start.5 = (f32[2,1,128]{2,1,0:T(1,128)S(1)}, f32[2,1,128]{2,1,0:T(1,128)S(1)}, u32[]{:S(2)}, u32[]{:S(2)}) collective-permute-start(f32[2,1,128]{2,1,0:T(1,128)S(1)} %get-tuple-element.35), channel_id=1, source_target_pairs={{0,4},{4,8},{8,12},{12,16},{16,20},{20,24},{24,28},{1,5},{5,9},{9,... | collective-permute-start | bytes 3080 | tf_op jit(solution)/shard_map/ppermute | solution.py:23
  34.6 4.5 %collective-permute-start.7 = (f32[2,10,1]{2,1,0:T(8,128)S(1)}, f32[2,10,1]{2,1,0:T(8,128)S(1)}, u32[]{:S(2)}, u32[]{:S(2)}) collective-permute-start(f32[2,10,1]{2,1,0:T(8,128)S(1)} %get-tuple-element.28), channel_id=1, source_target_pairs={{0,1},{1,2},{2,3},{4,5},{5,6},{6,7},{8,9},{9,10},{10,11},{12,13},{... | collective-permute-start | bytes 248 | tf_op jit(solution)/shard_map/ppermute | solution.py:23
  39.2 1.4 collective-permute-done.7
  42.0 3.8 %collective-permute-start.9 = (f32[1,128]{1,0:T(1,128)S(1)}, f32[1,128]{1,0:T(1,128)S(1)}, u32[]{:S(2)}, u32[]{:S(2)}) collective-permute-start(f32[1,128]{1,0:T(1,128)S(1)} %get-tuple-element.41), channel_id=1, source_target_pairs={{0,4},{4,8},{8,12},{12,16},{16,20},{20,24},{24,28},{1,5},{5,9},{9,... | collective-permute-start | bytes 1544 | tf_op jit(solution)/shard_map/ppermute | solution.py:23
  48.0 4.5 %collective-permute-start.11 = (f32[10,1]{1,0:T(8,128)S(1)}, f32[10,1]{1,0:T(8,128)S(1)}, u32[]{:S(2)}, u32[]{:S(2)}) collective-permute-start(f32[10,1]{1,0:T(8,128)S(1)} %get-tuple-element.34), channel_id=1, source_target_pairs={{0,1},{1,2},{2,3},{4,5},{5,6},{6,7},{8,9},{9,10},{10,11},{12,13},{... | collective-permute-start | bytes 128 | tf_op jit(solution)/shard_map/ppermute | solution.py:23
  52.6 1.3 collective-permute-done.11
  54.6 17.6 %all-reduce = (f32[]{:T(128)}, f32[]{:T(128)}) all-reduce(f32[]{:T(128)} %get-tuple-element.5, f32[]{:T(128)} %get-tuple-element.4), channel_id=1, replica_groups=mesh['blocks'=8,'group'=4] {'blocks'}, use_global_device_ids=true, to_apply=%region_2.3 | all-reduce | flops 2 | bytes 16 | tf_op jit(solution)/shard_map/psum | solution.py:82
  72.3 13.7 %all-reduce.1 = (f32[]{:T(128)}, f32[]{:T(128)}) all-reduce(f32[]{:T(128)} %get-tuple-element.6, f32[]{:T(128)} %get-tuple-element.7), channel_id=1, replica_groups=mesh['blocks'=8,'group'=4] {'group'}, use_global_device_ids=true, to_apply=%region_3.4 | all-reduce | flops 2 | bytes 16 | tf_op jit(solution)/shard_map/psum | solution.py:83
  87.9 12.4 %psum.88 = f32[]{:T(128)} all-reduce(f32[]{:T(128)} %get-tuple-element.12), channel_id=1, replica_groups=mesh['blocks'=8,'group'=4] {'blocks'}, use_global_device_ids=true, to_apply=%region_8.9 | all-reduce | flops 1 | bytes 8 | tf_op jit(solution)/shard_map/psum | solution.py:82
  100.3 9.0 %psum.89 = f32[]{:T(128)} all-reduce(f32[]{:T(128)} %psum.88), channel_id=1, replica_groups=mesh['blocks'=8,'group'=4] {'group'}, use_global_device_ids=true, to_apply=%region_9.10 | all-reduce | flops 1 | bytes 8 | tf_op jit(solution)/shard_map/psum | solution.py:83
  110.7 1.3 collective-permute-start.12
  112.0 3.0 %collective-permute-start.13 = (f32[1,128]{1,0:T(1,128)S(1)}, f32[1,128]{1,0:T(1,128)S(1)}, u32[]{:S(2)}, u32[]{:S(2)}) collective-permute-start(f32[1,128]{1,0:T(1,128)S(1)} %get-tuple-element.39), channel_id=1, source_target_pairs={{0,4},{4,8},{8,12},{12,16},{16,20},{20,24},{24,28},{1,5},{5,9},{9,... | collective-permute-start | bytes 1544 | tf_op jit(solution)/shard_map/ppermute | solution.py:23
  117.2 4.5 %collective-permute-start.15 = (f32[10,1]{1,0:T(8,128)S(1)}, f32[10,1]{1,0:T(8,128)S(1)}, u32[]{:S(2)}, u32[]{:S(2)}) collective-permute-start(f32[10,1]{1,0:T(8,128)S(1)} %get-tuple-element.32), channel_id=1, source_target_pairs={{0,1},{1,2},{2,3},{4,5},{5,6},{6,7},{8,9},{9,10},{10,11},{12,13},{... | collective-permute-start | bytes 128 | tf_op jit(solution)/shard_map/ppermute | solution.py:23
  121.7 1.3 collective-permute-done.15
  123.8 15.0 %psum.90 = f32[]{:T(128)} all-reduce(f32[]{:T(128)} %get-tuple-element.10), channel_id=1, replica_groups=mesh['blocks'=8,'group'=4] {'blocks'}, use_global_device_ids=true, to_apply=%region_11.12 | all-reduce | flops 1 | bytes 8 | tf_op jit(solution)/shard_map/psum | solution.py:82
  138.8 12.1 %psum.91 = f32[]{:T(128)} all-reduce(f32[]{:T(128)} %psum.90), channel_id=1, replica_groups=mesh['blocks'=8,'group'=4] {'group'}, use_global_device_ids=true, to_apply=%region_12.13 | all-reduce | flops 1 | bytes 8 | tf_op jit(solution)/shard_map/psum | solution.py:83
  152.8 12.4 %psum.92 = f32[]{:T(128)} all-reduce(f32[]{:T(128)} %multiply_reduce_fusion), channel_id=1, replica_groups=mesh['blocks'=8,'group'=4] {'blocks'}, use_global_device_ids=true, to_apply=%region_14.15 | all-reduce | flops 1 | bytes 8 | tf_op jit(solution)/shard_map/psum | solution.py:82
  165.2 9.4 %psum.93 = f32[]{:T(128)} all-reduce(f32[]{:T(128)} %psum.92), channel_id=1, replica_groups=mesh['blocks'=8,'group'=4] {'group'}, use_global_device_ids=true, to_apply=%region_15.16 | all-reduce | flops 1 | bytes 8 | tf_op jit(solution)/shard_map/psum | solution.py:83
  177.3 3.0 %collective-permute-start.17 = (f32[1,128]{1,0:T(1,128)S(1)}, f32[1,128]{1,0:T(1,128)S(1)}, u32[]{:S(2)}, u32[]{:S(2)}) collective-permute-start(f32[1,128]{1,0:T(1,128)S(1)} %get-tuple-element.37), channel_id=1, source_target_pairs={{0,4},{4,8},{8,12},{12,16},{16,20},{20,24},{24,28},{1,5},{5,9},{9,... | collective-permute-start | bytes 1544 | tf_op jit(solution)/shard_map/ppermute | solution.py:23
  182.5 4.5 %collective-permute-start.19 = (f32[10,1]{1,0:T(8,128)S(1)}, f32[10,1]{1,0:T(8,128)S(1)}, u32[]{:S(2)}, u32[]{:S(2)}) collective-permute-start(f32[10,1]{1,0:T(8,128)S(1)} %get-tuple-element.30), channel_id=1, source_target_pairs={{0,1},{1,2},{2,3},{4,5},{5,6},{6,7},{8,9},{9,10},{10,11},{12,13},{... | collective-permute-start | bytes 128 | tf_op jit(solution)/shard_map/ppermute | solution.py:23
  187.1 1.3 collective-permute-done.19
  189.1 14.8 %psum.94 = f32[]{:T(128)} all-reduce(f32[]{:T(128)} %fusion.22), channel_id=1, replica_groups=mesh['blocks'=8,'group'=4] {'blocks'}, use_global_device_ids=true, to_apply=%region_17.18 | all-reduce | flops 1 | bytes 8 | tf_op jit(solution)/shard_map/psum | solution.py:82
  204.9 11.9 %psum.95 = f32[]{:T(128)} all-reduce(f32[]{:T(128)} %psum.94), channel_id=1, replica_groups=mesh['blocks'=8,'group'=4] {'group'}, use_global_device_ids=true, to_apply=%region_18.19 | all-reduce | flops 1 | bytes 8 | tf_op jit(solution)/shard_map/psum | solution.py:83
  (83 shorter events, 22.5 us)
Async XLA Ops:
  2.8 6.4 %collective-permute-start = (f32[36,4,2,128]{3,0,2,1:T(8,128)S(1)}, f32[36,4,2,128]{3,0,2,1:T(8,128)S(1)}, u32[]{:S(2)}, u32[]{:S(2)}) collective-permute-start(f32[36,4,2,128]{3,0,2,1:T(8,128)S(1)} %get-tuple-element.26), channel_id=1, source_target_pairs={{4,0},{8,4},{12,8},{16,12},{20,16},{24,20},{28,24},{5,1},{9,5},{13... | collective-permute-start | bytes 442376 | tf_op jit(solution)/shard_map/ppermute | solution.py:24
  4.1 5.1 %collective-permute-start.1 = (f32[36,4,2,128]{3,0,2,1:T(8,128)S(1)}, f32[36,4,2,128]{3,0,2,1:T(8,128)S(1)}, u32[]{:S(2)}, u32[]{:S(2)}) collective-permute-start(f32[36,4,2,128]{3,0,2,1:T(8,128)S(1)} %get-tuple-element.25), channel_id=1, source_target_pairs={{0,4},{4,8},{8,12},{12,16},{16,20},{20,24},{24,28},{1,5},{5,9},{9,... | collective-permute-start | bytes 442376 | tf_op jit(solution)/shard_map/ppermute | solution.py:23
  9.2 14.5 %copy-start.2 = (f32[36,4,2,128]{3,0,2,1:T(8,128)}, f32[36,4,2,128]{3,0,2,1:T(8,128)S(1)}, u32[]{:S(2)}) copy-start(f32[36,4,2,128]{3,0,2,1:T(8,128)S(1)} %collective-permute-done.1) | copy-start | bytes 442372
  10.2 7.2 %collective-permute-start.3 = (f32[36,4,12,2]{0,2,3,1:T(8,128)S(1)}, f32[36,4,12,2]{0,2,3,1:T(8,128)S(1)}, u32[]{:S(2)}, u32[]{:S(2)}) collective-permute-start(f32[36,4,12,2]{0,2,3,1:T(8,128)S(1)} %copy.9), channel_id=1, source_target_pairs={{0,1},{1,2},{2,3},{4,5},{5,6},{6,7},{8,9},{9,10},{10,11},{12,13},{... | collective-permute-start | bytes 41480 | tf_op jit(solution)/shard_map/ppermute | solution.py:23
  15.6 6.8 %collective-permute-start.2 = (f32[36,4,12,2]{0,2,3,1:T(8,128)S(1)}, f32[36,4,12,2]{0,2,3,1:T(8,128)S(1)}, u32[]{:S(2)}, u32[]{:S(2)}) collective-permute-start(f32[36,4,12,2]{0,2,3,1:T(8,128)S(1)} %copy.7), channel_id=1, source_target_pairs={{1,0},{2,1},{3,2},{5,4},{6,5},{7,6},{9,8},{10,9},{11,10},{13,12},{... | collective-permute-start | bytes 41480 | tf_op jit(solution)/shard_map/ppermute | solution.py:24
  23.8 1.8 copy-start
  23.8 1.8 copy-start.1
  23.8 1.8 copy-start.3
  23.8 1.8 copy-start.4
  23.8 1.8 copy-start.5
  23.8 1.8 copy-start.6
  25.7 14.9 %copy-start.7 = (s32[8,128]{1,0:T(8,128)S(1)}, s32[8,128]{1,0:T(8,128)}, u32[]{:S(2)}) copy-start(s32[8,128]{1,0:T(8,128)} %param.7) | copy-start | bytes 12292
  25.7 14.9 %copy-start.8 = (f32[8,128]{1,0:T(8,128)S(1)}, f32[8,128]{1,0:T(8,128)}, u32[]{:S(2)}) copy-start(f32[8,128]{1,0:T(8,128)} %param.6) | copy-start | bytes 12292
  25.7 14.9 %copy-start.9 = (f32[8,128]{1,0:T(8,128)S(1)}, f32[8,128]{1,0:T(8,128)}, u32[]{:S(2)}) copy-start(f32[8,128]{1,0:T(8,128)} %param.5) | copy-start | bytes 12292
  28.1 4.3 %collective-permute-start.4 = (f32[2,1,128]{2,1,0:T(1,128)S(1)}, f32[2,1,128]{2,1,0:T(1,128)S(1)}, u32[]{:S(2)}, u32[]{:S(2)}) collective-permute-start(f32[2,1,128]{2,1,0:T(1,128)S(1)} %get-tuple-element.36), channel_id=1, source_target_pairs={{4,0},{8,4},{12,8},{16,12},{20,16},{24,20},{28,24},{5,1},{9,5},{13... | collective-permute-start | bytes 3080 | tf_op jit(solution)/shard_map/ppermute | solution.py:24
  29.4 3.8 %collective-permute-start.5 = (f32[2,1,128]{2,1,0:T(1,128)S(1)}, f32[2,1,128]{2,1,0:T(1,128)S(1)}, u32[]{:S(2)}, u32[]{:S(2)}) collective-permute-start(f32[2,1,128]{2,1,0:T(1,128)S(1)} %get-tuple-element.35), channel_id=1, source_target_pairs={{0,4},{4,8},{8,12},{12,16},{16,20},{20,24},{24,28},{1,5},{5,9},{9,... | collective-permute-start | bytes 3080 | tf_op jit(solution)/shard_map/ppermute | solution.py:23
  33.3 5.8 %collective-permute-start.6 = (f32[2,10,1]{2,1,0:T(8,128)S(1)}, f32[2,10,1]{2,1,0:T(8,128)S(1)}, u32[]{:S(2)}, u32[]{:S(2)}) collective-permute-start(f32[2,10,1]{2,1,0:T(8,128)S(1)} %get-tuple-element.27), channel_id=1, source_target_pairs={{1,0},{2,1},{3,2},{5,4},{6,5},{7,6},{9,8},{10,9},{11,10},{13,12},{... | collective-permute-start | bytes 248 | tf_op jit(solution)/shard_map/ppermute | solution.py:24
  34.6 6.0 %collective-permute-start.7 = (f32[2,10,1]{2,1,0:T(8,128)S(1)}, f32[2,10,1]{2,1,0:T(8,128)S(1)}, u32[]{:S(2)}, u32[]{:S(2)}) collective-permute-start(f32[2,10,1]{2,1,0:T(8,128)S(1)} %get-tuple-element.28), channel_id=1, source_target_pairs={{0,1},{1,2},{2,3},{4,5},{5,6},{6,7},{8,9},{9,10},{10,11},{12,13},{... | collective-permute-start | bytes 248 | tf_op jit(solution)/shard_map/ppermute | solution.py:23
  40.7 5.1 %collective-permute-start.8 = (f32[1,128]{1,0:T(1,128)S(1)}, f32[1,128]{1,0:T(1,128)S(1)}, u32[]{:S(2)}, u32[]{:S(2)}) collective-permute-start(f32[1,128]{1,0:T(1,128)S(1)} %get-tuple-element.42), channel_id=1, source_target_pairs={{4,0},{8,4},{12,8},{16,12},{20,16},{24,20},{28,24},{5,1},{9,5},{13... | collective-permute-start | bytes 1544 | tf_op jit(solution)/shard_map/ppermute | solution.py:24
  42.0 4.6 %collective-permute-start.9 = (f32[1,128]{1,0:T(1,128)S(1)}, f32[1,128]{1,0:T(1,128)S(1)}, u32[]{:S(2)}, u32[]{:S(2)}) collective-permute-start(f32[1,128]{1,0:T(1,128)S(1)} %get-tuple-element.41), channel_id=1, source_target_pairs={{0,4},{4,8},{8,12},{12,16},{16,20},{20,24},{24,28},{1,5},{5,9},{9,... | collective-permute-start | bytes 1544 | tf_op jit(solution)/shard_map/ppermute | solution.py:23
  46.7 5.8 %collective-permute-start.10 = (f32[10,1]{1,0:T(8,128)S(1)}, f32[10,1]{1,0:T(8,128)S(1)}, u32[]{:S(2)}, u32[]{:S(2)}) collective-permute-start(f32[10,1]{1,0:T(8,128)S(1)} %get-tuple-element.33), channel_id=1, source_target_pairs={{1,0},{2,1},{3,2},{5,4},{6,5},{7,6},{9,8},{10,9},{11,10},{13,12},{... | collective-permute-start | bytes 128 | tf_op jit(solution)/shard_map/ppermute | solution.py:24
  48.0 5.9 %collective-permute-start.11 = (f32[10,1]{1,0:T(8,128)S(1)}, f32[10,1]{1,0:T(8,128)S(1)}, u32[]{:S(2)}, u32[]{:S(2)}) collective-permute-start(f32[10,1]{1,0:T(8,128)S(1)} %get-tuple-element.34), channel_id=1, source_target_pairs={{0,1},{1,2},{2,3},{4,5},{5,6},{6,7},{8,9},{9,10},{10,11},{12,13},{... | collective-permute-start | bytes 128 | tf_op jit(solution)/shard_map/ppermute | solution.py:23
  110.7 4.3 %collective-permute-start.12 = (f32[1,128]{1,0:T(1,128)S(1)}, f32[1,128]{1,0:T(1,128)S(1)}, u32[]{:S(2)}, u32[]{:S(2)}) collective-permute-start(f32[1,128]{1,0:T(1,128)S(1)} %get-tuple-element.40), channel_id=1, source_target_pairs={{4,0},{8,4},{12,8},{16,12},{20,16},{24,20},{28,24},{5,1},{9,5},{13... | collective-permute-start | bytes 1544 | tf_op jit(solution)/shard_map/ppermute | solution.py:24
  112.0 3.8 %collective-permute-start.13 = (f32[1,128]{1,0:T(1,128)S(1)}, f32[1,128]{1,0:T(1,128)S(1)}, u32[]{:S(2)}, u32[]{:S(2)}) collective-permute-start(f32[1,128]{1,0:T(1,128)S(1)} %get-tuple-element.39), channel_id=1, source_target_pairs={{0,4},{4,8},{8,12},{12,16},{16,20},{20,24},{24,28},{1,5},{5,9},{9,... | collective-permute-start | bytes 1544 | tf_op jit(solution)/shard_map/ppermute | solution.py:23
  115.9 5.8 %collective-permute-start.14 = (f32[10,1]{1,0:T(8,128)S(1)}, f32[10,1]{1,0:T(8,128)S(1)}, u32[]{:S(2)}, u32[]{:S(2)}) collective-permute-start(f32[10,1]{1,0:T(8,128)S(1)} %get-tuple-element.31), channel_id=1, source_target_pairs={{1,0},{2,1},{3,2},{5,4},{6,5},{7,6},{9,8},{10,9},{11,10},{13,12},{... | collective-permute-start | bytes 128 | tf_op jit(solution)/shard_map/ppermute | solution.py:24
  117.2 5.9 %collective-permute-start.15 = (f32[10,1]{1,0:T(8,128)S(1)}, f32[10,1]{1,0:T(8,128)S(1)}, u32[]{:S(2)}, u32[]{:S(2)}) collective-permute-start(f32[10,1]{1,0:T(8,128)S(1)} %get-tuple-element.32), channel_id=1, source_target_pairs={{0,1},{1,2},{2,3},{4,5},{5,6},{6,7},{8,9},{9,10},{10,11},{12,13},{... | collective-permute-start | bytes 128 | tf_op jit(solution)/shard_map/ppermute | solution.py:23
  176.0 4.3 %collective-permute-start.16 = (f32[1,128]{1,0:T(1,128)S(1)}, f32[1,128]{1,0:T(1,128)S(1)}, u32[]{:S(2)}, u32[]{:S(2)}) collective-permute-start(f32[1,128]{1,0:T(1,128)S(1)} %get-tuple-element.38), channel_id=1, source_target_pairs={{4,0},{8,4},{12,8},{16,12},{20,16},{24,20},{28,24},{5,1},{9,5},{13... | collective-permute-start | bytes 1544 | tf_op jit(solution)/shard_map/ppermute | solution.py:24
  177.3 3.8 %collective-permute-start.17 = (f32[1,128]{1,0:T(1,128)S(1)}, f32[1,128]{1,0:T(1,128)S(1)}, u32[]{:S(2)}, u32[]{:S(2)}) collective-permute-start(f32[1,128]{1,0:T(1,128)S(1)} %get-tuple-element.37), channel_id=1, source_target_pairs={{0,4},{4,8},{8,12},{12,16},{16,20},{20,24},{24,28},{1,5},{5,9},{9,... | collective-permute-start | bytes 1544 | tf_op jit(solution)/shard_map/ppermute | solution.py:23
  181.3 5.8 %collective-permute-start.18 = (f32[10,1]{1,0:T(8,128)S(1)}, f32[10,1]{1,0:T(8,128)S(1)}, u32[]{:S(2)}, u32[]{:S(2)}) collective-permute-start(f32[10,1]{1,0:T(8,128)S(1)} %get-tuple-element.29), channel_id=1, source_target_pairs={{1,0},{2,1},{3,2},{5,4},{6,5},{7,6},{9,8},{10,9},{11,10},{13,12},{... | collective-permute-start | bytes 128 | tf_op jit(solution)/shard_map/ppermute | solution.py:24
  182.5 5.9 %collective-permute-start.19 = (f32[10,1]{1,0:T(8,128)S(1)}, f32[10,1]{1,0:T(8,128)S(1)}, u32[]{:S(2)}, u32[]{:S(2)}) collective-permute-start(f32[10,1]{1,0:T(8,128)S(1)} %get-tuple-element.30), channel_id=1, source_target_pairs={{0,1},{1,2},{2,3},{4,5},{5,6},{6,7},{8,9},{9,10},{10,11},{12,13},{... | collective-permute-start | bytes 128 | tf_op jit(solution)/shard_map/ppermute | solution.py:23
where the time goes:
time: 221 us; the launch traced here: 219 us
  blocking collectives  128 us (58%)
  starting transfers between devices  52 us (24%)
  waiting for transfers between devices  13.6 us (6%)
  other arithmetic  12.1 us (5%)
  between operations  7.91 us (4%)
  local copies, waits for them, and re-layouts  4.79 us (2%)
    psum x5, blocking collectives, global_total(): part_sum = lax.psum(value, 'blocks')  72.3 us
    psum x5, blocking collectives, global_total(): return lax.psum(part_sum, 'group')  56.1 us
    ppermute x10, starting transfers between devices, padded_2(): before = lax.ppermute(last, axis, up)  39.1 us
    ppermute x10, starting transfers between devices, padded_2(): after = lax.ppermute(initial, axis, down)  12.9 us
    ppermute x10, waiting for transfers between devices, padded_2(): before = lax.ppermute(last, axis, up)  8.89 us
    ppermute x10, waiting for transfers between devices, padded_2(): after = lax.ppermute(initial, axis, down)  4.72 us
  transfers between devices with their start and end apart: 20, of which 10 were waited for; matrix products, arithmetic and copies ran while one was open for 1% of the time, Pallas kernels for 0%

commit v1 on v0

v1 whole, which is shorter than its diff:
```python
import jax
import jax.numpy as jnp
from jax import lax
from jax.experimental import pallas as pl
from jax.experimental.pallas import tpu as pltpu
from jax.sharding import PartitionSpec as P

ITERS = 3

time_step = 0.25
hyper_visc = 0.025
mixing = 0.2
gravity = 4.0
rotation = 0.2

COMPS = 4
ROWS = 8
LANES = 128
SLOT = 8
PER = LANES // SLOT
EXT = 12
F32 = jnp.float32
VMEM = pl.BlockSpec(memory_space=pltpu.VMEM)


def iota(axis):
    return lax.broadcasted_iota(jnp.int32, (ROWS, LANES), axis)


def roll(x, shift, axis):
    return pltpu.roll(x, shift % x.shape[axis], axis)


def swap_pairs(mesh_shape, along):
    nb, ng = mesh_shape
    first, second = [], []
    for b in range(nb):
        for g in range(ng):
            me = b * ng + g
            if along == "blocks":
                one = (b ^ 1, g)
                two = ((b - 1) ^ 1) + 1
                two = (two, g) if 0 <= two < nb else (b, g ^ 1)
            else:
                one = (b, g ^ 1)
                two = ((g - 1) ^ 1) + 1
                two = (b, two) if 0 <= two < ng else (b ^ 1, g)
            first.append((me, one[0] * ng + one[1]))
            second.append((me, two[0] * ng + two[1]))
    return first, second


def pack_kernel(state_ref, mask_ref, m_ref, pack_ref):
    sea = mask_ref[...].astype(F32)
    slot = iota(1) // SLOT
    tiles = state_ref.shape[0] // ROWS
    for p in range(tiles // PER):
        acc = jnp.zeros((ROWS, LANES), F32)
        for q in range(PER):
            at = pl.ds((p * PER + q) * ROWS, ROWS)
            x = state_ref[at, :] * sea
            m_ref[at, :] = x
            acc = jnp.where(slot == q, roll(x, SLOT * q + SLOT // 2, 1), acc)
        pack_ref[pl.ds(p * ROWS, ROWS), :] = acc


def edge_kernel(m_ref, pack_ref, first_ref, second_ref, delta_ref, one_ref, two_ref):
    g = lax.axis_index("group")
    ng = lax.axis_size("group")
    geven = lax.rem(g, 2) == 0
    beven = lax.rem(lax.axis_index("blocks"), 2) == 0
    half = lax.rem(iota(1), SLOT) < SLOT // 2
    has_left = (g > 0).astype(F32)
    has_right = (g < ng - 1).astype(F32)
    packs = pack_ref.shape[0] // ROWS
    eights = m_ref.shape[0] // 64
    base = one_ref.shape[0] - 2 * ROWS
    for p in range(packs):
        at = pl.ds(p * ROWS, ROWS)
        first, second = first_ref[at, :], second_ref[at, :]
        from_left = jnp.where(geven, second, first) * has_left
        from_right = jnp.where(geven, first, second) * has_right
        delta_ref[at, :] = jnp.where(half, from_left, from_right) - pack_ref[at, :]

    def fill(low_ref, high_ref):
        for r in range(2):
            for s in range(eights):
                at = pl.ds((r * eights + s) * ROWS, ROWS)
                low_ref[at, :] = m_ref[pl.ds(64 * s + r, ROWS, stride=ROWS), :]
                high_ref[at, :] = m_ref[pl.ds(64 * s + 6 + r, ROWS, stride=ROWS), :]
        for p in range(packs):
            low_ref[pl.ds(base + p, 1), :] = delta_ref[pl.ds(ROWS * p, 1), :]
            high_ref[pl.ds(base + p, 1), :] = delta_ref[pl.ds(ROWS * p + ROWS - 1, 1), :]

    pl.when(beven)(lambda: fill(two_ref, one_ref))
    pl.when(jnp.logical_not(beven))(lambda: fill(one_ref, two_ref))


def step_kernel(
    m_ref, pack_ref, delta_ref, one_ref, two_ref, mask_ref, height_ref, damp_ref, new_ref, field_ref, ext_ref, corr_ref
):
    b, nb = lax.axis_index("blocks"), lax.axis_size("blocks")
    g, ng = lax.axis_index("group"), lax.axis_size("group")
    even = lax.rem(b, 2) == 0
    has_up = (b > 0).astype(F32)
    has_down = (b < nb - 1).astype(F32)
    row, lane = iota(0), iota(1)
    tiles = m_ref.shape[0] // ROWS
    levels = tiles // COMPS
    eights = tiles // ROWS
    packs = tiles // PER
    base = one_ref.shape[0] - 2 * ROWS

    for t in range(tiles):
        ext_ref[pl.ds(EXT * t + 2, ROWS), :] = m_ref[pl.ds(ROWS * t, ROWS), :]
    for r in range(2):
        for s in range(eights):
            at = pl.ds((r * eights + s) * ROWS, ROWS)
            one, two = one_ref[at, :], two_ref[at, :]
            up = jnp.where(even, two, one) * has_up
            down = jnp.where(even, one, two) * has_down
            ext_ref[pl.ds(EXT * ROWS * s + r, ROWS, stride=EXT), :] = up
            ext_ref[pl.ds(EXT * ROWS * s + 10 + r, ROWS, stride=EXT), :] = down

    in_slot = lax.rem(lane, SLOT)
    left_half = in_slot < SLOT // 2
    comp = lax.rem(lane // SLOT, COMPS)
    near = (in_slot == 3) | (in_slot == 4)
    far = (in_slot >= 2) & (in_slot <= 5)
    sign = jnp.where(in_slot == 3, -0.5 * time_step, jnp.where(in_slot == 4, 0.5 * time_step, 0.0))
    for p in range(packs):
        at = pl.ds(p * ROWS, ROWS)
        d = delta_ref[at, :]
        one, two = one_ref[pl.ds(base + p, 1), :], two_ref[pl.ds(base + p, 1), :]
        up = jnp.where(even, two, one) * has_up
        down = jnp.where(even, one, two) * has_down
        dv = jnp.where(row == 0, up, roll(d, 1, 0)) + jnp.where(row == ROWS - 1, down, roll(d, -1, 0))
        x2 = jnp.where(left_half, roll(d, -2, 1), roll(d, 2, 1))
        x1 = jnp.where(left_half, roll(d, -1, 1), roll(d, 1, 1))
        y = 2.0 * dv - 8.0 * d
        y1 = jnp.where(left_half, roll(y, -1, 1), roll(y, 1, 1))
        own = pack_ref[at, :]
        v = own
        for c in range(3):
            v = jnp.where(comp == c, roll(own, -SLOT * (3 - c), 1), v)
        corr_ref[at, :] = (
            jnp.where(far, -hyper_visc * x2, 0.0) + jnp.where(near, -hyper_visc * y1, 0.0) + sign * v * x1
        )

    sea = mask_ref[...].astype(F32)
    edge_rows = jnp.where((row == 0) & (b == 0), 1.0, 0.0) + jnp.where((row == ROWS - 1) & (b == nb - 1), 1.0, 0.0)
    edge_cols = jnp.where((lane == 0) & (g == 0), 1.0, 0.0) + jnp.where((lane == LANES - 1) & (g == ng - 1), 1.0, 0.0)
    centre = 1.0 - 2.0 * mixing + hyper_visc * (edge_rows + edge_cols)
    col = (lane + g * LANES).astype(F32)
    coriolis = time_step * rotation * (2.0 * (col + 0.5) / (ng * LANES) - 1.0)
    border = (lane < SLOT // 2) | (lane >= LANES - SLOT // 2)
    sums = [jnp.zeros((ROWS, LANES), F32) for _ in range(2)]

    def own(level, c):
        level = min(max(level, 0), levels - 1)
        return m_ref[pl.ds(ROWS * (COMPS * level + c), ROWS), :]

    for k in range(levels):
        u, v = own(k, 2), own(k, 3)
        for c in range(COMPS):
            t = COMPS * k + c
            x = own(k, c)
            up2 = ext_ref[pl.ds(EXT * t, ROWS), :]
            up1 = ext_ref[pl.ds(EXT * t + 1, ROWS), :]
            dn1 = ext_ref[pl.ds(EXT * t + 3, ROWS), :]
            dn2 = ext_ref[pl.ds(EXT * t + 4, ROWS), :]
            left, right = roll(x, 1, 1), roll(x, -1, 1)
            near1 = up1 + dn1
            q = (left + right) + 2.0 * near1 - 6.0 * x
            biharm = (roll(q, 1, 1) + roll(q, -1, 1)) - 2.0 * q + (up2 + dn2) - 4.0 * near1 + 6.0 * x
            advect = u * (dn1 - up1) + v * (right - left)
            out = centre * x - hyper_visc * biharm - 0.5 * time_step * advect + mixing * (own(k - 1, c) + own(k + 1, c))
            if c == 2:
                out = out + coriolis * v
            if c == 3:
                out = out - coriolis * u
            p, s = divmod(t, PER)
            fix = roll(corr_ref[pl.ds(p * ROWS, ROWS), :], -(SLOT * s + SLOT // 2), 1)
            out = sea * (out + jnp.where(border, fix, 0.0))
            new_ref[pl.ds(ROWS * t, ROWS), :] = out
            if c >= 2:
                sums[c - 2] = sums[c - 2] + out
    field_ref[0:8, :] = sums[0] / levels
    field_ref[8:16, :] = sums[1] / levels
    field_ref[16:24, :] = sea * damp_ref[...] * height_ref[...]
    field_ref[24:32, :] = sea * (4.0 + damp_ref[...])


def call(kernel, outs, *args, scratch=(), flops=0):
    return pl.pallas_call(
        kernel,
        out_shape=[jax.ShapeDtypeStruct(s, F32) for s in outs],
        in_specs=[VMEM] * len(args),
        out_specs=[VMEM] * len(outs),
        scratch_shapes=[pltpu.VMEM(s, F32) for s in scratch],
        compiler_params=pltpu.CompilerParams(vmem_limit_bytes=32 * 1024 * 1024),
        cost_estimate=pl.CostEstimate(flops=flops, bytes_accessed=0, transcendentals=0),
    )(*args)


def on_device(ocean_state, surface_height, surface_damping, land_mask, *, shape):
    nb, ng = shape
    axes = ("blocks", "group")
    levels = ocean_state.shape[0]
    tiles = levels * COMPS
    state = ocean_state.reshape(tiles * ROWS, LANES)
    g_one, g_two = swap_pairs(shape, "group")
    b_one, b_two = swap_pairs(shape, "blocks")
    packs = tiles // PER

    m, pack = call(pack_kernel, [state.shape, (packs * ROWS, LANES)], state, land_mask)
    first = lax.ppermute(pack, axes, g_one)
    second = lax.ppermute(pack, axes, g_two)
    message = (tiles * 2 + 2 * ROWS, LANES)
    delta, one, two = call(edge_kernel, [pack.shape, message, message], m, pack, first, second)
    one = lax.ppermute(one, axes, b_one)
    two = lax.ppermute(two, axes, b_two)
    new_state, fields = call(
        step_kernel,
        [state.shape, (4 * ROWS, LANES)],
        m,
        pack,
        delta,
        one,
        two,
        land_mask,
        surface_height,
        surface_damping,
        scratch=[(tiles * EXT, LANES), pack.shape],
    )
    whole = lax.all_to_all(jnp.broadcast_to(fields[None], (nb * ng,) + fields.shape), axes, 0, 0)
    whole = whole.reshape(nb, ng, 4, ROWS, LANES).transpose(2, 0, 3, 1, 4).reshape(4, nb * ROWS, ng * LANES)
    east, north, forced, diagonal = whole[0], whole[1], whole[2], whole[3]
    sea = (diagonal > 0).astype(F32)

    def shifts(f):
        f = jnp.pad(f, 1)
        return f[2:, 1:-1], f[:-2, 1:-1], f[1:-1, 2:], f[1:-1, :-2]

    e, n = shifts(east), shifts(north)
    direction = forced - gravity * sea * (0.5 * (e[0] - e[1] + n[2] - n[3]))
    residual = direction
    total = jnp.zeros_like(direction)
    norm = jnp.sum(residual * residual)
    for iteration in range(ITERS):
        image = diagonal * direction - sea * sum(shifts(direction))
        alpha = norm / jnp.sum(direction * image)
        total = total + alpha * direction
        residual = residual - alpha * image
        following = jnp.sum(residual * residual)
        direction = residual + following / norm * direction
        norm = following
    b, g = lax.axis_index("blocks"), lax.axis_index("group")
    surface = lax.dynamic_slice(total, (b * ROWS, g * LANES), (ROWS, LANES))
    return new_state.reshape(ocean_state.shape), surface


def solution(mesh):
    placed = (
        P(None, None, "blocks", "group"),
        P("blocks", "group"),
        P("blocks", "group"),
        P("blocks", "group"),
    )
    shape = (mesh.shape["blocks"], mesh.shape["group"])

    def body(*args):
        return on_device(*args, shape=shape)

    return jax.shard_map(
        body,
        mesh=mesh,
        in_specs=placed,
        out_specs=(P(None, None, "blocks", "group"), P("blocks", "group")),
        check_vma=False,
    )
```

time: 221 us -> 58.2 us (0.26)
  blocking collectives: 128 us -> 0 us
  starting transfers between devices: 52 us -> 12.8 us
  Pallas kernels: 0 us -> 10.9 us
  other arithmetic: 12.1 us -> 4.28 us
  waiting for transfers between devices: 13.6 us -> 19.5 us
    psum x10 -> x0, blocking collectives: 128 us -> none  [the longest x5 72.3 us: global_total(): part_sum = lax.psum(value, 'blocks')]
    ppermute x20 -> x4, starting transfers between devices: 52 us -> 6.36 us  [the longest x1 3.2 us: on_device(): two = lax.ppermute(two, axes, b_two)]
    all_to_all x0 -> x1, waiting for transfers between devices: none -> 14.4 us  [on_device(): lax.all_to_all(jnp.broadcast_to(fields[None], (nb * ng,) + fields.shape),...]
    pallas_call x0 -> x3, Pallas kernels: none -> 10.9 us  [call(): pl.pallas_call(kernel, out_shape=[jax.ShapeDtypeStruct(s, F32) for s in o...]
    ppermute x20 -> x4, waiting for transfers between devices: 13.6 us -> 5.15 us  [the longest x1 3.21 us: on_device(): two = lax.ppermute(two, axes, b_two)]
    all_to_all x0 -> x1, starting transfers between devices: none -> 6.45 us  [on_device(): lax.all_to_all(jnp.broadcast_to(fields[None], (nb * ng,) + fields.shape),...]
    mul x5 -> x0, other arithmetic: 4.71 us -> none  [the longest x1 2.33 us: on_device(): new_state = sea_mask * updated]
    slice x14 -> x0, local copies, waits for them, and re-layouts: 2.88 us -> none  [the longest x2 1.16 us: on_device(): below_level = jnp.concatenate([masked[1:], masked[-1:]], axis=0)]
  transfers between devices with their start and end apart: 20 -> 5, of which waited for: 10 -> 3; matrix products, arithmetic and copies ran while one was open for 1% -> 0% of each run, Pallas kernels for 0% -> 0%
where the time goes in v1:
time: 58.2 us; the launch traced here: 57.1 us
  waiting for transfers between devices  19.5 us (34%)
  starting transfers between devices  12.8 us (22%)
  Pallas kernels  10.9 us (19%)
  between operations  6.97 us (12%)
  other arithmetic  4.28 us (7%)
  local copies, waits for them, and re-layouts  2.62 us (5%)
    all_to_all x1, waiting for transfers between devices, on_device(): lax.all_to_all(jnp.broadcast_to(fields[None], (nb * ng,) + fields.shape),...  14.4 us
    pallas_call x3, Pallas kernels, call(): pl.pallas_call(kernel, out_shape=[jax.ShapeDtypeStruct(s, F32) for s in o...  10.9 us
    all_to_all x1, starting transfers between devices, on_device(): lax.all_to_all(jnp.broadcast_to(fields[None], (nb * ng,) + fields.shape),...  6.45 us
    ppermute x1, waiting for transfers between devices, on_device(): two = lax.ppermute(two, axes, b_two)  3.21 us
    ppermute x1, starting transfers between devices, on_device(): two = lax.ppermute(two, axes, b_two)  3.2 us
    ppermute x1, starting transfers between devices, on_device(): first = lax.ppermute(pack, axes, g_one)  3.08 us
    reduce_sum x3, other arithmetic, on_device(): alpha = norm / jnp.sum(direction * image)  2.21 us
    ppermute x1, waiting for transfers between devices, on_device(): first = lax.ppermute(pack, axes, g_one)  1.93 us
  transfers between devices with their start and end apart: 5, of which 3 were waited for; matrix products, arithmetic and copies ran while one was open for 0% of the time, Pallas kernels for 0%

profile of v1, /device:TPU:0, one launch (start us, length us, event | category | flops | bytes accessed | tf_op | source)
XLA Modules:
  0.0 57.1 jit_solution(7638124863365027703)
XLA Ops:
  0.6 0.0 copy-start
  0.6 1.1 %copy-done = f32[36,4,8,128]{3,2,1,0:T(8,128)S(1)} copy-done((f32[36,4,8,128]{3,2,1,0:T(8,128)S(1)}, f32[36,4,8,128]{3,2,1,0:T(8,128)}, u32[]{:S(2)}) %copy-start) | copy-done | bytes 589848
  1.7 0.0 copy-start.1
  1.7 0.7 %copy-done.1 = s32[8,128]{1,0:T(8,128)S(1)} copy-done((s32[8,128]{1,0:T(8,128)S(1)}, s32[8,128]{1,0:T(8,128)}, u32[]{:S(2)}) %copy-start.1) | copy-done | bytes 4120
  2.4 0.2 shard_map.59
  2.6 3.1 %collective-permute-start = (f32[72,128]{1,0:T(8,128)S(1)}, f32[72,128]{1,0:T(8,128)S(1)}, u32[]{:S(2)}, u32[]{:S(2)}) collective-permute-start(f32[72,128]{1,0:T(8,128)S(1)} %get-tuple-element.10.pack_ref), channel_id=1, source_target_pairs={{0,1},{1,0},{2,3},{3,2},{4,5},{5,4},{6,7},{7,6},{8,9},{9,8},{10,11... | collective-permute-start | bytes 110600 | tf_op jit(solution)/shard_map/ppermute | solution.py:217
  5.7 0.0 collective-permute-start.1
  5.7 1.9 %collective-permute-done.first_ref = f32[72,128]{1,0:T(8,128)S(1)} collective-permute-done((f32[72,128]{1,0:T(8,128)S(1)}, f32[72,128]{1,0:T(8,128)S(1)}, u32[]{:S(2)}, u32[]{:S(2)}) %collective-permute-start) | collective-permute-done | bytes 36896 | tf_op jit(solution)/shard_map/ppermute | solution.py:217
  7.6 0.0 collective-permute-done.1.second_ref
  7.6 0.0 copy-start.3
  7.6 0.1 shard_map.60
  7.7 0.0 copy-start.2
  7.7 0.1 collective-permute-start.2
  7.8 3.2 %collective-permute-start.3 = (f32[304,128]{1,0:T(8,128)S(1)}, f32[304,128]{1,0:T(8,128)S(1)}, u32[]{:S(2)}, u32[]{:S(2)}) collective-permute-start(f32[304,128]{1,0:T(8,128)S(1)} %get-tuple-element.13), channel_id=1, source_target_pairs={{0,1},{1,0},{2,3},{3,2},{4,8},{5,9},{6,10},{7,11},{8,4},{9,5},{10,... | collective-permute-start | bytes 466952 | tf_op jit(solution)/shard_map/ppermute | solution.py:222
  11.0 0.0 collective-permute-done.2.one_ref
  11.0 3.2 %collective-permute-done.3.two_ref = f32[304,128]{1,0:T(8,128)S(1)} collective-permute-done((f32[304,128]{1,0:T(8,128)S(1)}, f32[304,128]{1,0:T(8,128)S(1)}, u32[]{:S(2)}, u32[]{:S(2)}) %collective-permute-start.3) | collective-permute-done | bytes 155680 | tf_op jit(solution)/shard_map/ppermute | solution.py:222
  14.2 0.0 copy-done.3
  14.2 0.0 copy-done.2
  14.2 10.6 %shard_map.61 = (f32[1152,128]{1,0:T(8,128)}, f32[32,128]{1,0:T(8,128)S(1)}) custom-call(f32[1152,128]{1,0:T(8,128)S(1)} %get-tuple-element.9.m_ref, f32[72,128]{1,0:T(8,128)S(1)} %get-tuple-element.10.pack_ref, f32[72,128]{1,0:T(8,128)S(1)} %get-tuple-element.11.delta_ref, f32[304,128]{1,0:T(8,128)S(1)} %collective-permute-done.2.one_ref, ...), custom_call_target="tpu_custom_call" | custom-call | tf_op jit(solution)/shard_map/pallas_call | solution.py:195
  24.9 0.8 %broadcast_in_dim.2 = f32[32,32,128]{2,1,0:T(8,128)} broadcast(f32[32,128]{1,0:T(8,128)S(1)} %get-tuple-element.15), dimensions={1,2} | broadcast | bytes 540672 | tf_op jit(solution)/shard_map/broadcast_in_dim | solution.py:236
  25.7 6.4 %all-to-all-start = ((f32[32,32,128]{2,1,0:T(8,128)}), f32[32,32,128]{2,1,0:T(8,128)S(1)}, u32[]{:S(2)}, u32[]{:S(2)}) async-start(f32[32,32,128]{2,1,0:T(8,128)} %broadcast_in_dim.2), calls=%async_computation | async-start | bytes 1048576 | tf_op jit(solution)/shard_map/all_to_all | solution.py:236
  32.2 14.4 %all-to-all-done = f32[32,32,128]{2,1,0:T(8,128)S(1)} async-done(((f32[32,32,128]{2,1,0:T(8,128)}), f32[32,32,128]{2,1,0:T(8,128)S(1)}, u32[]{:S(2)}, u32[]{:S(2)}) %all-to-all-start) | async-done | bytes 524320 | tf_op jit(solution)/shard_map/all_to_all | solution.py:236
  46.6 0.1 fusion.5
  46.7 0.7 %multiply_reduce_fusion.3 = (f32[]{:T(128)}, f32[]{:T(128)}, f32[64,512]{1,0:T(8,128)S(1)}) fusion(f32[64,512]{1,0:T(8,128)S(1)} %get-tuple-element.23, pred[64,512]{1,0:T(8,128)(4,1)S(1)} %get-tuple-element.24, f32[4,8,8,4,128]{4,2,0,3,1:T(8,128)S(1)} %bitcast.29), kind=kLoop, calls=%fused_computation.50 | loop fusion | flops 327678 | bytes 425992 | tf_op jit(solution)/shard_map/reduce_sum | solution.py:252
  48.7 0.6 %multiply_reduce_fusion.2 = (f32[]{:T(128)}, f32[64,512]{1,0:T(8,128)S(1)}) fusion(f32[64,512]{1,0:T(8,128)S(1)} %get-tuple-element.23, f32[64,512]{1,0:T(8,128)S(1)} %get-tuple-element.22, f32[]{:T(128)S(6)} %div.15), kind=kLoop, calls=%fused_computation.48 | loop fusion | flops 131071 | bytes 393224 | tf_op jit(solution)/shard_map/reduce_sum | solution.py:255
  50.6 0.7 %multiply_reduce_fusion.1 = (f32[]{:T(128)}, f32[64,512]{1,0:T(8,128)S(1)}) fusion(f32[64,512]{1,0:T(8,128)S(1)} %multiply_add_fusion.1, pred[64,512]{1,0:T(8,128)(4,1)S(1)} %get-tuple-element.24, f32[4,8,8,4,128]{4,2,0,3,1:T(8,128)S(1)} %bitcast.30), kind=kLoop, calls=%fused_computation.46 | loop fusion | flops 262143 | bytes 425988 | tf_op jit(solution)/shard_map/reduce_sum | solution.py:252
  52.6 0.6 %multiply_reduce_fusion = f32[]{:T(128)} fusion(f32[64,512]{1,0:T(8,128)S(1)} %get-tuple-element.21, f32[64,512]{1,0:T(8,128)S(1)} %get-tuple-element.19, f32[]{:T(128)S(6)} %div.17), kind=kLoop, calls=%fused_computation.44 | loop fusion | flops 131071 | bytes 262152 | tf_op jit(solution)/shard_map/reduce_sum | solution.py:255
  54.5 0.7 %fusion.22 = f32[]{:T(128)} fusion(f32[64,512]{1,0:T(8,128)S(1)} %multiply_add_fusion, pred[64,512]{1,0:T(8,128)(4,1)S(1)} %get-tuple-element.24, f32[4,8,8,4,128]{4,2,0,3,1:T(8,128)S(1)} %bitcast.31), kind=kLoop, calls=%fused_computation.38 | loop fusion | flops 262143 | bytes 294916 | tf_op jit(solution)/shard_map/reduce_sum | solution.py:252
  56.5 0.6 %fusion.24 = f32[8,128]{1,0:T(8,128)} fusion(f32[64,512]{1,0:T(8,128)S(1)} %multiply_add_fusion, s32[]{:T(128)S(6)} %select_n.6, s32[]{:T(128)S(6)} %select_n.7, f32[64,512]{1,0:T(8,128)S(1)} %multiply_add_fusion.1, f32[64,512]{1,0:T(8,128)S(1)} %get-tuple-element.23, f32[]{:T(128)S(6)} %div.19, f32[]{:T(128)S(6)} %div.17, f32[]{:T(128)S(6)} %div.15), kind=kLoop, calls=%fused_computation.54 | loop fusion | flops 5120 | bytes 16404 | tf_op jit(solution)/shard_map/add | solution.py:253
  (3 shorter events, 0.1 us)
Async XLA Ops:
  0.6 1.1 %copy-start = (f32[36,4,8,128]{3,2,1,0:T(8,128)S(1)}, f32[36,4,8,128]{3,2,1,0:T(8,128)}, u32[]{:S(2)}) copy-start(f32[36,4,8,128]{3,2,1,0:T(8,128)} %param.4) | copy-start | bytes 1769476
  1.7 0.7 %copy-start.1 = (s32[8,128]{1,0:T(8,128)S(1)}, s32[8,128]{1,0:T(8,128)}, u32[]{:S(2)}) copy-start(s32[8,128]{1,0:T(8,128)} %mask_ref.3) | copy-start | bytes 12292
  2.6 5.0 %collective-permute-start = (f32[72,128]{1,0:T(8,128)S(1)}, f32[72,128]{1,0:T(8,128)S(1)}, u32[]{:S(2)}, u32[]{:S(2)}) collective-permute-start(f32[72,128]{1,0:T(8,128)S(1)} %get-tuple-element.10.pack_ref), channel_id=1, source_target_pairs={{0,1},{1,0},{2,3},{3,2},{4,5},{5,4},{6,7},{7,6},{8,9},{9,8},{10,11... | collective-permute-start | bytes 110600 | tf_op jit(solution)/shard_map/ppermute | solution.py:217
  5.7 1.9 %collective-permute-start.1 = (f32[72,128]{1,0:T(8,128)S(1)}, f32[72,128]{1,0:T(8,128)S(1)}, u32[]{:S(2)}, u32[]{:S(2)}) collective-permute-start(f32[72,128]{1,0:T(8,128)S(1)} %get-tuple-element.10.pack_ref), channel_id=1, source_target_pairs={{0,4},{1,2},{2,1},{3,7},{4,0},{5,6},{6,5},{7,3},{8,12},{9,10},{10,... | collective-permute-start | bytes 110600 | tf_op jit(solution)/shard_map/ppermute | solution.py:218
  7.6 6.6 %copy-start.3 = (f32[8,128]{1,0:T(8,128)S(1)}, f32[8,128]{1,0:T(8,128)}, u32[]{:S(2)}) copy-start(f32[8,128]{1,0:T(8,128)} %damp_ref.1) | copy-start | bytes 12292
  7.7 6.5 %copy-start.2 = (f32[8,128]{1,0:T(8,128)S(1)}, f32[8,128]{1,0:T(8,128)}, u32[]{:S(2)}) copy-start(f32[8,128]{1,0:T(8,128)} %height_ref.1) | copy-start | bytes 12292
  7.7 3.3 %collective-permute-start.2 = (f32[304,128]{1,0:T(8,128)S(1)}, f32[304,128]{1,0:T(8,128)S(1)}, u32[]{:S(2)}, u32[]{:S(2)}) collective-permute-start(f32[304,128]{1,0:T(8,128)S(1)} %get-tuple-element.12), channel_id=1, source_target_pairs={{0,4},{1,5},{2,6},{3,7},{4,0},{5,1},{6,2},{7,3},{8,12},{9,13},{10,... | collective-permute-start | bytes 466952 | tf_op jit(solution)/shard_map/ppermute | solution.py:221
  7.8 6.4 %collective-permute-start.3 = (f32[304,128]{1,0:T(8,128)S(1)}, f32[304,128]{1,0:T(8,128)S(1)}, u32[]{:S(2)}, u32[]{:S(2)}) collective-permute-start(f32[304,128]{1,0:T(8,128)S(1)} %get-tuple-element.13), channel_id=1, source_target_pairs={{0,1},{1,0},{2,3},{3,2},{4,8},{5,9},{6,10},{7,11},{8,4},{9,5},{10,... | collective-permute-start | bytes 466952 | tf_op jit(solution)/shard_map/ppermute | solution.py:222
  25.7 20.8 %all-to-all-start = ((f32[32,32,128]{2,1,0:T(8,128)}), f32[32,32,128]{2,1,0:T(8,128)S(1)}, u32[]{:S(2)}, u32[]{:S(2)}) async-start(f32[32,32,128]{2,1,0:T(8,128)} %broadcast_in_dim.2), calls=%async_computation | async-start | bytes 1048576 | tf_op jit(solution)/shard_map/all_to_all | solution.py:236

commit v2 on v0

v2 whole, which is shorter than its diff:
```python
import jax
import jax.numpy as jnp
from jax import lax
from jax.experimental import pallas as pl
from jax.experimental.pallas import tpu as pltpu
from jax.sharding import PartitionSpec as P

ITERS = 3

time_step = 0.25
hyper_visc = 0.025
mixing = 0.2
gravity = 4.0
rotation = 0.2

COMPS = 4
ROWS = 8
LANES = 128
SLOT = 8
PER = LANES // SLOT
EXT = 12
FLAT = 6
STRIP = 16
SHIFT = 4.5
F32 = jnp.float32
VMEM = pl.BlockSpec(memory_space=pltpu.VMEM)
HBM = pl.BlockSpec(memory_space=pltpu.HBM)


def iota(axis, rows=ROWS, lanes=LANES):
    return lax.broadcasted_iota(jnp.int32, (rows, lanes), axis)


def roll(x, shift, axis):
    return pltpu.roll(x, shift % x.shape[axis], axis)


def tile(k):
    return pl.ds(k * ROWS, ROWS)


def swap_pairs(mesh_shape, along):
    nb, ng = mesh_shape
    first, second = [], []
    for b in range(nb):
        for g in range(ng):
            me = b * ng + g
            if along == "blocks":
                one = (b ^ 1, g)
                two = ((b - 1) ^ 1) + 1
                two = (two, g) if 0 <= two < nb else (b, g ^ 1)
            else:
                one = (b, g ^ 1)
                two = ((g - 1) ^ 1) + 1
                two = (b, two) if 0 <= two < ng else (b ^ 1, g)
            first.append((me, one[0] * ng + one[1]))
            second.append((me, two[0] * ng + two[1]))
    return first, second


class Layout:
    def __init__(self, tiles):
        self.tiles = tiles
        self.levels = tiles // COMPS
        self.packs = tiles // PER
        self.eights = tiles // ROWS
        self.pad = -(-self.packs // ROWS) * ROWS
        self.edge = 2 * tiles
        self.delta = self.edge + self.pad
        self.flat = self.delta + self.pad
        self.strip = self.flat + FLAT * ROWS
        self.rows = self.strip + ROWS


class Place:
    def __init__(self):
        self.b, self.nb = lax.axis_index("blocks"), lax.axis_size("blocks")
        self.g, self.ng = lax.axis_index("group"), lax.axis_size("group")
        self.b_even = lax.rem(self.b, 2) == 0
        self.g_even = lax.rem(self.g, 2) == 0
        self.up = (self.b > 0).astype(F32)
        self.down = (self.b < self.nb - 1).astype(F32)
        self.left = (self.g > 0).astype(F32)
        self.right = (self.g < self.ng - 1).astype(F32)

    def from_up(self, one, two):
        return jnp.where(self.b_even, two, one) * self.up

    def from_down(self, one, two):
        return jnp.where(self.b_even, one, two) * self.down


def pack_kernel(
    state_hbm, mask_hbm, height_hbm, damp_hbm, m_ref, pack_ref, flat_ref, state_ref, mask_ref, height_ref, damp_ref, sems
):
    lay = Layout(m_ref.shape[0] // ROWS)
    chunk = PER * ROWS
    small = [(mask_hbm, mask_ref), (height_hbm, height_ref), (damp_hbm, damp_ref)]
    copies = [pltpu.make_async_copy(a, b, sems.at[k]) for k, (a, b) in enumerate(small)]
    for p in range(lay.packs):
        at = pl.ds(p * chunk, chunk)
        copies.append(pltpu.make_async_copy(state_hbm.at[at], state_ref.at[at], sems.at[3 + p]))
    for copy in copies:
        copy.start()
    for copy in copies[:3]:
        copy.wait()
    sea = mask_ref[...].astype(F32)
    row, lane = iota(0), iota(1)
    slot = lane // SLOT
    sums = [jnp.zeros((ROWS, LANES), F32) for _ in range(4)]
    for p in range(lay.packs):
        copies[3 + p].wait()
        acc = jnp.zeros((ROWS, LANES), F32)
        for k in range(PER // COMPS):
            x = []
            for c in range(COMPS):
                q = COMPS * k + c
                x.append(state_ref[tile(p * PER + q), :] * sea)
                m_ref[tile(p * PER + q), :] = x[c]
                acc = jnp.where(slot == q, roll(x[c], SLOT * q + SLOT // 2, 1), acc)
            u_up, u_down = jnp.where(row == 0, 0.0, x[2]), jnp.where(row == ROWS - 1, 0.0, x[2])
            v_left, v_right = jnp.where(lane == 0, 0.0, x[3]), jnp.where(lane == LANES - 1, 0.0, x[3])
            for f in range(2):
                y = x[2 + f]
                sums[f] = sums[f] + y
                sums[2 + f] = sums[2 + f] + (
                    (u_down * roll(y, -1, 0) - u_up * roll(y, 1, 0))
                    + (v_right * roll(y, -1, 1) - v_left * roll(y, 1, 1))
                )
        pack_ref[tile(p), :] = acc
    damp = damp_ref[...]
    flat = [sums[0], sums[1], 0.5 * sums[2], 0.5 * sums[3], sea * damp * height_ref[...], sea * (4.0 + damp)]
    acc = jnp.zeros((ROWS, LANES), F32)
    for f in range(FLAT):
        flat_ref[tile(f), :] = flat[f]
        acc = jnp.where(lane // STRIP == f, roll(flat[f], STRIP * f + STRIP // 2, 1), acc)
    pack_ref[tile(lay.packs), :] = acc


def spread(x, of):
    comp = lax.rem(lax.broadcasted_iota(jnp.int32, x.shape, 1) // SLOT, COMPS)
    out = x
    for c in range(COMPS):
        if c != of:
            out = jnp.where(comp == c, roll(x, SLOT * (c - of), 1), out)
    return out


def across(x):
    half = lax.rem(lax.broadcasted_iota(jnp.int32, x.shape, 1), SLOT) < SLOT // 2
    return jnp.where(half, roll(x, -1, 1), roll(x, 1, 1))


def fold(x):
    step = SLOT * COMPS
    while step < LANES:
        x = x + roll(x, step, 1)
        step *= 2
    return x


def edge_kernel(m_ref, pack_ref, flat_ref, first_ref, second_ref, own_ref, near_ref, delta_ref, one_ref, two_ref):
    lay = Layout(m_ref.shape[0] // ROWS)
    at = Place()
    lane = iota(1)
    in_slot = lax.rem(lane, SLOT)
    half = in_slot < SLOT // 2
    sign = jnp.where(in_slot == SLOT // 2 - 1, 0.5, jnp.where(in_slot == SLOT // 2, -0.5, 0.0))

    def beyond(p, low):
        first, second = first_ref[tile(p), :], second_ref[tile(p), :]
        from_left = jnp.where(at.g_even, second, first) * at.left
        from_right = jnp.where(at.g_even, first, second) * at.right
        return jnp.where(low, from_left, from_right)

    near_ref[...] = jnp.zeros(near_ref.shape, F32)
    inner = jnp.zeros((ROWS, LANES), F32)
    outer = jnp.zeros((ROWS, LANES), F32)
    for p in range(lay.packs):
        own, far = pack_ref[tile(p), :], beyond(p, half)
        delta_ref[tile(p), :] = far - own
        near_ref[p : p + 1, :] = far[0:1]
        near_ref[lay.pad + p : lay.pad + p + 1, :] = far[ROWS - 1 : ROWS]
        inner = inner + spread(own, 3) * across(far)
        outer = outer + spread(far, 3) * across(own)
    inner, outer = fold(sign * inner), fold(sign * outer)
    strip = beyond(lay.packs, lax.rem(lane, STRIP) < STRIP // 2)
    for f in range(FLAT):
        value = flat_ref[tile(f), :]
        if 2 <= f <= 3:
            border = (lane == 0) | (lane == LANES - 1)
            value = value + jnp.where(border, roll(inner, -(SLOT * f + SLOT // 2), 1), 0.0)
            mid = STRIP * f + STRIP // 2
            border = (lane == mid - 1) | (lane == mid)
            strip = strip + jnp.where(border, roll(outer, mid - (SLOT * f + SLOT // 2), 1), 0.0)
        own_ref[tile(f), :] = value
    own_ref[tile(FLAT), :] = strip

    def fill(low_ref, high_ref):
        for r in range(2):
            for s in range(lay.eights):
                to = tile(r * lay.eights + s)
                low_ref[to, :] = m_ref[pl.ds(ROWS * ROWS * s + r, ROWS, stride=ROWS), :]
                high_ref[to, :] = m_ref[pl.ds(ROWS * ROWS * s + ROWS - 2 + r, ROWS, stride=ROWS), :]
        low_ref[pl.ds(lay.edge, lay.pad), :] = near_ref[0 : lay.pad, :]
        high_ref[pl.ds(lay.edge, lay.pad), :] = near_ref[lay.pad :, :]
        for ref in (low_ref, high_ref):
            ref[pl.ds(lay.delta, lay.pad), :] = jnp.zeros((lay.pad, LANES), F32)
            ref[pl.ds(lay.flat, (FLAT + 1) * ROWS), :] = own_ref[...]
        for p in range(lay.packs):
            low_ref[pl.ds(lay.delta + p, 1), :] = delta_ref[pl.ds(ROWS * p, 1), :]
            high_ref[pl.ds(lay.delta + p, 1), :] = delta_ref[pl.ds(ROWS * p + ROWS - 1, 1), :]

    pl.when(at.b_even)(lambda: fill(two_ref, one_ref))
    pl.when(jnp.logical_not(at.b_even))(lambda: fill(one_ref, two_ref))


def moment_kernel(m_ref, own_ref, near_ref, one_ref, two_ref, basis_ref, send_ref, wide_ref):
    lay = Layout(m_ref.shape[0] // ROWS)
    at = Place()
    row, lane = iota(0), iota(1)
    outside = (lane < STRIP // 2) | (lane >= LANES - STRIP // 2)
    rows = 3 * ROWS

    def neighbours(where):
        return at.from_up(one_ref[where, :], two_ref[where, :]), at.from_down(one_ref[where, :], two_ref[where, :])

    strips = neighbours(pl.ds(lay.strip, ROWS))
    strips = (strips[0], own_ref[tile(FLAT), :], strips[1])
    for f in range(FLAT):
        fields = neighbours(pl.ds(lay.flat + f * ROWS, ROWS))
        fields = (fields[0], own_ref[tile(f), :], fields[1])
        for k in range(3):
            to = pl.ds(f * rows + k * ROWS, ROWS)
            wide_ref[to, 0:LANES] = fields[k]
            side = roll(strips[k], -(STRIP * f + STRIP // 2), 1)
            wide_ref[to, LANES : 2 * LANES] = jnp.where(outside, side, 0.0)

    comp = lax.rem(row, COMPS)
    cross = [jnp.zeros((ROWS, LANES), F32) for _ in range(4)]
    for s in range(lay.eights):
        above = neighbours(tile(lay.eights + s))[0]
        below = neighbours(tile(s))[1]
        top = m_ref[pl.ds(ROWS * ROWS * s, ROWS, stride=ROWS), :]
        bottom = m_ref[pl.ds(ROWS * ROWS * s + ROWS - 1, ROWS, stride=ROWS), :]

        def flow(x):
            return jnp.where(comp == 3, roll(x, 1, 0), x)

        cross[0] = cross[0] + flow(above) * top
        cross[1] = cross[1] - flow(top) * above
        cross[2] = cross[2] + flow(bottom) * below
        cross[3] = cross[3] - flow(below) * bottom
    cross = [0.5 * (x + roll(x, COMPS, 0)) for x in cross]
    above, below = neighbours(pl.ds(lay.edge, lay.pad))
    top, bottom = near_ref[0 : lay.pad, :], near_ref[lay.pad :, :]

    def flow_packed(x):
        return roll(x, SLOT, 1)

    def corner(a, b):
        comp = lax.rem(iota(1, lay.pad) // SLOT, COMPS)
        x = jnp.where(comp == 3, flow_packed(a), a) * b
        return 0.5 * fold(jnp.sum(x, axis=0, keepdims=True))

    corners = [corner(above, top), -corner(top, above), corner(bottom, below), -corner(below, bottom)]
    border = (iota(1, 1) < SLOT // 2) | (iota(1, 1) >= LANES - SLOT // 2)
    for f in (2, 3):
        for k, at_row in enumerate((ROWS - 1, ROWS, 2 * ROWS - 1, 2 * ROWS)):
            to = pl.ds(f * rows + at_row, 1)
            wide_ref[to, 0:LANES] = wide_ref[to, 0:LANES] + cross[k][f : f + 1]
            side = roll(corners[k], -(SLOT * f + SLOT // 2), 1)
            wide_ref[to, LANES : 2 * LANES] = wide_ref[to, LANES : 2 * LANES] + jnp.where(border, side, 0.0)

    sum_u, sum_v, adv_u, adv_v, forcing, diagonal = [wide_ref[pl.ds(f * rows, rows), :] for f in range(FLAT)]
    sea = jnp.where(diagonal > 0.0, 1.0, 0.0)
    shape = (rows, 2 * LANES)
    i = iota(0, *shape) - ROWS + at.b * ROWS
    j = iota(1, *shape)
    j = jnp.where(j < LANES + LANES // 2, j, j - 2 * LANES) + at.g * LANES
    total_rows, total_cols = at.nb * ROWS, at.ng * LANES
    edges = (
        jnp.where(i == 0, 1.0, 0.0)
        + jnp.where(i == total_rows - 1, 1.0, 0.0)
        + jnp.where(j == 0, 1.0, 0.0)
        + jnp.where(j == total_cols - 1, 1.0, 0.0)
    )
    coriolis = rotation * (2.0 * (j.astype(F32) + 0.5) / total_cols - 1.0)

    def both(x, n, axis):
        return roll(x, n, axis) + roll(x, -n, axis)

    def transport(x, turn, adv):
        near = both(x, 1, 0)
        linear = (
            (1.0 - hyper_visc * (20.0 - edges)) * x
            + 8.0 * hyper_visc * near
            - hyper_visc * (both(x, 2, 0) + both(x, 2, 1))
            + both(8.0 * hyper_visc * x - 2.0 * hyper_visc * near, 1, 1)
        )
        return sea * (linear + time_step * (turn - adv)) / lay.levels

    east = transport(sum_u, coriolis * sum_v, adv_u)
    north = transport(sum_v, -coriolis * sum_u, adv_v)
    divergence = 0.5 * (roll(east, -1, 0) - roll(east, 1, 0) + roll(north, -1, 1) - roll(north, 1, 1))
    v = [forcing - gravity * sea * divergence]
    own_diagonal = diagonal - SHIFT
    for _ in range(ITERS):
        x = v[-1]
        v.append(own_diagonal * x - sea * (both(x, 1, 0) + both(x, 1, 1)))
    v = [x[ROWS : 2 * ROWS, 0:LANES] for x in v]
    for k in range(ITERS):
        basis_ref[tile(k), :] = v[k]
    line = jnp.zeros((ROWS, LANES), F32)
    for k in range(2 * ITERS):
        part = jnp.sum(v[k // 2] * v[k - k // 2], axis=0, keepdims=True)
        line = jnp.where(row == k, part, line)
    line = jnp.sum(line, axis=1, keepdims=True)
    line = jnp.sum(jnp.where(row == lane, line, 0.0), axis=0, keepdims=True)
    send_ref[...] = jnp.broadcast_to(line, send_ref.shape)


def solve_kernel(got_ref, basis_ref, out_ref):
    line = jnp.sum(got_ref[...], axis=0, keepdims=True)
    lane = iota(1, 1)
    moment = [jnp.sum(jnp.where(lane == k, line, 0.0), axis=1, keepdims=True) for k in range(2 * ITERS)]

    def dot(a, b):
        total = None
        for k in range(len(a) + len(b) - 1):
            weight = sum(a[n] * b[k - n] for n in range(len(a)) if 0 <= k - n < len(b))
            total = weight * moment[k] if total is None else total + weight * moment[k]
        return total

    def add(a, scale, b):
        out = list(a) + [0.0] * (len(b) - len(a))
        return [x + scale * b[n] if n < len(b) else x for n, x in enumerate(out)]

    def image(a):
        return [SHIFT * (a[n] if n < len(a) else 0.0) + (a[n - 1] if n else 0.0) for n in range(len(a) + 1)]

    one = jnp.ones((1, 1), F32)
    residual, direction, surface = [one], [one], []
    norm = dot(residual, residual)
    for iteration in range(ITERS):
        applied = image(direction)
        alpha = norm / dot(direction, applied)
        surface = add(surface, alpha, direction)
        if iteration + 1 < ITERS:
            residual = add(residual, -alpha, applied)
            following = dot(residual, residual)
            direction = add(residual, following / norm, direction)
            norm = following
    out = surface[0] * basis_ref[tile(0), :]
    for k in range(1, ITERS):
        out = out + surface[k] * basis_ref[tile(k), :]
    out_ref[...] = out


def step_kernel(m_ref, pack_ref, delta_ref, one_ref, two_ref, mask_ref, new_ref, ext_ref, corr_ref):
    lay = Layout(m_ref.shape[0] // ROWS)
    at = Place()
    row, lane = iota(0), iota(1)
    for t in range(lay.tiles):
        ext_ref[pl.ds(EXT * t + 2, ROWS), :] = m_ref[tile(t), :]
    for r in range(2):
        for s in range(lay.eights):
            one, two = one_ref[tile(r * lay.eights + s), :], two_ref[tile(r * lay.eights + s), :]
            ext_ref[pl.ds(EXT * ROWS * s + r, ROWS, stride=EXT), :] = at.from_up(one, two)
            ext_ref[pl.ds(EXT * ROWS * s + ROWS + 2 + r, ROWS, stride=EXT), :] = at.from_down(one, two)

    in_slot = lax.rem(lane, SLOT)
    half = in_slot < SLOT // 2
    near = (in_slot == 3) | (in_slot == 4)
    far = (in_slot >= 2) & (in_slot <= 5)
    sign = jnp.where(in_slot == 3, -0.5 * time_step, jnp.where(in_slot == 4, 0.5 * time_step, 0.0))
    for p in range(lay.packs):
        d = delta_ref[tile(p), :]
        one, two = one_ref[pl.ds(lay.delta + p, 1), :], two_ref[pl.ds(lay.delta + p, 1), :]
        dv = jnp.where(row == 0, at.from_up(one, two), roll(d, 1, 0)) + jnp.where(
            row == ROWS - 1, at.from_down(one, two), roll(d, -1, 0)
        )
        second = jnp.where(half, roll(d, -2, 1), roll(d, 2, 1))
        corr_ref[tile(p), :] = (
            jnp.where(far, -hyper_visc * second, 0.0)
            + jnp.where(near, across(hyper_visc * (8.0 * d - 2.0 * dv)), 0.0)
            + sign * spread(pack_ref[tile(p), :], 3) * across(d)
        )

    sea = mask_ref[...].astype(F32)
    edges = (
        jnp.where((row == 0) & (at.b == 0), 1.0, 0.0)
        + jnp.where((row == ROWS - 1) & (at.b == at.nb - 1), 1.0, 0.0)
        + jnp.where((lane == 0) & (at.g == 0), 1.0, 0.0)
        + jnp.where((lane == LANES - 1) & (at.g == at.ng - 1), 1.0, 0.0)
    )
    centre = 1.0 - 2.0 * mixing - hyper_visc * (20.0 - edges)
    col = (lane + at.g * LANES).astype(F32)
    coriolis = time_step * rotation * (2.0 * (col + 0.5) / (at.ng * LANES) - 1.0)
    border = (lane < SLOT // 2) | (lane >= LANES - SLOT // 2)

    def own(level, c):
        return m_ref[tile(COMPS * min(max(level, 0), lay.levels - 1) + c), :]

    for k in range(lay.levels):
        u, v = own(k, 2), own(k, 3)
        half_u, half_v = 0.5 * time_step * u, 0.5 * time_step * v
        for c in range(COMPS):
            t = COMPS * k + c
            x = own(k, c)
            up2, up1, dn1, dn2 = [ext_ref[pl.ds(EXT * t + n, ROWS), :] for n in (0, 1, 3, 4)]
            left, right = roll(x, 1, 1), roll(x, -1, 1)
            near1 = up1 + dn1
            q = 8.0 * hyper_visc * x - 2.0 * hyper_visc * near1
            out = (
                centre * x
                + (roll(q, 1, 1) + roll(q, -1, 1))
                + 8.0 * hyper_visc * near1
                - hyper_visc * ((up2 + dn2) + (roll(x, 2, 1) + roll(x, -2, 1)))
                - (half_u * (dn1 - up1) + half_v * (right - left))
                + mixing * (own(k - 1, c) + own(k + 1, c))
            )
            if c == 2:
                out = out + coriolis * v
            if c == 3:
                out = out - coriolis * u
            p, s = divmod(t, PER)
            fix = roll(corr_ref[tile(p), :], -(SLOT * s + SLOT // 2), 1)
            new_ref[tile(t), :] = sea * (out + jnp.where(border, fix, 0.0))


def call(kernel, outs, *args, scratch=(), specs=None, flops=0):
    return pl.pallas_call(
        kernel,
        out_shape=[jax.ShapeDtypeStruct(s, F32) for s in outs],
        in_specs=specs or [VMEM] * len(args),
        out_specs=[VMEM] * len(outs),
        scratch_shapes=[pltpu.VMEM(s, F32) if isinstance(s, tuple) else s for s in scratch],
        compiler_params=pltpu.CompilerParams(vmem_limit_bytes=32 * 1024 * 1024),
        cost_estimate=pl.CostEstimate(flops=flops, bytes_accessed=0, transcendentals=0),
    )(*args)


def on_device(ocean_state, surface_height, surface_damping, land_mask, *, shape):
    nb, ng = shape
    axes = ("blocks", "group")
    state = ocean_state.reshape(-1, LANES)
    lay = Layout(state.shape[0] // ROWS)
    g_one, g_two = swap_pairs(shape, "group")
    b_one, b_two = swap_pairs(shape, "blocks")
    one_tile = (ROWS, LANES)
    packed = (lay.packs * ROWS, LANES)
    flats = (FLAT * ROWS, LANES)

    m, pack, flat = call(
        pack_kernel,
        [state.shape, (packed[0] + ROWS, LANES), flats],
        state,
        land_mask,
        surface_height,
        surface_damping,
        specs=[HBM] * 4,
        scratch=[
            state.shape,
            pltpu.VMEM(one_tile, land_mask.dtype),
            one_tile,
            one_tile,
            pltpu.SemaphoreType.DMA((3 + lay.packs,)),
        ],
    )
    first = lax.ppermute(pack, axes, g_one)
    second = lax.ppermute(pack, axes, g_two)
    message = (lay.rows, LANES)
    own, near, delta, one, two = call(
        edge_kernel,
        [(flats[0] + ROWS, LANES), (2 * lay.pad, LANES), packed, message, message],
        m,
        pack,
        flat,
        first,
        second,
    )
    one = lax.ppermute(one, axes, b_one)
    two = lax.ppermute(two, axes, b_two)
    basis, sent = call(
        moment_kernel,
        [(ITERS * ROWS, LANES), (nb * ng, LANES)],
        m,
        own,
        near,
        one,
        two,
        scratch=[(FLAT * 3 * ROWS, 2 * LANES)],
    )
    got = lax.all_to_all(sent, axes, 0, 0, tiled=True)
    (new_state,) = call(
        step_kernel, [state.shape], m, pack, delta, one, two, land_mask, scratch=[(lay.tiles * EXT, LANES), packed],
        flops=20_000_000,
    )
    (surface,) = call(solve_kernel, [one_tile], got, basis)
    return new_state.reshape(ocean_state.shape), surface


def solution(mesh):
    placed = (
        P(None, None, "blocks", "group"),
        P("blocks", "group"),
        P("blocks", "group"),
        P("blocks", "group"),
    )
    shape = (mesh.shape["blocks"], mesh.shape["group"])

    def body(*args):
        return on_device(*args, shape=shape)

    return jax.shard_map(
        body,
        mesh=mesh,
        in_specs=placed,
        out_specs=(P(None, None, "blocks", "group"), P("blocks", "group")),
        check_vma=False,
    )
```

time: 221 us -> 34.4 us (0.16)
  blocking collectives: 128 us -> 0 us
  starting transfers between devices: 52 us -> 13.2 us
  other arithmetic: 12.1 us -> 0 us
  between operations: 7.91 us -> 0.69 us
  Pallas kernels: 0 us -> 6.38 us
  waiting for transfers between devices: 13.6 us -> 10.7 us
    psum x10 -> x0, blocking collectives: 128 us -> none  [the longest x5 72.3 us: global_total(): part_sum = lax.psum(value, 'blocks')]
    ppermute x20 -> x4, starting transfers between devices: 52 us -> 6.37 us  [the longest x1 3.21 us: on_device(): two = lax.ppermute(two, axes, b_two)]
    ppermute x20 -> x4, waiting for transfers between devices: 13.6 us -> 5.59 us  [the longest x1 3.6 us: on_device(): two = lax.ppermute(two, axes, b_two)]
    all_to_all x0 -> x1, starting transfers between devices: none -> 6.84 us  [on_device(): got = lax.all_to_all(sent, axes, 0, 0, tiled=True)]
    pallas_call x0 -> x5, Pallas kernels: none -> 6.38 us  [call(): pl.pallas_call(kernel, out_shape=[jax.ShapeDtypeStruct(s, F32) for s in o...]
    all_to_all x0 -> x1, waiting for transfers between devices: none -> 5.11 us  [on_device(): got = lax.all_to_all(sent, axes, 0, 0, tiled=True)]
    mul x5 -> x0, other arithmetic: 4.71 us -> none  [the longest x1 2.33 us: on_device(): new_state = sea_mask * updated]
    reduce_sum x6 -> x0, other arithmetic: 3.28 us -> none  [the longest x3 2.04 us: on_device(): step_size = norm_now / global_total(jnp.sum(direction * applied))]
  transfers between devices with their start and end apart: 20 -> 5, of which waited for: 10 -> 3; matrix products, arithmetic and copies ran while one was open for 1% -> 0% of each run, Pallas kernels for 0% -> 6%
where the time goes in v2:
time: 34.4 us; the launch traced here: 34.1 us
  starting transfers between devices  13.2 us (38%)
  waiting for transfers between devices  10.7 us (31%)
  Pallas kernels  6.38 us (19%)
  local copies, waits for them, and re-layouts  3.12 us (9%)
  between operations  0.69 us (2%)
    all_to_all x1, starting transfers between devices, on_device(): got = lax.all_to_all(sent, axes, 0, 0, tiled=True)  6.84 us
    pallas_call x5, Pallas kernels, call(): pl.pallas_call(kernel, out_shape=[jax.ShapeDtypeStruct(s, F32) for s in o...  6.38 us
    all_to_all x1, waiting for transfers between devices, on_device(): got = lax.all_to_all(sent, axes, 0, 0, tiled=True)  5.11 us
    ppermute x1, waiting for transfers between devices, on_device(): two = lax.ppermute(two, axes, b_two)  3.6 us
    ppermute x1, starting transfers between devices, on_device(): two = lax.ppermute(two, axes, b_two)  3.21 us
    unnamed x10, local copies, waits for them, and re-layouts  3.12 us
    ppermute x1, starting transfers between devices, on_device(): first = lax.ppermute(pack, axes, g_one)  3.09 us
    ppermute x1, waiting for transfers between devices, on_device(): first = lax.ppermute(pack, axes, g_one)  1.98 us
  transfers between devices with their start and end apart: 5, of which 3 were waited for; matrix products, arithmetic and copies ran while one was open for 0% of the time, Pallas kernels for 6%

profile of v2, /device:TPU:0, one launch (start us, length us, event | category | flops | bytes accessed | tf_op | source)
XLA Modules:
  0.0 34.1 jit_solution(8392026436867445937)
XLA Ops:
  0.6 0.0 copy-start
  0.6 1.1 %copy-done = f32[36,4,8,128]{3,2,1,0:T(8,128)S(1)} copy-done((f32[36,4,8,128]{3,2,1,0:T(8,128)S(1)}, f32[36,4,8,128]{3,2,1,0:T(8,128)}, u32[]{:S(2)}) %copy-start) | copy-done | bytes 589848
  1.7 0.0 copy-start.1
  1.7 0.7 %copy-done.1 = s32[8,128]{1,0:T(8,128)S(1)} copy-done((s32[8,128]{1,0:T(8,128)S(1)}, s32[8,128]{1,0:T(8,128)}, u32[]{:S(2)}) %copy-start.1) | copy-done | bytes 4120
  2.4 0.0 copy-start.3
  2.4 0.7 %copy-done.3 = f32[8,128]{1,0:T(8,128)S(1)} copy-done((f32[8,128]{1,0:T(8,128)S(1)}, f32[8,128]{1,0:T(8,128)}, u32[]{:S(2)}) %copy-start.3) | copy-done | bytes 4120
  3.1 0.0 copy-start.4
  3.1 0.7 %copy-done.4 = f32[8,128]{1,0:T(8,128)S(1)} copy-done((f32[8,128]{1,0:T(8,128)S(1)}, f32[8,128]{1,0:T(8,128)}, u32[]{:S(2)}) %copy-start.4) | copy-done | bytes 4120
  3.8 1.9 %shard_map.59 = (f32[1152,128]{1,0:T(8,128)S(1)}, f32[80,128]{1,0:T(8,128)S(1)}, f32[48,128]{1,0:T(8,128)S(1)}) custom-call(f32[1152,128]{1,0:T(8,128)S(1)} %bitcast.6, s32[8,128]{1,0:T(8,128)S(1)} %copy-done.1, f32[8,128]{1,0:T(8,128)S(1)} %copy-done.3, f32[8,128]{1,0:T(8,128)S(1)} %copy-done.4), custom_call_target="tpu_custom_call" | custom-call | tf_op jit(solution)/shard_map/pallas_call | solution.py:433
  5.6 3.1 %collective-permute-start = (f32[80,128]{1,0:T(8,128)S(1)}, f32[80,128]{1,0:T(8,128)S(1)}, u32[]{:S(2)}, u32[]{:S(2)}) collective-permute-start(f32[80,128]{1,0:T(8,128)S(1)} %get-tuple-element.13.pack_ref), channel_id=1, source_target_pairs={{0,1},{1,0},{2,3},{3,2},{4,5},{5,4},{6,7},{7,6},{8,9},{9,8},{10,11... | collective-permute-start | bytes 122888 | tf_op jit(solution)/shard_map/ppermute | solution.py:471
  8.7 0.0 collective-permute-start.1
  8.7 2.0 %collective-permute-done.first_ref = f32[80,128]{1,0:T(8,128)S(1)} collective-permute-done((f32[80,128]{1,0:T(8,128)S(1)}, f32[80,128]{1,0:T(8,128)S(1)}, u32[]{:S(2)}, u32[]{:S(2)}) %collective-permute-start) | collective-permute-done | bytes 40992 | tf_op jit(solution)/shard_map/ppermute | solution.py:471
  10.7 0.0 collective-permute-done.1.second_ref
  10.7 0.4 %shard_map.60 = (f32[56,128]{1,0:T(8,128)S(1)}, f32[32,128]{1,0:T(8,128)S(1)}, f32[72,128]{1,0:T(8,128)S(1)}, f32[376,128]{1,0:T(8,128)S(1)}, f32[376,128]{1,0:T(8,128)S(1)}) custom-call(f32[1152,128]{1,0:T(8,128)S(1)} %get-tuple-element.12.m_ref, f32[80,128]{1,0:T(8,128)S(1)} %get-tuple-element.13.pack_ref, f32[48,128]{1,0:T(8,128)S(1)} %get-tuple-element.14.flat_ref, ...), custom_call_target="tpu_custom_call" | custom-call | tf_op jit(solution)/shard_map/pallas_call | solution.py:433
  11.1 0.1 collective-permute-start.2
  11.2 3.2 %collective-permute-start.3 = (f32[376,128]{1,0:T(8,128)S(1)}, f32[376,128]{1,0:T(8,128)S(1)}, u32[]{:S(2)}, u32[]{:S(2)}) collective-permute-start(f32[376,128]{1,0:T(8,128)S(1)} %get-tuple-element.17), channel_id=1, source_target_pairs={{0,1},{1,0},{2,3},{3,2},{4,8},{5,9},{6,10},{7,11},{8,4},{9,5},{10,... | collective-permute-start | bytes 577544 | tf_op jit(solution)/shard_map/ppermute | solution.py:484
  14.4 0.0 collective-permute-done.2.one_ref
  14.4 3.6 %collective-permute-done.3.two_ref = f32[376,128]{1,0:T(8,128)S(1)} collective-permute-done((f32[376,128]{1,0:T(8,128)S(1)}, f32[376,128]{1,0:T(8,128)S(1)}, u32[]{:S(2)}, u32[]{:S(2)}) %collective-permute-start.3) | collective-permute-done | bytes 192544 | tf_op jit(solution)/shard_map/ppermute | solution.py:484
  18.0 1.3 %shard_map.62 = (f32[24,128]{1,0:T(8,128)S(1)}, f32[32,128]{1,0:T(8,128)}) custom-call(f32[1152,128]{1,0:T(8,128)S(1)} %get-tuple-element.12.m_ref, f32[56,128]{1,0:T(8,128)S(1)} %get-tuple-element.18.own_ref, f32[32,128]{1,0:T(8,128)S(1)} %get-tuple-element.19.near_ref, f32[376,128]{1,0:T(8,128)S(1)} %collective-permute-done.2.one_ref, ...), custom_call_target="tpu_custom_call" | custom-call | tf_op jit(solution)/shard_map/pallas_call | solution.py:433
  19.3 0.0 copy-start.2
  19.3 6.8 %all-to-all-start = ((f32[32,1,128]{2,1,0:T(1,128)}), f32[32,1,128]{2,1,0:T(1,128)S(1)}, u32[]{:S(2)}, u32[]{:S(2)}) async-start(f32[32,1,128]{2,1,0:T(1,128)} %bitcast.3), calls=%async_computation | async-start | bytes 32768 | tf_op jit(solution)/shard_map/all_to_all | solution.py:495
  26.2 0.0 copy-done.2
  26.2 2.1 %shard_map.61 = f32[1152,128]{1,0:T(8,128)} custom-call(f32[1152,128]{1,0:T(8,128)S(1)} %get-tuple-element.12.m_ref, f32[80,128]{1,0:T(8,128)S(1)} %get-tuple-element.13.pack_ref, f32[72,128]{1,0:T(8,128)S(1)} %get-tuple-element.15.delta_ref, f32[376,128]{1,0:T(8,128)S(1)} %collective-permute-done.2.one_ref, f32[376,128]{1,0:T(8,128)S(1)} %collective-permute-done.3.two_ref, ...), custom_call_target="tpu_custom_call" | custom-call | flops 20000000 | tf_op jit(solution)/shard_map/pallas_call | solution.py:433
  28.2 5.1 %all-to-all-done = f32[32,1,128]{2,1,0:T(1,128)S(1)} async-done(((f32[32,1,128]{2,1,0:T(1,128)}), f32[32,1,128]{2,1,0:T(1,128)S(1)}, u32[]{:S(2)}, u32[]{:S(2)}) %all-to-all-start) | async-done | bytes 16416 | tf_op jit(solution)/shard_map/all_to_all | solution.py:495
  33.4 0.7 %shard_map.63 = f32[8,128]{1,0:T(8,128)} custom-call(f32[32,128]{1,0:T(8,128)S(1)} %bitcast.7, f32[24,128]{1,0:T(8,128)S(1)} %get-tuple-element.21.basis_ref), custom_call_target="tpu_custom_call" | custom-call | tf_op jit(solution)/shard_map/pallas_call | solution.py:433
Async XLA Ops:
  0.6 1.1 %copy-start = (f32[36,4,8,128]{3,2,1,0:T(8,128)S(1)}, f32[36,4,8,128]{3,2,1,0:T(8,128)}, u32[]{:S(2)}) copy-start(f32[36,4,8,128]{3,2,1,0:T(8,128)} %param.4) | copy-start | bytes 1769476
  1.7 0.7 %copy-start.1 = (s32[8,128]{1,0:T(8,128)S(1)}, s32[8,128]{1,0:T(8,128)}, u32[]{:S(2)}) copy-start(s32[8,128]{1,0:T(8,128)} %mask_ref.1) | copy-start | bytes 12292
  2.4 0.7 %copy-start.3 = (f32[8,128]{1,0:T(8,128)S(1)}, f32[8,128]{1,0:T(8,128)}, u32[]{:S(2)}) copy-start(f32[8,128]{1,0:T(8,128)} %height_hbm.1) | copy-start | bytes 12292
  3.1 0.7 %copy-start.4 = (f32[8,128]{1,0:T(8,128)S(1)}, f32[8,128]{1,0:T(8,128)}, u32[]{:S(2)}) copy-start(f32[8,128]{1,0:T(8,128)} %damp_hbm.1) | copy-start | bytes 12292
  5.6 5.1 %collective-permute-start = (f32[80,128]{1,0:T(8,128)S(1)}, f32[80,128]{1,0:T(8,128)S(1)}, u32[]{:S(2)}, u32[]{:S(2)}) collective-permute-start(f32[80,128]{1,0:T(8,128)S(1)} %get-tuple-element.13.pack_ref), channel_id=1, source_target_pairs={{0,1},{1,0},{2,3},{3,2},{4,5},{5,4},{6,7},{7,6},{8,9},{9,8},{10,11... | collective-permute-start | bytes 122888 | tf_op jit(solution)/shard_map/ppermute | solution.py:471
  8.7 2.0 %collective-permute-start.1 = (f32[80,128]{1,0:T(8,128)S(1)}, f32[80,128]{1,0:T(8,128)S(1)}, u32[]{:S(2)}, u32[]{:S(2)}) collective-permute-start(f32[80,128]{1,0:T(8,128)S(1)} %get-tuple-element.13.pack_ref), channel_id=1, source_target_pairs={{0,4},{1,2},{2,1},{3,7},{4,0},{5,6},{6,5},{7,3},{8,12},{9,10},{10,... | collective-permute-start | bytes 122888 | tf_op jit(solution)/shard_map/ppermute | solution.py:472
  11.1 3.3 %collective-permute-start.2 = (f32[376,128]{1,0:T(8,128)S(1)}, f32[376,128]{1,0:T(8,128)S(1)}, u32[]{:S(2)}, u32[]{:S(2)}) collective-permute-start(f32[376,128]{1,0:T(8,128)S(1)} %get-tuple-element.16), channel_id=1, source_target_pairs={{0,4},{1,5},{2,6},{3,7},{4,0},{5,1},{6,2},{7,3},{8,12},{9,13},{10,... | collective-permute-start | bytes 577544 | tf_op jit(solution)/shard_map/ppermute | solution.py:483
  11.2 6.8 %collective-permute-start.3 = (f32[376,128]{1,0:T(8,128)S(1)}, f32[376,128]{1,0:T(8,128)S(1)}, u32[]{:S(2)}, u32[]{:S(2)}) collective-permute-start(f32[376,128]{1,0:T(8,128)S(1)} %get-tuple-element.17), channel_id=1, source_target_pairs={{0,1},{1,0},{2,3},{3,2},{4,8},{5,9},{6,10},{7,11},{8,4},{9,5},{10,... | collective-permute-start | bytes 577544 | tf_op jit(solution)/shard_map/ppermute | solution.py:484
  19.3 6.9 %copy-start.2 = (s32[8,128]{1,0:T(8,128)S(1)}, s32[8,128]{1,0:T(8,128)}, u32[]{:S(2)}) copy-start(s32[8,128]{1,0:T(8,128)} %mask_ref.1) | copy-start | bytes 12292
  19.3 14.0 %all-to-all-start = ((f32[32,1,128]{2,1,0:T(1,128)}), f32[32,1,128]{2,1,0:T(1,128)S(1)}, u32[]{:S(2)}, u32[]{:S(2)}) async-start(f32[32,1,128]{2,1,0:T(1,128)} %bitcast.3), calls=%async_computation | async-start | bytes 32768 | tf_op jit(solution)/shard_map/all_to_all | solution.py:495

commit v3 on v2

--- a/solution.py
+++ b/solution.py
@@ -21,6 +21,8 @@
 EXT = 12
 FLAT = 6
 STRIP = 16
+FL_A = 10**9
+FL_B = 10**9
 SHIFT = 4.5
 F32 = jnp.float32
 VMEM = pl.BlockSpec(memory_space=pltpu.VMEM)
@@ -65,11 +67,24 @@
         self.packs = tiles // PER
         self.eights = tiles // ROWS
         self.pad = -(-self.packs // ROWS) * ROWS
-        self.edge = 2 * tiles
-        self.delta = self.edge + self.pad
-        self.flat = self.delta + self.pad
+        self.flow = -(-self.levels // ROWS) * ROWS
+        self.edge = 2 * self.flow
+        self.flat = self.edge + self.pad
         self.strip = self.flat + FLAT * ROWS
-        self.rows = self.strip + ROWS
+        self.first = self.strip + ROWS
+        self.delta = 2 * tiles
+        self.second = self.delta + self.pad
+
+    def level_rows(self, m_ref, comp, row):
+        step = COMPS * ROWS
+        parts = []
+        for start in range(0, self.levels, ROWS):
+            count = min(ROWS, self.levels - start)
+            x = m_ref[pl.ds(start * step + comp * ROWS + row, count, stride=step), :]
+            if count < ROWS:
+                x = jnp.concatenate([x, jnp.zeros((ROWS - count, LANES), F32)], axis=0)
+            parts.append(x)
+        return parts
 
 
 class Place:
@@ -102,15 +117,18 @@
         copies.append(pltpu.make_async_copy(state_hbm.at[at], state_ref.at[at], sems.at[3 + p]))
     for copy in copies:
         copy.start()
-    for copy in copies[:3]:
+    for copy in copies[: 3 + lay.packs // 2]:
         copy.wait()
     sea = mask_ref[...].astype(F32)
     row, lane = iota(0), iota(1)
     slot = lane // SLOT
-    sums = [jnp.zeros((ROWS, LANES), F32) for _ in range(4)]
+    sum_u = sum_v = uu = uv = vu = zero = jnp.zeros((ROWS, LANES), F32)
+    across_u = across_v = across_vu = zero
     for p in range(lay.packs):
-        copies[3 + p].wait()
-        acc = jnp.zeros((ROWS, LANES), F32)
+        if p == lay.packs // 2:
+            for copy in copies[3 + p :]:
+                copy.wait()
+        acc = zero
         for k in range(PER // COMPS):
             x = []
             for c in range(COMPS):
@@ -118,18 +136,26 @@
                 x.append(state_ref[tile(p * PER + q), :] * sea)
                 m_ref[tile(p * PER + q), :] = x[c]
                 acc = jnp.where(slot == q, roll(x[c], SLOT * q + SLOT // 2, 1), acc)
-            u_up, u_down = jnp.where(row == 0, 0.0, x[2]), jnp.where(row == ROWS - 1, 0.0, x[2])
-            v_left, v_right = jnp.where(lane == 0, 0.0, x[3]), jnp.where(lane == LANES - 1, 0.0, x[3])
-            for f in range(2):
-                y = x[2 + f]
-                sums[f] = sums[f] + y
-                sums[2 + f] = sums[2 + f] + (
-                    (u_down * roll(y, -1, 0) - u_up * roll(y, 1, 0))
-                    + (v_right * roll(y, -1, 1) - v_left * roll(y, 1, 1))
-                )
+            u, v = x[2:]
+            below_u, below_v = roll(u, -1, 0), roll(v, -1, 0)
+            right_u, right_v = roll(u, -1, 1), roll(v, -1, 1)
+            sum_u, sum_v = sum_u + u, sum_v + v
+            uu, uv, vu = uu + u * below_u, uv + u * below_v, vu + v * below_u
+            across_u, across_v, across_vu = across_u + v * right_u, across_v + v * right_v, across_vu + u * right_v
         pack_ref[tile(p), :] = acc
+
+    def step_down(ahead, back):
+        inner = row < ROWS - 1
+        return jnp.where(inner, ahead, 0.0) - roll(jnp.where(inner, back, 0.0), 1, 0)
+
+    def step_right(ahead, back):
+        inner = lane < LANES - 1
+        return jnp.where(inner, ahead, 0.0) - roll(jnp.where(inner, back, 0.0), 1, 1)
+
+    advect_u = 0.5 * (step_down(uu, uu) + step_right(across_u, across_vu))
+    advect_v = 0.5 * (step_down(uv, vu) + step_right(across_v, across_v))
     damp = damp_ref[...]
-    flat = [sums[0], sums[1], 0.5 * sums[2], 0.5 * sums[3], sea * damp * height_ref[...], sea * (4.0 + damp)]
+    flat = [sum_u, sum_v, advect_u, advect_v, sea * damp * height_ref[...], sea * (4.0 + damp)]
     acc = jnp.zeros((ROWS, LANES), F32)
     for f in range(FLAT):
         flat_ref[tile(f), :] = flat[f]
@@ -159,7 +185,9 @@
     return x
 
 
-def edge_kernel(m_ref, pack_ref, flat_ref, first_ref, second_ref, own_ref, near_ref, delta_ref, one_ref, two_ref):
+def edge_kernel(
+    m_ref, pack_ref, flat_ref, first_ref, second_ref, own_ref, near_ref, delta_ref, one_ref, two_ref
+):
     lay = Layout(m_ref.shape[0] // ROWS)
     at = Place()
     lane = iota(1)
@@ -197,19 +225,30 @@
     own_ref[tile(FLAT), :] = strip
 
     def fill(low_ref, high_ref):
-        for r in range(2):
-            for s in range(lay.eights):
-                to = tile(r * lay.eights + s)
-                low_ref[to, :] = m_ref[pl.ds(ROWS * ROWS * s + r, ROWS, stride=ROWS), :]
-                high_ref[to, :] = m_ref[pl.ds(ROWS * ROWS * s + ROWS - 2 + r, ROWS, stride=ROWS), :]
-        low_ref[pl.ds(lay.edge, lay.pad), :] = near_ref[0 : lay.pad, :]
-        high_ref[pl.ds(lay.edge, lay.pad), :] = near_ref[lay.pad :, :]
-        for ref in (low_ref, high_ref):
+        for ref, row, rows in ((low_ref, 0, slice(0, lay.pad)), (high_ref, ROWS - 1, slice(lay.pad, 2 * lay.pad))):
+            for c in (2, 3):
+                for n, x in enumerate(lay.level_rows(m_ref, c, row)):
+                    ref[pl.ds((c - 2) * lay.flow + n * ROWS, ROWS), :] = x
+            ref[pl.ds(lay.edge, lay.pad), :] = near_ref[rows, :]
+            ref[pl.ds(lay.flat, (FLAT + 1) * ROWS), :] = own_ref[...]
+
+    pl.when(at.b_even)(lambda: fill(two_ref, one_ref))
+    pl.when(jnp.logical_not(at.b_even))(lambda: fill(one_ref, two_ref))
+
+
+def rest_kernel(m_ref, delta_ref, one_ref, two_ref):
+    lay = Layout(m_ref.shape[0] // ROWS)
+    at = Place()
+
+    def fill(low_ref, high_ref):
+        for ref, row in ((low_ref, 0), (high_ref, ROWS - 1)):
+            for r in range(2):
+                for s in range(lay.eights):
+                    start = ROWS * ROWS * s + (row - 1 if row else 0) + r
+                    ref[tile(r * lay.eights + s), :] = m_ref[pl.ds(start, ROWS, stride=ROWS), :]
             ref[pl.ds(lay.delta, lay.pad), :] = jnp.zeros((lay.pad, LANES), F32)
-            ref[pl.ds(lay.flat, (FLAT + 1) * ROWS), :] = own_ref[...]
-        for p in range(lay.packs):
-            low_ref[pl.ds(lay.delta + p, 1), :] = delta_ref[pl.ds(ROWS * p, 1), :]
-            high_ref[pl.ds(lay.delta + p, 1), :] = delta_ref[pl.ds(ROWS * p + ROWS - 1, 1), :]
+            for p in range(lay.packs):
+                ref[pl.ds(lay.delta + p, 1), :] = delta_ref[pl.ds(ROWS * p + row, 1), :]
 
     pl.when(at.b_even)(lambda: fill(two_ref, one_ref))
     pl.when(jnp.logical_not(at.b_even))(lambda: fill(one_ref, two_ref))
@@ -236,22 +275,18 @@
             side = roll(strips[k], -(STRIP * f + STRIP // 2), 1)
             wide_ref[to, LANES : 2 * LANES] = jnp.where(outside, side, 0.0)
 
-    comp = lax.rem(row, COMPS)
-    cross = [jnp.zeros((ROWS, LANES), F32) for _ in range(4)]
-    for s in range(lay.eights):
-        above = neighbours(tile(lay.eights + s))[0]
-        below = neighbours(tile(s))[1]
-        top = m_ref[pl.ds(ROWS * ROWS * s, ROWS, stride=ROWS), :]
-        bottom = m_ref[pl.ds(ROWS * ROWS * s + ROWS - 1, ROWS, stride=ROWS), :]
-
-        def flow(x):
-            return jnp.where(comp == 3, roll(x, 1, 0), x)
-
-        cross[0] = cross[0] + flow(above) * top
-        cross[1] = cross[1] - flow(top) * above
-        cross[2] = cross[2] + flow(bottom) * below
-        cross[3] = cross[3] - flow(below) * bottom
-    cross = [0.5 * (x + roll(x, COMPS, 0)) for x in cross]
+    own_rows = [[lay.level_rows(m_ref, c, r) for c in (2, 3)] for r in (0, ROWS - 1)]
+    cross = []
+    for f in range(2):
+        total = [jnp.zeros((ROWS, LANES), F32) for _ in range(4)]
+        for n in range(lay.flow // ROWS):
+            flow = neighbours(tile(n))
+            carried = neighbours(pl.ds(f * lay.flow + n * ROWS, ROWS))
+            total[0] = total[0] + flow[0] * own_rows[0][f][n]
+            total[1] = total[1] - own_rows[0][0][n] * carried[0]
+            total[2] = total[2] + own_rows[1][0][n] * carried[1]
+            total[3] = total[3] - flow[1] * own_rows[1][f][n]
+        cross.append([0.5 * jnp.sum(x, axis=0, keepdims=True) for x in total])
     above, below = neighbours(pl.ds(lay.edge, lay.pad))
     top, bottom = near_ref[0 : lay.pad, :], near_ref[lay.pad :, :]
 
@@ -268,7 +303,7 @@
     for f in (2, 3):
         for k, at_row in enumerate((ROWS - 1, ROWS, 2 * ROWS - 1, 2 * ROWS)):
             to = pl.ds(f * rows + at_row, 1)
-            wide_ref[to, 0:LANES] = wide_ref[to, 0:LANES] + cross[k][f : f + 1]
+            wide_ref[to, 0:LANES] = wide_ref[to, 0:LANES] + cross[f - 2][k]
             side = roll(corners[k], -(SLOT * f + SLOT // 2), 1)
             wide_ref[to, LANES : 2 * LANES] = wide_ref[to, LANES : 2 * LANES] + jnp.where(border, side, 0.0)
 
@@ -320,7 +355,7 @@
     send_ref[...] = jnp.broadcast_to(line, send_ref.shape)
 
 
-def solve_kernel(got_ref, basis_ref, out_ref):
+def solve_kernel(got_ref, basis_ref, done_ref, out_ref):
     line = jnp.sum(got_ref[...], axis=0, keepdims=True)
     lane = iota(1, 1)
     moment = [jnp.sum(jnp.where(lane == k, line, 0.0), axis=1, keepdims=True) for k in range(2 * ITERS)]
@@ -357,7 +392,7 @@
     out_ref[...] = out
 
 
-def step_kernel(m_ref, pack_ref, delta_ref, one_ref, two_ref, mask_ref, new_ref, ext_ref, corr_ref):
+def step_kernel(m_ref, pack_ref, delta_ref, one_ref, two_ref, mask_ref, new_ref, done_ref, ext_ref, corr_ref):
     lay = Layout(m_ref.shape[0] // ROWS)
     at = Place()
     row, lane = iota(0), iota(1)
@@ -388,6 +423,7 @@
         )
 
     sea = mask_ref[...].astype(F32)
+    done_ref[...] = sea
     edges = (
         jnp.where((row == 0) & (at.b == 0), 1.0, 0.0)
         + jnp.where((row == ROWS - 1) & (at.b == at.nb - 1), 1.0, 0.0)
@@ -429,14 +465,14 @@
             new_ref[tile(t), :] = sea * (out + jnp.where(border, fix, 0.0))
 
 
-def call(kernel, outs, *args, scratch=(), specs=None, flops=0):
+def call(kernel, outs, *args, scratch=(), specs=None, flops=0, vmem=8):
     return pl.pallas_call(
         kernel,
-        out_shape=[jax.ShapeDtypeStruct(s, F32) for s in outs],
+        out_shape=[jax.ShapeDtypeStruct(s, F32) if isinstance(s, tuple) else s for s in outs],
         in_specs=specs or [VMEM] * len(args),
         out_specs=[VMEM] * len(outs),
         scratch_shapes=[pltpu.VMEM(s, F32) if isinstance(s, tuple) else s for s in scratch],
-        compiler_params=pltpu.CompilerParams(vmem_limit_bytes=32 * 1024 * 1024),
+        compiler_params=pltpu.CompilerParams(vmem_limit_bytes=vmem * 1024 * 1024),
         cost_estimate=pl.CostEstimate(flops=flops, bytes_accessed=0, transcendentals=0),
     )(*args)
 
@@ -455,10 +491,7 @@
     m, pack, flat = call(
         pack_kernel,
         [state.shape, (packed[0] + ROWS, LANES), flats],
-        state,
-        land_mask,
-        surface_height,
-        surface_damping,
+        *[pltpu.with_memory_space_constraint(x, pltpu.HBM) for x in (state, land_mask, surface_height, surface_damping)],
         specs=[HBM] * 4,
         scratch=[
             state.shape,
@@ -470,7 +503,7 @@
     )
     first = lax.ppermute(pack, axes, g_one)
     second = lax.ppermute(pack, axes, g_two)
-    message = (lay.rows, LANES)
+    message, rest = (lay.first, LANES), (lay.second, LANES)
     own, near, delta, one, two = call(
         edge_kernel,
         [(flats[0] + ROWS, LANES), (2 * lay.pad, LANES), packed, message, message],
@@ -482,22 +515,26 @@
     )
     one = lax.ppermute(one, axes, b_one)
     two = lax.ppermute(two, axes, b_two)
+    one_rest, two_rest = call(rest_kernel, [rest, rest], m, delta)
+    one_rest = lax.ppermute(one_rest, axes, b_one)
+    two_rest = lax.ppermute(two_rest, axes, b_two)
     basis, sent = call(
         moment_kernel,
-        [(ITERS * ROWS, LANES), (nb * ng, LANES)],
+        [(ITERS * ROWS, LANES), pltpu.VMEM((nb * ng, LANES), F32)],
         m,
         own,
         near,
         one,
         two,
         scratch=[(FLAT * 3 * ROWS, 2 * LANES)],
+        flops=FL_A,
     )
     got = lax.all_to_all(sent, axes, 0, 0, tiled=True)
-    (new_state,) = call(
-        step_kernel, [state.shape], m, pack, delta, one, two, land_mask, scratch=[(lay.tiles * EXT, LANES), packed],
-        flops=20_000_000,
-    )
-    (surface,) = call(solve_kernel, [one_tile], got, basis)
+    new_state, done = call(
+        step_kernel, [state.shape, one_tile], m, pack, delta, one_rest, two_rest, land_mask, scratch=[(lay.tiles * EXT, LANES), packed],
+        flops=FL_B,
+    )
+    (surface,) = call(solve_kernel, [one_tile], got, basis, done)
     return new_state.reshape(ocean_state.shape), surface
 
 

time: 34.4 us -> 28.2 us (0.82)
  local copies, waits for them, and re-layouts: 3.12 us -> 0.01 us
  waiting for transfers between devices: 10.7 us -> 7.7 us
    unnamed x10 -> x2, local copies, waits for them, and re-layouts: 3.12 us -> 0.01 us
    ppermute x1, waiting for transfers between devices: 3.6 us -> 0.64 us  [on_device(): two = lax.ppermute(two, axes, b_two)]
    all_to_all x1, starting transfers between devices: 6.84 us -> 4.97 us  [on_device(): got = lax.all_to_all(sent, axes, 0, 0, tiled=True)]
    ppermute x0 -> x2, starting transfers between devices: none -> 1.66 us  [the longest x1 1.59 us: on_device(): two_rest = lax.ppermute(two_rest, axes, b_two)]
    ppermute x1, starting transfers between devices: 3.21 us -> 2.09 us  [on_device(): two = lax.ppermute(two, axes, b_two)]
    ppermute x1, starting transfers between devices: 3.09 us -> 4.15 us  [on_device(): first = lax.ppermute(pack, axes, g_one)]
    ppermute x1, starting transfers between devices: 0.01 us -> 0.52 us  [on_device(): second = lax.ppermute(pack, axes, g_two)]
    pallas_call x5 -> x6, Pallas kernels: 6.38 us -> 6.11 us  [call(): pl.pallas_call(kernel, out_shape=[jax.ShapeDtypeStruct(s, F32) if isinsta...]
  transfers between devices with their start and end apart: 5 -> 7, of which waited for: 3 -> 3; matrix products, arithmetic and copies ran while one was open for 0% -> 0% of each run, Pallas kernels for 6% -> 12%
where the time goes in v3:
time: 28.2 us; the launch traced here: 28 us
  starting transfers between devices  13.5 us (48%)
  waiting for transfers between devices  7.7 us (27%)
  Pallas kernels  6.11 us (22%)
  between operations  0.71 us (3%)
    pallas_call x6, Pallas kernels, call(): pl.pallas_call(kernel, out_shape=[jax.ShapeDtypeStruct(s, F32) if isinsta...  6.11 us
    all_to_all x1, waiting for transfers between devices, on_device(): got = lax.all_to_all(sent, axes, 0, 0, tiled=True)  5.08 us
    all_to_all x1, starting transfers between devices, on_device(): got = lax.all_to_all(sent, axes, 0, 0, tiled=True)  4.97 us
    ppermute x1, starting transfers between devices, on_device(): first = lax.ppermute(pack, axes, g_one)  4.15 us
    ppermute x1, starting transfers between devices, on_device(): two = lax.ppermute(two, axes, b_two)  2.09 us
    ppermute x1, waiting for transfers between devices, on_device(): first = lax.ppermute(pack, axes, g_one)  1.98 us
    ppermute x1, starting transfers between devices, on_device(): two_rest = lax.ppermute(two_rest, axes, b_two)  1.59 us
    ppermute x1, waiting for transfers between devices, on_device(): two = lax.ppermute(two, axes, b_two)  0.64 us
  transfers between devices with their start and end apart: 7, of which 3 were waited for; matrix products, arithmetic and copies ran while one was open for 0% of the time, Pallas kernels for 12%

profile of v3, /device:TPU:0, one launch (start us, length us, event | category | flops | bytes accessed | tf_op | source)
XLA Modules:
  0.0 28.0 jit_solution(2276595931881517698)
XLA Ops:
  0.6 1.5 %shard_map.59 = (f32[1152,128]{1,0:T(8,128)S(1)}, f32[80,128]{1,0:T(8,128)S(1)}, f32[48,128]{1,0:T(8,128)S(1)}) custom-call(f32[1152,128]{1,0:T(8,128)} %bitcast.7, s32[8,128]{1,0:T(8,128)} %mask_ref.1, f32[8,128]{1,0:T(8,128)} %height_hbm.1, f32[8,128]{1,0:T(8,128)} %damp_hbm.1), custom_call_target="tpu_custom_call" | custom-call | tf_op jit(solution)/shard_map/pallas_call | solution.py:469
  2.1 0.5 %collective-permute-start.1 = (f32[80,128]{1,0:T(8,128)S(1)}, f32[80,128]{1,0:T(8,128)S(1)}, u32[]{:S(2)}, u32[]{:S(2)}) collective-permute-start(f32[80,128]{1,0:T(8,128)S(1)} %get-tuple-element.17.pack_ref), channel_id=1, source_target_pairs={{0,4},{1,2},{2,1},{3,7},{4,0},{5,6},{6,5},{7,3},{8,12},{9,10},{10,... | collective-permute-start | bytes 122888 | tf_op jit(solution)/shard_map/ppermute | solution.py:505
  2.7 4.1 %collective-permute-start = (f32[80,128]{1,0:T(8,128)S(1)}, f32[80,128]{1,0:T(8,128)S(1)}, u32[]{:S(2)}, u32[]{:S(2)}) collective-permute-start(f32[80,128]{1,0:T(8,128)S(1)} %get-tuple-element.17.pack_ref), channel_id=1, source_target_pairs={{0,1},{1,0},{2,3},{3,2},{4,5},{5,4},{6,7},{7,6},{8,9},{9,8},{10,11... | collective-permute-start | bytes 122888 | tf_op jit(solution)/shard_map/ppermute | solution.py:504
  6.8 0.0 collective-permute-done.1.second_ref
  6.8 2.0 %collective-permute-done.first_ref = f32[80,128]{1,0:T(8,128)S(1)} collective-permute-done((f32[80,128]{1,0:T(8,128)S(1)}, f32[80,128]{1,0:T(8,128)S(1)}, u32[]{:S(2)}, u32[]{:S(2)}) %collective-permute-start) | collective-permute-done | bytes 40992 | tf_op jit(solution)/shard_map/ppermute | solution.py:504
  8.8 0.4 %shard_map.60 = (f32[56,128]{1,0:T(8,128)S(1)}, f32[32,128]{1,0:T(8,128)S(1)}, f32[72,128]{1,0:T(8,128)S(1)}, f32[152,128]{1,0:T(8,128)S(1)}, f32[152,128]{1,0:T(8,128)S(1)}) custom-call(f32[1152,128]{1,0:T(8,128)S(1)} %get-tuple-element.16.m_ref, f32[80,128]{1,0:T(8,128)S(1)} %get-tuple-element.17.pack_ref, f32[48,128]{1,0:T(8,128)S(1)} %get-tuple-element.18.flat_ref, ...), custom_call_target="tpu_custom_call" | custom-call | tf_op jit(solution)/shard_map/pallas_call | solution.py:469
  9.2 0.1 collective-permute-start.4
  9.3 2.1 %collective-permute-start.5 = (f32[152,128]{1,0:T(8,128)S(1)}, f32[152,128]{1,0:T(8,128)S(1)}, u32[]{:S(2)}, u32[]{:S(2)}) collective-permute-start(f32[152,128]{1,0:T(8,128)S(1)} %get-tuple-element.26), channel_id=1, source_target_pairs={{0,1},{1,0},{2,3},{3,2},{4,8},{5,9},{6,10},{7,11},{8,4},{9,5},{10,... | collective-permute-start | bytes 233480 | tf_op jit(solution)/shard_map/ppermute | solution.py:517
  11.4 0.1 shard_map.61
  11.5 0.1 collective-permute-start.2
  11.5 1.6 %collective-permute-start.3 = (f32[304,128]{1,0:T(8,128)S(1)}, f32[304,128]{1,0:T(8,128)S(1)}, u32[]{:S(2)}, u32[]{:S(2)}) collective-permute-start(f32[304,128]{1,0:T(8,128)S(1)} %get-tuple-element.21), channel_id=1, source_target_pairs={{0,1},{1,0},{2,3},{3,2},{4,8},{5,9},{6,10},{7,11},{8,4},{9,5},{10,... | collective-permute-start | bytes 466952 | tf_op jit(solution)/shard_map/ppermute | solution.py:520
  13.1 0.0 collective-permute-done.4.one_ref
  13.1 0.6 %collective-permute-done.5.two_ref = f32[152,128]{1,0:T(8,128)S(1)} collective-permute-done((f32[152,128]{1,0:T(8,128)S(1)}, f32[152,128]{1,0:T(8,128)S(1)}, u32[]{:S(2)}, u32[]{:S(2)}) %collective-permute-start.5) | collective-permute-done | bytes 77856 | tf_op jit(solution)/shard_map/ppermute | solution.py:517
  13.8 1.3 %shard_map.63 = (f32[24,128]{1,0:T(8,128)S(1)}, f32[32,128]{1,0:T(8,128)}) custom-call(f32[1152,128]{1,0:T(8,128)S(1)} %get-tuple-element.16.m_ref, f32[56,128]{1,0:T(8,128)S(1)} %get-tuple-element.23.own_ref, f32[32,128]{1,0:T(8,128)S(1)} %get-tuple-element.24.near_ref, f32[152,128]{1,0:T(8,128)S(1)} %collective-permute-done.4.one_ref, ...), custom_call_target="tpu_custom_call" | custom-call | flops 1000000000 | tf_op jit(solution)/shard_map/pallas_call | solution.py:469
  15.1 0.0 copy-start
  15.1 5.0 %all-to-all-start = ((f32[32,1,128]{2,1,0:T(1,128)}), f32[32,1,128]{2,1,0:T(1,128)S(1)}, u32[]{:S(2)}, u32[]{:S(2)}) async-start(f32[32,1,128]{2,1,0:T(1,128)} %bitcast.3), calls=%async_computation | async-start | bytes 32768 | tf_op jit(solution)/shard_map/all_to_all | solution.py:532
  20.1 0.0 collective-permute-done.2.one_ref
  20.1 0.0 collective-permute-done.3.two_ref
  20.1 0.0 copy-done
  20.1 2.1 %shard_map.62 = (f32[1152,128]{1,0:T(8,128)}, f32[8,128]{1,0:T(8,128)S(1)}) custom-call(f32[1152,128]{1,0:T(8,128)S(1)} %get-tuple-element.16.m_ref, f32[80,128]{1,0:T(8,128)S(1)} %get-tuple-element.17.pack_ref, f32[72,128]{1,0:T(8,128)S(1)} %get-tuple-element.19.delta_ref, f32[304,128]{1,0:T(8,128)S(1)} %collective-permute-done.2.one_ref, ...), custom_call_target="tpu_custom_call" | custom-call | flops 1000000000 | tf_op jit(solution)/shard_map/pallas_call | solution.py:469
  22.1 5.1 %all-to-all-done = f32[32,1,128]{2,1,0:T(1,128)S(1)} async-done(((f32[32,1,128]{2,1,0:T(1,128)}), f32[32,1,128]{2,1,0:T(1,128)S(1)}, u32[]{:S(2)}, u32[]{:S(2)}) %all-to-all-start) | async-done | bytes 16416 | tf_op jit(solution)/shard_map/all_to_all | solution.py:532
  27.2 0.7 %shard_map.64 = f32[8,128]{1,0:T(8,128)} custom-call(f32[32,128]{1,0:T(8,128)S(1)} %bitcast.6, f32[24,128]{1,0:T(8,128)S(1)} %get-tuple-element.28.basis_ref, f32[8,128]{1,0:T(8,128)S(1)} %get-tuple-element.29.done_ref), custom_call_target="tpu_custom_call" | custom-call | tf_op jit(solution)/shard_map/pallas_call | solution.py:469
Async XLA Ops:
  2.1 4.7 %collective-permute-start.1 = (f32[80,128]{1,0:T(8,128)S(1)}, f32[80,128]{1,0:T(8,128)S(1)}, u32[]{:S(2)}, u32[]{:S(2)}) collective-permute-start(f32[80,128]{1,0:T(8,128)S(1)} %get-tuple-element.17.pack_ref), channel_id=1, source_target_pairs={{0,4},{1,2},{2,1},{3,7},{4,0},{5,6},{6,5},{7,3},{8,12},{9,10},{10,... | collective-permute-start | bytes 122888 | tf_op jit(solution)/shard_map/ppermute | solution.py:505
  2.7 6.1 %collective-permute-start = (f32[80,128]{1,0:T(8,128)S(1)}, f32[80,128]{1,0:T(8,128)S(1)}, u32[]{:S(2)}, u32[]{:S(2)}) collective-permute-start(f32[80,128]{1,0:T(8,128)S(1)} %get-tuple-element.17.pack_ref), channel_id=1, source_target_pairs={{0,1},{1,0},{2,3},{3,2},{4,5},{5,4},{6,7},{7,6},{8,9},{9,8},{10,11... | collective-permute-start | bytes 122888 | tf_op jit(solution)/shard_map/ppermute | solution.py:504
  9.2 3.9 %collective-permute-start.4 = (f32[152,128]{1,0:T(8,128)S(1)}, f32[152,128]{1,0:T(8,128)S(1)}, u32[]{:S(2)}, u32[]{:S(2)}) collective-permute-start(f32[152,128]{1,0:T(8,128)S(1)} %get-tuple-element.25), channel_id=1, source_target_pairs={{0,4},{1,5},{2,6},{3,7},{4,0},{5,1},{6,2},{7,3},{8,12},{9,13},{10,... | collective-permute-start | bytes 233480 | tf_op jit(solution)/shard_map/ppermute | solution.py:516
  9.3 4.5 %collective-permute-start.5 = (f32[152,128]{1,0:T(8,128)S(1)}, f32[152,128]{1,0:T(8,128)S(1)}, u32[]{:S(2)}, u32[]{:S(2)}) collective-permute-start(f32[152,128]{1,0:T(8,128)S(1)} %get-tuple-element.26), channel_id=1, source_target_pairs={{0,1},{1,0},{2,3},{3,2},{4,8},{5,9},{6,10},{7,11},{8,4},{9,5},{10,... | collective-permute-start | bytes 233480 | tf_op jit(solution)/shard_map/ppermute | solution.py:517
  11.5 8.6 %collective-permute-start.2 = (f32[304,128]{1,0:T(8,128)S(1)}, f32[304,128]{1,0:T(8,128)S(1)}, u32[]{:S(2)}, u32[]{:S(2)}) collective-permute-start(f32[304,128]{1,0:T(8,128)S(1)} %get-tuple-element.20), channel_id=1, source_target_pairs={{0,4},{1,5},{2,6},{3,7},{4,0},{5,1},{6,2},{7,3},{8,12},{9,13},{10,... | collective-permute-start | bytes 466952 | tf_op jit(solution)/shard_map/ppermute | solution.py:519
  11.5 8.5 %collective-permute-start.3 = (f32[304,128]{1,0:T(8,128)S(1)}, f32[304,128]{1,0:T(8,128)S(1)}, u32[]{:S(2)}, u32[]{:S(2)}) collective-permute-start(f32[304,128]{1,0:T(8,128)S(1)} %get-tuple-element.21), channel_id=1, source_target_pairs={{0,1},{1,0},{2,3},{3,2},{4,8},{5,9},{6,10},{7,11},{8,4},{9,5},{10,... | collective-permute-start | bytes 466952 | tf_op jit(solution)/shard_map/ppermute | solution.py:520
  15.1 5.0 %copy-start = (s32[8,128]{1,0:T(8,128)S(1)}, s32[8,128]{1,0:T(8,128)}, u32[]{:S(2)}) copy-start(s32[8,128]{1,0:T(8,128)} %mask_ref.1) | copy-start | bytes 12292
  15.1 12.1 %all-to-all-start = ((f32[32,1,128]{2,1,0:T(1,128)}), f32[32,1,128]{2,1,0:T(1,128)S(1)}, u32[]{:S(2)}, u32[]{:S(2)}) async-start(f32[32,1,128]{2,1,0:T(1,128)} %bitcast.3), calls=%async_computation | async-start | bytes 32768 | tf_op jit(solution)/shard_map/all_to_all | solution.py:532

commit v4 on v3

--- a/solution.py
+++ b/solution.py
@@ -1,3 +1,5 @@
+import functools
+
 import jax
 import jax.numpy as jnp
 from jax import lax
@@ -21,8 +23,7 @@
 EXT = 12
 FLAT = 6
 STRIP = 16
-FL_A = 10**9
-FL_B = 10**9
+LONG = 10**9
 SHIFT = 4.5
 F32 = jnp.float32
 VMEM = pl.BlockSpec(memory_space=pltpu.VMEM)
@@ -68,23 +69,11 @@
         self.eights = tiles // ROWS
         self.pad = -(-self.packs // ROWS) * ROWS
         self.flow = -(-self.levels // ROWS) * ROWS
-        self.edge = 2 * self.flow
-        self.flat = self.edge + self.pad
+        self.edge = 0
+        self.delta = self.pad
+        self.flat = 2 * self.pad
         self.strip = self.flat + FLAT * ROWS
-        self.first = self.strip + ROWS
-        self.delta = 2 * tiles
-        self.second = self.delta + self.pad
-
-    def level_rows(self, m_ref, comp, row):
-        step = COMPS * ROWS
-        parts = []
-        for start in range(0, self.levels, ROWS):
-            count = min(ROWS, self.levels - start)
-            x = m_ref[pl.ds(start * step + comp * ROWS + row, count, stride=step), :]
-            if count < ROWS:
-                x = jnp.concatenate([x, jnp.zeros((ROWS - count, LANES), F32)], axis=0)
-            parts.append(x)
-        return parts
+        self.message = self.strip + ROWS
 
 
 class Place:
@@ -226,36 +215,68 @@
 
     def fill(low_ref, high_ref):
         for ref, row, rows in ((low_ref, 0, slice(0, lay.pad)), (high_ref, ROWS - 1, slice(lay.pad, 2 * lay.pad))):
-            for c in (2, 3):
-                for n, x in enumerate(lay.level_rows(m_ref, c, row)):
-                    ref[pl.ds((c - 2) * lay.flow + n * ROWS, ROWS), :] = x
             ref[pl.ds(lay.edge, lay.pad), :] = near_ref[rows, :]
-            ref[pl.ds(lay.flat, (FLAT + 1) * ROWS), :] = own_ref[...]
-
-    pl.when(at.b_even)(lambda: fill(two_ref, one_ref))
-    pl.when(jnp.logical_not(at.b_even))(lambda: fill(one_ref, two_ref))
-
-
-def rest_kernel(m_ref, delta_ref, one_ref, two_ref):
-    lay = Layout(m_ref.shape[0] // ROWS)
-    at = Place()
-
-    def fill(low_ref, high_ref):
-        for ref, row in ((low_ref, 0), (high_ref, ROWS - 1)):
-            for r in range(2):
-                for s in range(lay.eights):
-                    start = ROWS * ROWS * s + (row - 1 if row else 0) + r
-                    ref[tile(r * lay.eights + s), :] = m_ref[pl.ds(start, ROWS, stride=ROWS), :]
             ref[pl.ds(lay.delta, lay.pad), :] = jnp.zeros((lay.pad, LANES), F32)
             for p in range(lay.packs):
                 ref[pl.ds(lay.delta + p, 1), :] = delta_ref[pl.ds(ROWS * p + row, 1), :]
+            ref[pl.ds(lay.flat, (FLAT + 1) * ROWS), :] = own_ref[...]
 
     pl.when(at.b_even)(lambda: fill(two_ref, one_ref))
     pl.when(jnp.logical_not(at.b_even))(lambda: fill(one_ref, two_ref))
 
 
-def moment_kernel(m_ref, own_ref, near_ref, one_ref, two_ref, basis_ref, send_ref, wide_ref):
+def rows_kernel(m_ref, one_ref, two_ref):
     lay = Layout(m_ref.shape[0] // ROWS)
+
+    def fill(low_ref, high_ref):
+        for ref, row in ((low_ref, 0), (high_ref, ROWS - 2)):
+            for r in range(2):
+                for s in range(lay.eights):
+                    at = pl.ds(ROWS * ROWS * s + row + r, ROWS, stride=ROWS)
+                    ref[tile(r * lay.eights + s), :] = m_ref[at, :]
+
+    even = Place().b_even
+    pl.when(even)(lambda: fill(two_ref, one_ref))
+    pl.when(jnp.logical_not(even))(lambda: fill(one_ref, two_ref))
+
+
+def cross_kernel(m_ref, one_ref, two_ref, cross_ref):
+    lay = Layout(m_ref.shape[0] // ROWS)
+    at = Place()
+    row = iota(0)
+
+    def level_rows(ref, comp, first, count_rows):
+        parts = []
+        for start in range(0, lay.levels, ROWS):
+            count = min(ROWS, lay.levels - start)
+            x = ref[pl.ds((start * COMPS + comp) * count_rows + first, count, stride=COMPS * count_rows), :]
+            if count < ROWS:
+                x = jnp.concatenate([x, jnp.zeros((ROWS - count, LANES), F32)], axis=0)
+            parts.append(x)
+        return parts
+
+    def beyond(first):
+        return [[level_rows(ref, c, first, 1) for c in (2, 3)] for ref in (one_ref, two_ref)]
+
+    one, two = beyond(lay.tiles)
+    above = [[at.from_up(x, y) for x, y in zip(one[c], two[c])] for c in range(2)]
+    one, two = beyond(0)
+    below = [[at.from_down(x, y) for x, y in zip(one[c], two[c])] for c in range(2)]
+    top, bottom = [[level_rows(m_ref, c, r, ROWS) for c in (2, 3)] for r in (0, ROWS - 1)]
+
+    def total(flow, carried):
+        return 0.5 * jnp.sum(sum(x * y for x, y in zip(flow, carried)), axis=0, keepdims=True)
+
+    out = jnp.zeros((ROWS, LANES), F32)
+    for f in range(2):
+        sums = (total(above[0], top[f]), -total(top[0], above[f]), total(bottom[0], below[f]), -total(below[0], bottom[f]))
+        for k in range(4):
+            out = jnp.where(row == 4 * f + k, sums[k], out)
+    cross_ref[...] = out
+
+
+def moment_kernel(own_ref, near_ref, cross_ref, one_ref, two_ref, basis_ref, send_ref, wide_ref, *, levels):
+    lay = Layout(levels * COMPS)
     at = Place()
     row, lane = iota(0), iota(1)
     outside = (lane < STRIP // 2) | (lane >= LANES - STRIP // 2)
@@ -275,18 +296,6 @@
             side = roll(strips[k], -(STRIP * f + STRIP // 2), 1)
             wide_ref[to, LANES : 2 * LANES] = jnp.where(outside, side, 0.0)
 
-    own_rows = [[lay.level_rows(m_ref, c, r) for c in (2, 3)] for r in (0, ROWS - 1)]
-    cross = []
-    for f in range(2):
-        total = [jnp.zeros((ROWS, LANES), F32) for _ in range(4)]
-        for n in range(lay.flow // ROWS):
-            flow = neighbours(tile(n))
-            carried = neighbours(pl.ds(f * lay.flow + n * ROWS, ROWS))
-            total[0] = total[0] + flow[0] * own_rows[0][f][n]
-            total[1] = total[1] - own_rows[0][0][n] * carried[0]
-            total[2] = total[2] + own_rows[1][0][n] * carried[1]
-            total[3] = total[3] - flow[1] * own_rows[1][f][n]
-        cross.append([0.5 * jnp.sum(x, axis=0, keepdims=True) for x in total])
     above, below = neighbours(pl.ds(lay.edge, lay.pad))
     top, bottom = near_ref[0 : lay.pad, :], near_ref[lay.pad :, :]
 
@@ -303,7 +312,7 @@
     for f in (2, 3):
         for k, at_row in enumerate((ROWS - 1, ROWS, 2 * ROWS - 1, 2 * ROWS)):
             to = pl.ds(f * rows + at_row, 1)
-            wide_ref[to, 0:LANES] = wide_ref[to, 0:LANES] + cross[f - 2][k]
+            wide_ref[to, 0:LANES] = wide_ref[to, 0:LANES] + cross_ref[4 * (f - 2) + k : 4 * (f - 2) + k + 1, :]
             side = roll(corners[k], -(SLOT * f + SLOT // 2), 1)
             wide_ref[to, LANES : 2 * LANES] = wide_ref[to, LANES : 2 * LANES] + jnp.where(border, side, 0.0)
 
@@ -392,7 +401,9 @@
     out_ref[...] = out
 
 
-def step_kernel(m_ref, pack_ref, delta_ref, one_ref, two_ref, mask_ref, new_ref, done_ref, ext_ref, corr_ref):
+def step_kernel(
+    m_ref, pack_ref, delta_ref, rows_one_ref, rows_two_ref, one_ref, two_ref, mask_ref, new_ref, done_ref, ext_ref, corr_ref
+):
     lay = Layout(m_ref.shape[0] // ROWS)
     at = Place()
     row, lane = iota(0), iota(1)
@@ -400,7 +411,7 @@
         ext_ref[pl.ds(EXT * t + 2, ROWS), :] = m_ref[tile(t), :]
     for r in range(2):
         for s in range(lay.eights):
-            one, two = one_ref[tile(r * lay.eights + s), :], two_ref[tile(r * lay.eights + s), :]
+            one, two = rows_one_ref[tile(r * lay.eights + s), :], rows_two_ref[tile(r * lay.eights + s), :]
             ext_ref[pl.ds(EXT * ROWS * s + r, ROWS, stride=EXT), :] = at.from_up(one, two)
             ext_ref[pl.ds(EXT * ROWS * s + ROWS + 2 + r, ROWS, stride=EXT), :] = at.from_down(one, two)
 
@@ -503,7 +514,10 @@
     )
     first = lax.ppermute(pack, axes, g_one)
     second = lax.ppermute(pack, axes, g_two)
-    message, rest = (lay.first, LANES), (lay.second, LANES)
+    rows_one, rows_two = call(rows_kernel, [(2 * lay.tiles, LANES)] * 2, m)
+    rows_one = lax.ppermute(rows_one, axes, b_one)
+    rows_two = lax.ppermute(rows_two, axes, b_two)
+    message = (lay.message, LANES)
     own, near, delta, one, two = call(
         edge_kernel,
         [(flats[0] + ROWS, LANES), (2 * lay.pad, LANES), packed, message, message],
@@ -512,27 +526,36 @@
         flat,
         first,
         second,
+        flops=LONG,
     )
     one = lax.ppermute(one, axes, b_one)
     two = lax.ppermute(two, axes, b_two)
-    one_rest, two_rest = call(rest_kernel, [rest, rest], m, delta)
-    one_rest = lax.ppermute(one_rest, axes, b_one)
-    two_rest = lax.ppermute(two_rest, axes, b_two)
+    (cross,) = call(cross_kernel, [one_tile], m, rows_one, rows_two)
     basis, sent = call(
-        moment_kernel,
-        [(ITERS * ROWS, LANES), pltpu.VMEM((nb * ng, LANES), F32)],
-        m,
+        functools.partial(moment_kernel, levels=lay.levels),
+        [(ITERS * ROWS, LANES), (nb * ng, LANES)],
         own,
         near,
+        cross,
         one,
         two,
         scratch=[(FLAT * 3 * ROWS, 2 * LANES)],
-        flops=FL_A,
+        flops=LONG,
     )
     got = lax.all_to_all(sent, axes, 0, 0, tiled=True)
     new_state, done = call(
-        step_kernel, [state.shape, one_tile], m, pack, delta, one_rest, two_rest, land_mask, scratch=[(lay.tiles * EXT, LANES), packed],
-        flops=FL_B,
+        step_kernel,
+        [state.shape, one_tile],
+        m,
+        pack,
+        delta,
+        rows_one,
+        rows_two,
+        one,
+        two,
+        land_mask,
+        scratch=[(lay.tiles * EXT, LANES), packed],
+        flops=LONG,
     )
     (surface,) = call(solve_kernel, [one_tile], got, basis, done)
     return new_state.reshape(ocean_state.shape), surface

time: 28.2 us -> 27.6 us (0.979)
  waiting for transfers between devices: 7.7 us -> 7.32 us
  starting transfers between devices: 13.5 us -> 13.2 us
    ppermute x1, waiting for transfers between devices: 1.98 us -> 0.01 us  [on_device(): first = lax.ppermute(pack, axes, g_one)]
    ppermute x2, starting transfers between devices: 1.66 us -> 3.29 us  [the longest x1 2.73 us: on_device(): rows_two = lax.ppermute(rows_two, axes, b_two)]
    ppermute x1, starting transfers between devices: 4.15 us -> 3.09 us  [on_device(): first = lax.ppermute(pack, axes, g_one)]
    ppermute x2, waiting for transfers between devices: 0.01 us -> 0.86 us  [the longest x1 0.86 us: on_device(): rows_two = lax.ppermute(rows_two, axes, b_two)]
    ppermute x1, waiting for transfers between devices: 0.64 us -> 1.34 us  [on_device(): two = lax.ppermute(two, axes, b_two)]
    ppermute x1, starting transfers between devices: 0.52 us -> 0.01 us  [on_device(): second = lax.ppermute(pack, axes, g_two)]
    pallas_call x6 -> x7, Pallas kernels: 6.11 us -> 6.13 us  [call(): pl.pallas_call(kernel, out_shape=[jax.ShapeDtypeStruct(s, F32) if isinsta...]
  transfers between devices with their start and end apart: 7 -> 7, of which waited for: 3 -> 3; matrix products, arithmetic and copies ran while one was open for 0% -> 0% of each run, Pallas kernels for 12% -> 9%
where the time goes in v4:
time: 27.6 us; the launch traced here: 27.4 us
  starting transfers between devices  13.2 us (48%)
  waiting for transfers between devices  7.32 us (27%)
  Pallas kernels  6.13 us (22%)
  between operations  0.69 us (2%)
    pallas_call x7, Pallas kernels, call(): pl.pallas_call(kernel, out_shape=[jax.ShapeDtypeStruct(s, F32) if isinsta...  6.13 us
    all_to_all x1, waiting for transfers between devices, on_device(): got = lax.all_to_all(sent, axes, 0, 0, tiled=True)  5.12 us
    all_to_all x1, starting transfers between devices, on_device(): got = lax.all_to_all(sent, axes, 0, 0, tiled=True)  5.01 us
    ppermute x1, starting transfers between devices, on_device(): first = lax.ppermute(pack, axes, g_one)  3.09 us
    ppermute x1, starting transfers between devices, on_device(): rows_two = lax.ppermute(rows_two, axes, b_two)  2.73 us
    ppermute x1, starting transfers between devices, on_device(): two = lax.ppermute(two, axes, b_two)  1.83 us
    ppermute x1, waiting for transfers between devices, on_device(): two = lax.ppermute(two, axes, b_two)  1.34 us
    ppermute x1, waiting for transfers between devices, on_device(): rows_two = lax.ppermute(rows_two, axes, b_two)  0.86 us
  transfers between devices with their start and end apart: 7, of which 3 were waited for; matrix products, arithmetic and copies ran while one was open for 0% of the time, Pallas kernels for 9%

profile of v4, /device:TPU:0, one launch (start us, length us, event | category | flops | bytes accessed | tf_op | source)
XLA Modules:
  0.0 27.4 jit_solution(1246481560670952365)
XLA Ops:
  0.6 1.5 %shard_map.59 = (f32[1152,128]{1,0:T(8,128)S(1)}, f32[80,128]{1,0:T(8,128)S(1)}, f32[48,128]{1,0:T(8,128)S(1)}) custom-call(f32[1152,128]{1,0:T(8,128)} %bitcast.7, s32[8,128]{1,0:T(8,128)} %mask_ref.1, f32[8,128]{1,0:T(8,128)} %height_hbm.1, f32[8,128]{1,0:T(8,128)} %damp_hbm.1), custom_call_target="tpu_custom_call" | custom-call | tf_op jit(solution)/shard_map/pallas_call | solution.py:480
  2.1 3.1 %collective-permute-start = (f32[80,128]{1,0:T(8,128)S(1)}, f32[80,128]{1,0:T(8,128)S(1)}, u32[]{:S(2)}, u32[]{:S(2)}) collective-permute-start(f32[80,128]{1,0:T(8,128)S(1)} %get-tuple-element.17.pack_ref), channel_id=1, source_target_pairs={{0,1},{1,0},{2,3},{3,2},{4,5},{5,4},{6,7},{7,6},{8,9},{9,8},{10,11... | collective-permute-start | bytes 122888 | tf_op jit(solution)/shard_map/ppermute | solution.py:515
  5.2 0.0 collective-permute-start.1
  5.2 0.1 shard_map.61
  5.3 0.6 %collective-permute-start.2 = (f32[288,128]{1,0:T(8,128)S(1)}, f32[288,128]{1,0:T(8,128)S(1)}, u32[]{:S(2)}, u32[]{:S(2)}) collective-permute-start(f32[288,128]{1,0:T(8,128)S(1)} %get-tuple-element.20), channel_id=1, source_target_pairs={{0,4},{1,5},{2,6},{3,7},{4,0},{5,1},{6,2},{7,3},{8,12},{9,13},{10,... | collective-permute-start | bytes 442376 | tf_op jit(solution)/shard_map/ppermute | solution.py:518
  5.9 2.7 %collective-permute-start.3 = (f32[288,128]{1,0:T(8,128)S(1)}, f32[288,128]{1,0:T(8,128)S(1)}, u32[]{:S(2)}, u32[]{:S(2)}) collective-permute-start(f32[288,128]{1,0:T(8,128)S(1)} %get-tuple-element.21), channel_id=1, source_target_pairs={{0,1},{1,0},{2,3},{3,2},{4,8},{5,9},{6,10},{7,11},{8,4},{9,5},{10,... | collective-permute-start | bytes 442376 | tf_op jit(solution)/shard_map/ppermute | solution.py:519
  8.6 0.0 collective-permute-done.first_ref
  8.6 0.0 collective-permute-done.1.second_ref
  8.6 0.4 %shard_map.60 = (f32[56,128]{1,0:T(8,128)S(1)}, f32[32,128]{1,0:T(8,128)S(1)}, f32[72,128]{1,0:T(8,128)S(1)}, f32[88,128]{1,0:T(8,128)S(1)}, f32[88,128]{1,0:T(8,128)S(1)}) custom-call(f32[1152,128]{1,0:T(8,128)S(1)} %get-tuple-element.16.m_ref, f32[80,128]{1,0:T(8,128)S(1)} %get-tuple-element.17.pack_ref, f32[48,128]{1,0:T(8,128)S(1)} %get-tuple-element.18.flat_ref, ...), custom_call_target="tpu_custom_call" | custom-call | flops 1000000000 | tf_op jit(solution)/shard_map/pallas_call | solution.py:480
  9.0 0.0 collective-permute-start.4
  9.0 1.8 %collective-permute-start.5 = (f32[88,128]{1,0:T(8,128)S(1)}, f32[88,128]{1,0:T(8,128)S(1)}, u32[]{:S(2)}, u32[]{:S(2)}) collective-permute-start(f32[88,128]{1,0:T(8,128)S(1)} %get-tuple-element.23), channel_id=1, source_target_pairs={{0,1},{1,0},{2,3},{3,2},{4,8},{5,9},{6,10},{7,11},{8,4},{9,5},{10,... | collective-permute-start | bytes 135176 | tf_op jit(solution)/shard_map/ppermute | solution.py:532
  10.9 0.0 collective-permute-done.2.rows_one_ref.one_ref
  10.9 0.9 %collective-permute-done.3.rows_two_ref.two_ref = f32[288,128]{1,0:T(8,128)S(1)} collective-permute-done((f32[288,128]{1,0:T(8,128)S(1)}, f32[288,128]{1,0:T(8,128)S(1)}, u32[]{:S(2)}, u32[]{:S(2)}) %collective-permute-start.3) | collective-permute-done | bytes 147488 | tf_op jit(solution)/shard_map/ppermute | solution.py:519
  11.7 0.1 shard_map.63.cross_ref
  11.8 0.0 collective-permute-done.4.one_ref
  11.8 1.3 %collective-permute-done.5.two_ref = f32[88,128]{1,0:T(8,128)S(1)} collective-permute-done((f32[88,128]{1,0:T(8,128)S(1)}, f32[88,128]{1,0:T(8,128)S(1)}, u32[]{:S(2)}, u32[]{:S(2)}) %collective-permute-start.5) | collective-permute-done | bytes 45088 | tf_op jit(solution)/shard_map/ppermute | solution.py:532
  13.1 1.3 %shard_map.64 = (f32[24,128]{1,0:T(8,128)S(1)}, f32[32,128]{1,0:T(8,128)}) custom-call(f32[56,128]{1,0:T(8,128)S(1)} %get-tuple-element.25.own_ref, f32[32,128]{1,0:T(8,128)S(1)} %get-tuple-element.26.near_ref, f32[8,128]{1,0:T(8,128)S(1)} %shard_map.63.cross_ref, f32[88,128]{1,0:T(8,128)S(1)} %collective-permute-done.4.one_ref, ...), custom_call_target="tpu_custom_call" | custom-call | flops 1000000000 | tf_op jit(solution)/shard_map/pallas_call | solution.py:480
  14.5 0.0 copy-start
  14.5 5.0 %all-to-all-start = ((f32[32,1,128]{2,1,0:T(1,128)}), f32[32,1,128]{2,1,0:T(1,128)S(1)}, u32[]{:S(2)}, u32[]{:S(2)}) async-start(f32[32,1,128]{2,1,0:T(1,128)} %bitcast.3), calls=%async_computation | async-start | bytes 32768 | tf_op jit(solution)/shard_map/all_to_all | solution.py:545
  19.5 0.0 copy-done
  19.5 2.0 %shard_map.62 = (f32[1152,128]{1,0:T(8,128)}, f32[8,128]{1,0:T(8,128)S(1)}) custom-call(f32[1152,128]{1,0:T(8,128)S(1)} %get-tuple-element.16.m_ref, f32[80,128]{1,0:T(8,128)S(1)} %get-tuple-element.17.pack_ref, f32[72,128]{1,0:T(8,128)S(1)} %get-tuple-element.19.delta_ref, f32[288,128]{1,0:T(8,128)S(1)} %collective-permute-done.2.rows_one_ref.one_ref, ...), custom_call_target="tpu_custom_call" | custom-call | flops 1000000000 | tf_op jit(solution)/shard_map/pallas_call | solution.py:480
  21.5 5.1 %all-to-all-done = f32[32,1,128]{2,1,0:T(1,128)S(1)} async-done(((f32[32,1,128]{2,1,0:T(1,128)}), f32[32,1,128]{2,1,0:T(1,128)S(1)}, u32[]{:S(2)}, u32[]{:S(2)}) %all-to-all-start) | async-done | bytes 16416 | tf_op jit(solution)/shard_map/all_to_all | solution.py:545
  26.6 0.7 %shard_map.65 = f32[8,128]{1,0:T(8,128)} custom-call(f32[32,128]{1,0:T(8,128)S(1)} %bitcast.6, f32[24,128]{1,0:T(8,128)S(1)} %get-tuple-element.28.basis_ref, f32[8,128]{1,0:T(8,128)S(1)} %get-tuple-element.29.done_ref), custom_call_target="tpu_custom_call" | custom-call | tf_op jit(solution)/shard_map/pallas_call | solution.py:480
Async XLA Ops:
  2.1 6.5 %collective-permute-start = (f32[80,128]{1,0:T(8,128)S(1)}, f32[80,128]{1,0:T(8,128)S(1)}, u32[]{:S(2)}, u32[]{:S(2)}) collective-permute-start(f32[80,128]{1,0:T(8,128)S(1)} %get-tuple-element.17.pack_ref), channel_id=1, source_target_pairs={{0,1},{1,0},{2,3},{3,2},{4,5},{5,4},{6,7},{7,6},{8,9},{9,8},{10,11... | collective-permute-start | bytes 122888 | tf_op jit(solution)/shard_map/ppermute | solution.py:515
  5.2 3.4 %collective-permute-start.1 = (f32[80,128]{1,0:T(8,128)S(1)}, f32[80,128]{1,0:T(8,128)S(1)}, u32[]{:S(2)}, u32[]{:S(2)}) collective-permute-start(f32[80,128]{1,0:T(8,128)S(1)} %get-tuple-element.17.pack_ref), channel_id=1, source_target_pairs={{0,4},{1,2},{2,1},{3,7},{4,0},{5,6},{6,5},{7,3},{8,12},{9,10},{10,... | collective-permute-start | bytes 122888 | tf_op jit(solution)/shard_map/ppermute | solution.py:516
  5.3 5.6 %collective-permute-start.2 = (f32[288,128]{1,0:T(8,128)S(1)}, f32[288,128]{1,0:T(8,128)S(1)}, u32[]{:S(2)}, u32[]{:S(2)}) collective-permute-start(f32[288,128]{1,0:T(8,128)S(1)} %get-tuple-element.20), channel_id=1, source_target_pairs={{0,4},{1,5},{2,6},{3,7},{4,0},{5,1},{6,2},{7,3},{8,12},{9,13},{10,... | collective-permute-start | bytes 442376 | tf_op jit(solution)/shard_map/ppermute | solution.py:518
  5.9 5.8 %collective-permute-start.3 = (f32[288,128]{1,0:T(8,128)S(1)}, f32[288,128]{1,0:T(8,128)S(1)}, u32[]{:S(2)}, u32[]{:S(2)}) collective-permute-start(f32[288,128]{1,0:T(8,128)S(1)} %get-tuple-element.21), channel_id=1, source_target_pairs={{0,1},{1,0},{2,3},{3,2},{4,8},{5,9},{6,10},{7,11},{8,4},{9,5},{10,... | collective-permute-start | bytes 442376 | tf_op jit(solution)/shard_map/ppermute | solution.py:519
  9.0 2.8 %collective-permute-start.4 = (f32[88,128]{1,0:T(8,128)S(1)}, f32[88,128]{1,0:T(8,128)S(1)}, u32[]{:S(2)}, u32[]{:S(2)}) collective-permute-start(f32[88,128]{1,0:T(8,128)S(1)} %get-tuple-element.22), channel_id=1, source_target_pairs={{0,4},{1,5},{2,6},{3,7},{4,0},{5,1},{6,2},{7,3},{8,12},{9,13},{10,... | collective-permute-start | bytes 135176 | tf_op jit(solution)/shard_map/ppermute | solution.py:531
  9.0 4.1 %collective-permute-start.5 = (f32[88,128]{1,0:T(8,128)S(1)}, f32[88,128]{1,0:T(8,128)S(1)}, u32[]{:S(2)}, u32[]{:S(2)}) collective-permute-start(f32[88,128]{1,0:T(8,128)S(1)} %get-tuple-element.23), channel_id=1, source_target_pairs={{0,1},{1,0},{2,3},{3,2},{4,8},{5,9},{6,10},{7,11},{8,4},{9,5},{10,... | collective-permute-start | bytes 135176 | tf_op jit(solution)/shard_map/ppermute | solution.py:532
  14.5 5.0 %copy-start = (s32[8,128]{1,0:T(8,128)S(1)}, s32[8,128]{1,0:T(8,128)}, u32[]{:S(2)}) copy-start(s32[8,128]{1,0:T(8,128)} %mask_ref.1) | copy-start | bytes 12292
  14.5 12.2 %all-to-all-start = ((f32[32,1,128]{2,1,0:T(1,128)}), f32[32,1,128]{2,1,0:T(1,128)S(1)}, u32[]{:S(2)}, u32[]{:S(2)}) async-start(f32[32,1,128]{2,1,0:T(1,128)} %bitcast.3), calls=%async_computation | async-start | bytes 32768 | tf_op jit(solution)/shard_map/all_to_all | solution.py:545

commit v5 on v4

--- a/solution.py
+++ b/solution.py
@@ -124,7 +124,8 @@
                 q = COMPS * k + c
                 x.append(state_ref[tile(p * PER + q), :] * sea)
                 m_ref[tile(p * PER + q), :] = x[c]
-                acc = jnp.where(slot == q, roll(x[c], SLOT * q + SLOT // 2, 1), acc)
+                at = PER - 1 - q
+                acc = jnp.where(slot == at, roll(x[c], SLOT * at + SLOT // 2, 1), acc)
             u, v = x[2:]
             below_u, below_v = roll(u, -1, 0), roll(v, -1, 0)
             right_u, right_v = roll(u, -1, 1), roll(v, -1, 1)
@@ -152,12 +153,20 @@
     pack_ref[tile(lay.packs), :] = acc
 
 
+def packed_comp(shape):
+    return COMPS - 1 - lax.rem(lax.broadcasted_iota(jnp.int32, shape, 1) // SLOT, COMPS)
+
+
+def unpack(x, t):
+    return roll(x, -(SLOT * (PER - 1 - t % PER) + SLOT // 2), 1)
+
+
 def spread(x, of):
-    comp = lax.rem(lax.broadcasted_iota(jnp.int32, x.shape, 1) // SLOT, COMPS)
+    comp = packed_comp(x.shape)
     out = x
     for c in range(COMPS):
         if c != of:
-            out = jnp.where(comp == c, roll(x, SLOT * (c - of), 1), out)
+            out = jnp.where(comp == c, roll(x, SLOT * (of - c), 1), out)
     return out
 
 
@@ -206,10 +215,10 @@
         value = flat_ref[tile(f), :]
         if 2 <= f <= 3:
             border = (lane == 0) | (lane == LANES - 1)
-            value = value + jnp.where(border, roll(inner, -(SLOT * f + SLOT // 2), 1), 0.0)
+            value = value + jnp.where(border, unpack(inner, f), 0.0)
             mid = STRIP * f + STRIP // 2
             border = (lane == mid - 1) | (lane == mid)
-            strip = strip + jnp.where(border, roll(outer, mid - (SLOT * f + SLOT // 2), 1), 0.0)
+            strip = strip + jnp.where(border, roll(unpack(outer, f), mid, 1), 0.0)
         own_ref[tile(f), :] = value
     own_ref[tile(FLAT), :] = strip
 
@@ -275,7 +284,7 @@
     cross_ref[...] = out
 
 
-def moment_kernel(own_ref, near_ref, cross_ref, one_ref, two_ref, basis_ref, send_ref, wide_ref, *, levels):
+def moment_kernel(own_ref, near_ref, cross_ref, one_ref, two_ref, done_ref, basis_ref, send_ref, wide_ref, *, levels):
     lay = Layout(levels * COMPS)
     at = Place()
     row, lane = iota(0), iota(1)
@@ -300,11 +309,10 @@
     top, bottom = near_ref[0 : lay.pad, :], near_ref[lay.pad :, :]
 
     def flow_packed(x):
-        return roll(x, SLOT, 1)
+        return roll(x, -SLOT, 1)
 
     def corner(a, b):
-        comp = lax.rem(iota(1, lay.pad) // SLOT, COMPS)
-        x = jnp.where(comp == 3, flow_packed(a), a) * b
+        x = jnp.where(packed_comp(a.shape) == 3, flow_packed(a), a) * b
         return 0.5 * fold(jnp.sum(x, axis=0, keepdims=True))
 
     corners = [corner(above, top), -corner(top, above), corner(bottom, below), -corner(below, bottom)]
@@ -313,7 +321,7 @@
         for k, at_row in enumerate((ROWS - 1, ROWS, 2 * ROWS - 1, 2 * ROWS)):
             to = pl.ds(f * rows + at_row, 1)
             wide_ref[to, 0:LANES] = wide_ref[to, 0:LANES] + cross_ref[4 * (f - 2) + k : 4 * (f - 2) + k + 1, :]
-            side = roll(corners[k], -(SLOT * f + SLOT // 2), 1)
+            side = unpack(corners[k], f)
             wide_ref[to, LANES : 2 * LANES] = wide_ref[to, LANES : 2 * LANES] + jnp.where(border, side, 0.0)
 
     sum_u, sum_v, adv_u, adv_v, forcing, diagonal = [wide_ref[pl.ds(f * rows, rows), :] for f in range(FLAT)]
@@ -364,7 +372,28 @@
     send_ref[...] = jnp.broadcast_to(line, send_ref.shape)
 
 
-def solve_kernel(got_ref, basis_ref, done_ref, out_ref):
+def solve_kernel(
+    got_ref, basis_ref, one_ref, two_ref, mask_ref, state_in, state_ref, state_hbm, surface_hbm, surface_ref, sems
+):
+    lay = Layout(state_ref.shape[0] // ROWS)
+    at = Place()
+    place = pl.ds(lay.delta, lay.pad)
+    one, two = one_ref[place, :], two_ref[place, :]
+    in_slot = lax.rem(iota(1, lay.pad), SLOT)
+    border = (iota(1) < SLOT // 2) | (iota(1) >= LANES - SLOT // 2)
+    near = (in_slot == SLOT // 2 - 1) | (in_slot == SLOT // 2)
+    sea = mask_ref[...].astype(F32)
+    for row, delta in ((0, at.from_up(one, two)), (ROWS - 1, at.from_down(one, two))):
+        fix = jnp.where(near, across(-2.0 * hyper_visc * delta), 0.0)
+        for s in range(lay.eights):
+            p, q = divmod(s * ROWS, PER)
+            x = jnp.broadcast_to(fix[p : p + 1], (ROWS, LANES))
+            x = pltpu.roll(x, SLOT * q + SLOT // 2, 1, stride=SLOT, stride_axis=0)
+            to = pl.ds(ROWS * ROWS * s + row, ROWS, stride=ROWS)
+            state_ref[to, :] = state_ref[to, :] + sea[row : row + 1] * jnp.where(border, x, 0.0)
+    write = pltpu.make_async_copy(state_ref, state_hbm, sems.at[0])
+    write.start()
+
     line = jnp.sum(got_ref[...], axis=0, keepdims=True)
     lane = iota(1, 1)
     moment = [jnp.sum(jnp.where(lane == k, line, 0.0), axis=1, keepdims=True) for k in range(2 * ITERS)]
@@ -398,12 +427,14 @@
     out = surface[0] * basis_ref[tile(0), :]
     for k in range(1, ITERS):
         out = out + surface[k] * basis_ref[tile(k), :]
-    out_ref[...] = out
-
-
-def step_kernel(
-    m_ref, pack_ref, delta_ref, rows_one_ref, rows_two_ref, one_ref, two_ref, mask_ref, new_ref, done_ref, ext_ref, corr_ref
-):
+    surface_ref[...] = out
+    write_surface = pltpu.make_async_copy(surface_ref, surface_hbm, sems.at[1])
+    write_surface.start()
+    write.wait()
+    write_surface.wait()
+
+
+def step_kernel(m_ref, pack_ref, delta_ref, rows_one_ref, rows_two_ref, mask_ref, new_ref, done_ref, ext_ref, corr_ref):
     lay = Layout(m_ref.shape[0] // ROWS)
     at = Place()
     row, lane = iota(0), iota(1)
@@ -422,10 +453,7 @@
     sign = jnp.where(in_slot == 3, -0.5 * time_step, jnp.where(in_slot == 4, 0.5 * time_step, 0.0))
     for p in range(lay.packs):
         d = delta_ref[tile(p), :]
-        one, two = one_ref[pl.ds(lay.delta + p, 1), :], two_ref[pl.ds(lay.delta + p, 1), :]
-        dv = jnp.where(row == 0, at.from_up(one, two), roll(d, 1, 0)) + jnp.where(
-            row == ROWS - 1, at.from_down(one, two), roll(d, -1, 0)
-        )
+        dv = jnp.where(row == 0, 0.0, roll(d, 1, 0)) + jnp.where(row == ROWS - 1, 0.0, roll(d, -1, 0))
         second = jnp.where(half, roll(d, -2, 1), roll(d, 2, 1))
         corr_ref[tile(p), :] = (
             jnp.where(far, -hyper_visc * second, 0.0)
@@ -471,19 +499,19 @@
                 out = out + coriolis * v
             if c == 3:
                 out = out - coriolis * u
-            p, s = divmod(t, PER)
-            fix = roll(corr_ref[tile(p), :], -(SLOT * s + SLOT // 2), 1)
+            fix = unpack(corr_ref[tile(t // PER), :], t)
             new_ref[tile(t), :] = sea * (out + jnp.where(border, fix, 0.0))
 
 
-def call(kernel, outs, *args, scratch=(), specs=None, flops=0, vmem=8):
+def call(kernel, outs, *args, scratch=(), specs=None, out_specs=None, aliases=None, flops=0):
     return pl.pallas_call(
         kernel,
-        out_shape=[jax.ShapeDtypeStruct(s, F32) if isinstance(s, tuple) else s for s in outs],
+        out_shape=[jax.ShapeDtypeStruct(s, F32) for s in outs],
         in_specs=specs or [VMEM] * len(args),
-        out_specs=[VMEM] * len(outs),
+        out_specs=out_specs or [VMEM] * len(outs),
         scratch_shapes=[pltpu.VMEM(s, F32) if isinstance(s, tuple) else s for s in scratch],
-        compiler_params=pltpu.CompilerParams(vmem_limit_bytes=vmem * 1024 * 1024),
+        input_output_aliases=aliases or {},
+        compiler_params=pltpu.CompilerParams(vmem_limit_bytes=8 * 1024 * 1024),
         cost_estimate=pl.CostEstimate(flops=flops, bytes_accessed=0, transcendentals=0),
     )(*args)
 
@@ -526,11 +554,23 @@
         flat,
         first,
         second,
-        flops=LONG,
+        flops=10 * LONG,
     )
     one = lax.ppermute(one, axes, b_one)
     two = lax.ppermute(two, axes, b_two)
     (cross,) = call(cross_kernel, [one_tile], m, rows_one, rows_two)
+    part, done = call(
+        step_kernel,
+        [state.shape, one_tile],
+        m,
+        pack,
+        delta,
+        rows_one,
+        rows_two,
+        land_mask,
+        scratch=[(lay.tiles * EXT, LANES), packed],
+        flops=LONG,
+    )
     basis, sent = call(
         functools.partial(moment_kernel, levels=lay.levels),
         [(ITERS * ROWS, LANES), (nb * ng, LANES)],
@@ -539,25 +579,24 @@
         cross,
         one,
         two,
+        done,
         scratch=[(FLAT * 3 * ROWS, 2 * LANES)],
         flops=LONG,
     )
     got = lax.all_to_all(sent, axes, 0, 0, tiled=True)
-    new_state, done = call(
-        step_kernel,
-        [state.shape, one_tile],
-        m,
-        pack,
-        delta,
-        rows_one,
-        rows_two,
+    _, new_state, surface = call(
+        solve_kernel,
+        [state.shape, state.shape, one_tile],
+        got,
+        basis,
         one,
         two,
         land_mask,
-        scratch=[(lay.tiles * EXT, LANES), packed],
-        flops=LONG,
-    )
-    (surface,) = call(solve_kernel, [one_tile], got, basis, done)
+        part,
+        scratch=[one_tile, pltpu.SemaphoreType.DMA((2,))],
+        out_specs=[VMEM, HBM, HBM],
+        aliases={5: 0},
+    )
     return new_state.reshape(ocean_state.shape), surface
 
 

time: 27.6 us -> 26.8 us (0.971)
  blocking collectives: 0 us -> 11.3 us
  starting transfers between devices: 13.2 us -> 6.96 us
  waiting for transfers between devices: 7.32 us -> 2.56 us
  Pallas kernels: 6.13 us -> 5.05 us
    all_to_all x0 -> x1, blocking collectives: none -> 11.3 us  [on_device(): got = lax.all_to_all(sent, axes, 0, 0, tiled=True)]
    all_to_all x1 -> x0, waiting for transfers between devices: 5.12 us -> none  [on_device(): got = lax.all_to_all(sent, axes, 0, 0, tiled=True)]
    all_to_all x1 -> x0, starting transfers between devices: 5.01 us -> none  [on_device(): got = lax.all_to_all(sent, axes, 0, 0, tiled=True)]
    ppermute x1, starting transfers between devices: 2.73 us -> 0.07 us  [on_device(): rows_two = lax.ppermute(rows_two, axes, b_two)]
    ppermute x1, waiting for transfers between devices: 0.01 us -> 1.75 us  [on_device(): first = lax.ppermute(pack, axes, g_one)]
    ppermute x1, waiting for transfers between devices: 1.34 us -> 0.01 us  [on_device(): two = lax.ppermute(two, axes, b_two)]
    pallas_call x7, Pallas kernels: 6.13 us -> 5.05 us  [call(): pl.pallas_call(kernel, out_shape=[jax.ShapeDtypeStruct(s, F32) for s in o...]
    ppermute x1, starting transfers between devices: 3.09 us -> 4.15 us  [on_device(): first = lax.ppermute(pack, axes, g_one)]
  transfers between devices with their start and end apart: 7 -> 6, of which waited for: 3 -> 2; matrix products, arithmetic and copies ran while one was open for 0% -> 0% of each run, Pallas kernels for 9% -> 7%
where the time goes in v5:
time: 26.8 us; the launch traced here: 26.6 us
  blocking collectives  11.3 us (42%)
  starting transfers between devices  6.96 us (26%)
  Pallas kernels  5.05 us (19%)
  waiting for transfers between devices  2.56 us (10%)
  between operations  0.71 us (3%)
    all_to_all x1, blocking collectives, on_device(): got = lax.all_to_all(sent, axes, 0, 0, tiled=True)  11.3 us
    pallas_call x7, Pallas kernels, call(): pl.pallas_call(kernel, out_shape=[jax.ShapeDtypeStruct(s, F32) for s in o...  5.05 us
    ppermute x1, starting transfers between devices, on_device(): first = lax.ppermute(pack, axes, g_one)  4.15 us
    ppermute x1, starting transfers between devices, on_device(): two = lax.ppermute(two, axes, b_two)  2.09 us
    ppermute x1, waiting for transfers between devices, on_device(): first = lax.ppermute(pack, axes, g_one)  1.75 us
    ppermute x1, waiting for transfers between devices, on_device(): rows_two = lax.ppermute(rows_two, axes, b_two)  0.8 us
  transfers between devices with their start and end apart: 6, of which 2 were waited for; matrix products, arithmetic and copies ran while one was open for 0% of the time, Pallas kernels for 7%

profile of v5, /device:TPU:0, one launch (start us, length us, event | category | flops | bytes accessed | tf_op | source)
XLA Modules:
  0.0 26.6 jit_solution(14592613084358402650)
XLA Ops:
  0.6 1.5 %shard_map.59 = (f32[1152,128]{1,0:T(8,128)S(1)}, f32[80,128]{1,0:T(8,128)S(1)}, f32[48,128]{1,0:T(8,128)S(1)}) custom-call(f32[1152,128]{1,0:T(8,128)} %bitcast.8, s32[8,128]{1,0:T(8,128)} %mask_ref.3, f32[8,128]{1,0:T(8,128)} %height_hbm.1, f32[8,128]{1,0:T(8,128)} %damp_hbm.1), custom_call_target="tpu_custom_call" | custom-call | tf_op jit(solution)/shard_map/pallas_call | solution.py:507
  2.1 0.5 %collective-permute-start.1 = (f32[80,128]{1,0:T(8,128)S(1)}, f32[80,128]{1,0:T(8,128)S(1)}, u32[]{:S(2)}, u32[]{:S(2)}) collective-permute-start(f32[80,128]{1,0:T(8,128)S(1)} %get-tuple-element.19.pack_ref), channel_id=1, source_target_pairs={{0,4},{1,2},{2,1},{3,7},{4,0},{5,6},{6,5},{7,3},{8,12},{9,10},{10,... | collective-permute-start | bytes 122888 | tf_op jit(solution)/shard_map/ppermute | solution.py:544
  2.7 4.1 %collective-permute-start = (f32[80,128]{1,0:T(8,128)S(1)}, f32[80,128]{1,0:T(8,128)S(1)}, u32[]{:S(2)}, u32[]{:S(2)}) collective-permute-start(f32[80,128]{1,0:T(8,128)S(1)} %get-tuple-element.19.pack_ref), channel_id=1, source_target_pairs={{0,1},{1,0},{2,3},{3,2},{4,5},{5,4},{6,7},{7,6},{8,9},{9,8},{10,11... | collective-permute-start | bytes 122888 | tf_op jit(solution)/shard_map/ppermute | solution.py:543
  6.8 0.1 shard_map.61
  6.9 0.1 collective-permute-start.2
  7.0 0.1 collective-permute-start.3
  7.0 0.0 collective-permute-done.1.second_ref
  7.0 1.7 %collective-permute-done.first_ref = f32[80,128]{1,0:T(8,128)S(1)} collective-permute-done((f32[80,128]{1,0:T(8,128)S(1)}, f32[80,128]{1,0:T(8,128)S(1)}, u32[]{:S(2)}, u32[]{:S(2)}) %collective-permute-start) | collective-permute-done | bytes 40992 | tf_op jit(solution)/shard_map/ppermute | solution.py:543
  8.8 0.4 %shard_map.60 = (f32[56,128]{1,0:T(8,128)S(1)}, f32[32,128]{1,0:T(8,128)S(1)}, f32[72,128]{1,0:T(8,128)S(1)}, f32[88,128]{1,0:T(8,128)S(1)}, f32[88,128]{1,0:T(8,128)S(1)}) custom-call(f32[1152,128]{1,0:T(8,128)S(1)} %get-tuple-element.18.m_ref, f32[80,128]{1,0:T(8,128)S(1)} %get-tuple-element.19.pack_ref, f32[48,128]{1,0:T(8,128)S(1)} %get-tuple-element.20.flat_ref, ...), custom_call_target="tpu_custom_call" | custom-call | flops 10000000000 | tf_op jit(solution)/shard_map/pallas_call | solution.py:507
  9.2 0.0 copy-start
  9.2 0.1 collective-permute-start.4
  9.3 2.1 %collective-permute-start.5 = (f32[88,128]{1,0:T(8,128)S(1)}, f32[88,128]{1,0:T(8,128)S(1)}, u32[]{:S(2)}, u32[]{:S(2)}) collective-permute-start(f32[88,128]{1,0:T(8,128)S(1)} %get-tuple-element.26), channel_id=1, source_target_pairs={{0,1},{1,0},{2,3},{3,2},{4,8},{5,9},{6,10},{7,11},{8,4},{9,5},{10,... | collective-permute-start | bytes 135176 | tf_op jit(solution)/shard_map/ppermute | solution.py:560
  11.4 0.0 collective-permute-done.2.one_ref.rows_one_ref
  11.4 0.8 %collective-permute-done.3.two_ref.rows_two_ref = f32[288,128]{1,0:T(8,128)S(1)} collective-permute-done((f32[288,128]{1,0:T(8,128)S(1)}, f32[288,128]{1,0:T(8,128)S(1)}, u32[]{:S(2)}, u32[]{:S(2)}) %collective-permute-start.3) | collective-permute-done | bytes 147488 | tf_op jit(solution)/shard_map/ppermute | solution.py:547
  12.2 0.0 copy-done
  12.2 1.3 %shard_map.63 = (f32[1152,128]{1,0:T(8,128)S(1)}, f32[8,128]{1,0:T(8,128)S(1)}) custom-call(f32[1152,128]{1,0:T(8,128)S(1)} %get-tuple-element.18.m_ref, f32[80,128]{1,0:T(8,128)S(1)} %get-tuple-element.19.pack_ref, f32[72,128]{1,0:T(8,128)S(1)} %get-tuple-element.27.delta_ref, f32[288,128]{1,0:T(8,128)S(1)} %collective-permute-done.2.one_ref.rows_one_ref, ...), custom_call_target="tpu_custom_call" | custom-call | flops 1000000000 | tf_op jit(solution)/shard_map/pallas_call | solution.py:507
  13.4 0.1 shard_map.62.cross_ref
  13.5 0.0 collective-permute-done.4.one_ref
  13.5 0.0 collective-permute-done.5.two_ref
  13.5 0.7 %shard_map.64 = (f32[24,128]{1,0:T(8,128)S(1)}, f32[32,128]{1,0:T(8,128)S(1)}) custom-call(f32[56,128]{1,0:T(8,128)S(1)} %get-tuple-element.21.own_ref, f32[32,128]{1,0:T(8,128)S(1)} %get-tuple-element.22.near_ref, f32[8,128]{1,0:T(8,128)S(1)} %shard_map.62.cross_ref, f32[88,128]{1,0:T(8,128)S(1)} %collective-permute-done.4.one_ref, ...), custom_call_target="tpu_custom_call" | custom-call | flops 1000000000 | tf_op jit(solution)/shard_map/pallas_call | solution.py:507
  14.2 11.3 %all_to_all.11 = f32[32,1,128]{2,1,0:T(1,128)S(1)} all-to-all(f32[32,1,128]{2,1,0:T(1,128)S(1)} %bitcast.7), channel_id=1, replica_groups=mesh['blocks'=8,'group'=4] {'blocks','group'}, dimensions={0} | all-to-all | bytes 32768 | tf_op jit(solution)/shard_map/all_to_all | solution.py:586
  25.6 1.0 %shard_map.65 = (f32[1152,128]{1,0:T(8,128)S(1)}, f32[1152,128]{1,0:T(8,128)}, f32[8,128]{1,0:T(8,128)}) custom-call(f32[32,128]{1,0:T(8,128)S(1)} %bitcast.6, f32[24,128]{1,0:T(8,128)S(1)} %get-tuple-element.30.basis_ref, f32[88,128]{1,0:T(8,128)S(1)} %collective-permute-done.4.one_ref, ...), custom_call_target="tpu_custom_call", output_to_operand_aliasing={{0}: (5, {})} | custom-call | tf_op jit(solution)/shard_map/pallas_call | solution.py:507
Async XLA Ops:
  2.1 4.9 %collective-permute-start.1 = (f32[80,128]{1,0:T(8,128)S(1)}, f32[80,128]{1,0:T(8,128)S(1)}, u32[]{:S(2)}, u32[]{:S(2)}) collective-permute-start(f32[80,128]{1,0:T(8,128)S(1)} %get-tuple-element.19.pack_ref), channel_id=1, source_target_pairs={{0,4},{1,2},{2,1},{3,7},{4,0},{5,6},{6,5},{7,3},{8,12},{9,10},{10,... | collective-permute-start | bytes 122888 | tf_op jit(solution)/shard_map/ppermute | solution.py:544
  2.7 6.1 %collective-permute-start = (f32[80,128]{1,0:T(8,128)S(1)}, f32[80,128]{1,0:T(8,128)S(1)}, u32[]{:S(2)}, u32[]{:S(2)}) collective-permute-start(f32[80,128]{1,0:T(8,128)S(1)} %get-tuple-element.19.pack_ref), channel_id=1, source_target_pairs={{0,1},{1,0},{2,3},{3,2},{4,5},{5,4},{6,7},{7,6},{8,9},{9,8},{10,11... | collective-permute-start | bytes 122888 | tf_op jit(solution)/shard_map/ppermute | solution.py:543
  6.9 4.5 %collective-permute-start.2 = (f32[288,128]{1,0:T(8,128)S(1)}, f32[288,128]{1,0:T(8,128)S(1)}, u32[]{:S(2)}, u32[]{:S(2)}) collective-permute-start(f32[288,128]{1,0:T(8,128)S(1)} %get-tuple-element.23), channel_id=1, source_target_pairs={{0,4},{1,5},{2,6},{3,7},{4,0},{5,1},{6,2},{7,3},{8,12},{9,13},{10,... | collective-permute-start | bytes 442376 | tf_op jit(solution)/shard_map/ppermute | solution.py:546
  7.0 5.2 %collective-permute-start.3 = (f32[288,128]{1,0:T(8,128)S(1)}, f32[288,128]{1,0:T(8,128)S(1)}, u32[]{:S(2)}, u32[]{:S(2)}) collective-permute-start(f32[288,128]{1,0:T(8,128)S(1)} %get-tuple-element.24), channel_id=1, source_target_pairs={{0,1},{1,0},{2,3},{3,2},{4,8},{5,9},{6,10},{7,11},{8,4},{9,5},{10,... | collective-permute-start | bytes 442376 | tf_op jit(solution)/shard_map/ppermute | solution.py:547
  9.2 3.0 %copy-start = (s32[8,128]{1,0:T(8,128)S(1)}, s32[8,128]{1,0:T(8,128)}, u32[]{:S(2)}) copy-start(s32[8,128]{1,0:T(8,128)} %mask_ref.3) | copy-start | bytes 12292
  9.2 4.3 %collective-permute-start.4 = (f32[88,128]{1,0:T(8,128)S(1)}, f32[88,128]{1,0:T(8,128)S(1)}, u32[]{:S(2)}, u32[]{:S(2)}) collective-permute-start(f32[88,128]{1,0:T(8,128)S(1)} %get-tuple-element.25), channel_id=1, source_target_pairs={{0,4},{1,5},{2,6},{3,7},{4,0},{5,1},{6,2},{7,3},{8,12},{9,13},{10,... | collective-permute-start | bytes 135176 | tf_op jit(solution)/shard_map/ppermute | solution.py:559
  9.3 4.2 %collective-permute-start.5 = (f32[88,128]{1,0:T(8,128)S(1)}, f32[88,128]{1,0:T(8,128)S(1)}, u32[]{:S(2)}, u32[]{:S(2)}) collective-permute-start(f32[88,128]{1,0:T(8,128)S(1)} %get-tuple-element.26), channel_id=1, source_target_pairs={{0,1},{1,0},{2,3},{3,2},{4,8},{5,9},{6,10},{7,11},{8,4},{9,5},{10,... | collective-permute-start | bytes 135176 | tf_op jit(solution)/shard_map/ppermute | solution.py:560

commit v6 on v5

--- a/solution.py
+++ b/solution.py
@@ -20,7 +20,6 @@
 LANES = 128
 SLOT = 8
 PER = LANES // SLOT
-EXT = 12
 FLAT = 6
 STRIP = 16
 LONG = 10**9
@@ -70,10 +69,11 @@
         self.pad = -(-self.packs // ROWS) * ROWS
         self.flow = -(-self.levels // ROWS) * ROWS
         self.edge = 0
-        self.delta = self.pad
-        self.flat = 2 * self.pad
+        self.flat = self.pad
         self.strip = self.flat + FLAT * ROWS
         self.message = self.strip + ROWS
+        self.delta = 2 * tiles
+        self.rest = self.delta + self.pad
 
 
 class Place:
@@ -184,7 +184,7 @@
 
 
 def edge_kernel(
-    m_ref, pack_ref, flat_ref, first_ref, second_ref, own_ref, near_ref, delta_ref, one_ref, two_ref
+    m_ref, pack_ref, flat_ref, first_ref, second_ref, done_ref, own_ref, near_ref, delta_ref, one_ref, two_ref
 ):
     lay = Layout(m_ref.shape[0] // ROWS)
     at = Place()
@@ -223,26 +223,53 @@
     own_ref[tile(FLAT), :] = strip
 
     def fill(low_ref, high_ref):
-        for ref, row, rows in ((low_ref, 0, slice(0, lay.pad)), (high_ref, ROWS - 1, slice(lay.pad, 2 * lay.pad))):
+        for ref, rows in ((low_ref, slice(0, lay.pad)), (high_ref, slice(lay.pad, 2 * lay.pad))):
             ref[pl.ds(lay.edge, lay.pad), :] = near_ref[rows, :]
-            ref[pl.ds(lay.delta, lay.pad), :] = jnp.zeros((lay.pad, LANES), F32)
-            for p in range(lay.packs):
-                ref[pl.ds(lay.delta + p, 1), :] = delta_ref[pl.ds(ROWS * p + row, 1), :]
             ref[pl.ds(lay.flat, (FLAT + 1) * ROWS), :] = own_ref[...]
 
     pl.when(at.b_even)(lambda: fill(two_ref, one_ref))
     pl.when(jnp.logical_not(at.b_even))(lambda: fill(one_ref, two_ref))
 
 
-def rows_kernel(m_ref, one_ref, two_ref):
+def level_rows(m_ref, comp, row):
     lay = Layout(m_ref.shape[0] // ROWS)
+    step = COMPS * ROWS
+    parts = []
+    for start in range(0, lay.levels, ROWS):
+        count = min(ROWS, lay.levels - start)
+        x = m_ref[pl.ds(start * step + comp * ROWS + row, count, stride=step), :]
+        if count < ROWS:
+            x = jnp.concatenate([x, jnp.zeros((ROWS - count, LANES), F32)], axis=0)
+        parts.append(x)
+    return parts
+
+
+def flow_kernel(m_ref, one_ref, two_ref):
+    lay = Layout(m_ref.shape[0] // ROWS)
 
     def fill(low_ref, high_ref):
-        for ref, row in ((low_ref, 0), (high_ref, ROWS - 2)):
+        for ref, row in ((low_ref, 0), (high_ref, ROWS - 1)):
+            for c in range(2):
+                for n, x in enumerate(level_rows(m_ref, 2 + c, row)):
+                    ref[pl.ds(c * lay.flow + n * ROWS, ROWS), :] = x
+
+    even = Place().b_even
+    pl.when(even)(lambda: fill(two_ref, one_ref))
+    pl.when(jnp.logical_not(even))(lambda: fill(one_ref, two_ref))
+
+
+def rest_kernel(m_ref, delta_ref, after_ref, one_ref, two_ref):
+    lay = Layout(m_ref.shape[0] // ROWS)
+
+    def fill(low_ref, high_ref):
+        for ref, row, near in ((low_ref, 0, 0), (high_ref, ROWS - 2, ROWS - 1)):
             for r in range(2):
                 for s in range(lay.eights):
                     at = pl.ds(ROWS * ROWS * s + row + r, ROWS, stride=ROWS)
                     ref[tile(r * lay.eights + s), :] = m_ref[at, :]
+            ref[pl.ds(lay.delta, lay.pad), :] = jnp.zeros((lay.pad, LANES), F32)
+            for p in range(lay.packs):
+                ref[pl.ds(lay.delta + p, 1), :] = delta_ref[pl.ds(ROWS * p + near, 1), :]
 
     even = Place().b_even
     pl.when(even)(lambda: fill(two_ref, one_ref))
@@ -253,25 +280,14 @@
     lay = Layout(m_ref.shape[0] // ROWS)
     at = Place()
     row = iota(0)
-
-    def level_rows(ref, comp, first, count_rows):
-        parts = []
-        for start in range(0, lay.levels, ROWS):
-            count = min(ROWS, lay.levels - start)
-            x = ref[pl.ds((start * COMPS + comp) * count_rows + first, count, stride=COMPS * count_rows), :]
-            if count < ROWS:
-                x = jnp.concatenate([x, jnp.zeros((ROWS - count, LANES), F32)], axis=0)
-            parts.append(x)
-        return parts
-
-    def beyond(first):
-        return [[level_rows(ref, c, first, 1) for c in (2, 3)] for ref in (one_ref, two_ref)]
-
-    one, two = beyond(lay.tiles)
-    above = [[at.from_up(x, y) for x, y in zip(one[c], two[c])] for c in range(2)]
-    one, two = beyond(0)
-    below = [[at.from_down(x, y) for x, y in zip(one[c], two[c])] for c in range(2)]
-    top, bottom = [[level_rows(m_ref, c, r, ROWS) for c in (2, 3)] for r in (0, ROWS - 1)]
+    count = lay.flow // ROWS
+
+    def beyond(take, c):
+        where = [pl.ds(c * lay.flow + n * ROWS, ROWS) for n in range(count)]
+        return [take(one_ref[w, :], two_ref[w, :]) for w in where]
+
+    above, below = [[beyond(take, c) for c in range(2)] for take in (at.from_up, at.from_down)]
+    top, bottom = [[level_rows(m_ref, c, r) for c in (2, 3)] for r in (0, ROWS - 1)]
 
     def total(flow, carried):
         return 0.5 * jnp.sum(sum(x * y for x, y in zip(flow, carried)), axis=0, keepdims=True)
@@ -373,24 +389,37 @@
 
 
 def solve_kernel(
-    got_ref, basis_ref, one_ref, two_ref, mask_ref, state_in, state_ref, state_hbm, surface_hbm, surface_ref, sems
+    got_ref, basis_ref, m_ref, one_ref, two_ref, mask_ref, state_in, state_ref, state_hbm, surface_hbm, surface_ref, sems
 ):
     lay = Layout(state_ref.shape[0] // ROWS)
     at = Place()
     place = pl.ds(lay.delta, lay.pad)
-    one, two = one_ref[place, :], two_ref[place, :]
     in_slot = lax.rem(iota(1, lay.pad), SLOT)
+    comp = lax.rem(iota(0), COMPS)
     border = (iota(1) < SLOT // 2) | (iota(1) >= LANES - SLOT // 2)
     near = (in_slot == SLOT // 2 - 1) | (in_slot == SLOT // 2)
     sea = mask_ref[...].astype(F32)
-    for row, delta in ((0, at.from_up(one, two)), (ROWS - 1, at.from_down(one, two))):
-        fix = jnp.where(near, across(-2.0 * hyper_visc * delta), 0.0)
+    sides = ((at.from_up, 1, 0, 0, 1, 0.5 * time_step), (at.from_down, 0, 1, ROWS - 1, ROWS - 2, -0.5 * time_step))
+    for take, first, second, row, inner, slope in sides:
+        fix = jnp.where(near, across(-2.0 * hyper_visc * take(one_ref[place, :], two_ref[place, :])), 0.0)
         for s in range(lay.eights):
+            x1, x2 = [take(one_ref[w, :], two_ref[w, :]) for w in (tile(n * lay.eights + s) for n in (first, second))]
+            flow = m_ref[pl.ds(ROWS * ROWS * s + row, ROWS, stride=ROWS), :]
+            u = flow
+            for c in (0, 1, 3):
+                u = jnp.where(comp == c, roll(flow, c - 2, 0), u)
             p, q = divmod(s * ROWS, PER)
-            x = jnp.broadcast_to(fix[p : p + 1], (ROWS, LANES))
-            x = pltpu.roll(x, SLOT * q + SLOT // 2, 1, stride=SLOT, stride_axis=0)
+            corner = jnp.broadcast_to(fix[p : p + 1], (ROWS, LANES))
+            corner = pltpu.roll(corner, SLOT * q + SLOT // 2, 1, stride=SLOT, stride_axis=0)
+            more = (
+                hyper_visc * (8.0 * x1 - x2 - 2.0 * (roll(x1, 1, 1) + roll(x1, -1, 1)))
+                + slope * u * x1
+                + jnp.where(border, corner, 0.0)
+            )
             to = pl.ds(ROWS * ROWS * s + row, ROWS, stride=ROWS)
-            state_ref[to, :] = state_ref[to, :] + sea[row : row + 1] * jnp.where(border, x, 0.0)
+            state_ref[to, :] = state_ref[to, :] + sea[row : row + 1] * more
+            to = pl.ds(ROWS * ROWS * s + inner, ROWS, stride=ROWS)
+            state_ref[to, :] = state_ref[to, :] - (hyper_visc * sea[inner : inner + 1]) * x1
     write = pltpu.make_async_copy(state_ref, state_hbm, sems.at[0])
     write.start()
 
@@ -434,33 +463,10 @@
     write_surface.wait()
 
 
-def step_kernel(m_ref, pack_ref, delta_ref, rows_one_ref, rows_two_ref, mask_ref, new_ref, done_ref, ext_ref, corr_ref):
+def inner_kernel(m_ref, mask_ref, new_ref, done_ref):
     lay = Layout(m_ref.shape[0] // ROWS)
     at = Place()
     row, lane = iota(0), iota(1)
-    for t in range(lay.tiles):
-        ext_ref[pl.ds(EXT * t + 2, ROWS), :] = m_ref[tile(t), :]
-    for r in range(2):
-        for s in range(lay.eights):
-            one, two = rows_one_ref[tile(r * lay.eights + s), :], rows_two_ref[tile(r * lay.eights + s), :]
-            ext_ref[pl.ds(EXT * ROWS * s + r, ROWS, stride=EXT), :] = at.from_up(one, two)
-            ext_ref[pl.ds(EXT * ROWS * s + ROWS + 2 + r, ROWS, stride=EXT), :] = at.from_down(one, two)
-
-    in_slot = lax.rem(lane, SLOT)
-    half = in_slot < SLOT // 2
-    near = (in_slot == 3) | (in_slot == 4)
-    far = (in_slot >= 2) & (in_slot <= 5)
-    sign = jnp.where(in_slot == 3, -0.5 * time_step, jnp.where(in_slot == 4, 0.5 * time_step, 0.0))
-    for p in range(lay.packs):
-        d = delta_ref[tile(p), :]
-        dv = jnp.where(row == 0, 0.0, roll(d, 1, 0)) + jnp.where(row == ROWS - 1, 0.0, roll(d, -1, 0))
-        second = jnp.where(half, roll(d, -2, 1), roll(d, 2, 1))
-        corr_ref[tile(p), :] = (
-            jnp.where(far, -hyper_visc * second, 0.0)
-            + jnp.where(near, across(hyper_visc * (8.0 * d - 2.0 * dv)), 0.0)
-            + sign * spread(pack_ref[tile(p), :], 3) * across(d)
-        )
-
     sea = mask_ref[...].astype(F32)
     done_ref[...] = sea
     edges = (
@@ -472,7 +478,6 @@
     centre = 1.0 - 2.0 * mixing - hyper_visc * (20.0 - edges)
     col = (lane + at.g * LANES).astype(F32)
     coriolis = time_step * rotation * (2.0 * (col + 0.5) / (at.ng * LANES) - 1.0)
-    border = (lane < SLOT // 2) | (lane >= LANES - SLOT // 2)
 
     def own(level, c):
         return m_ref[tile(COMPS * min(max(level, 0), lay.levels - 1) + c), :]
@@ -483,7 +488,8 @@
         for c in range(COMPS):
             t = COMPS * k + c
             x = own(k, c)
-            up2, up1, dn1, dn2 = [ext_ref[pl.ds(EXT * t + n, ROWS), :] for n in (0, 1, 3, 4)]
+            up1, dn1 = jnp.where(row == 0, 0.0, roll(x, 1, 0)), jnp.where(row == ROWS - 1, 0.0, roll(x, -1, 0))
+            up2, dn2 = jnp.where(row < 2, 0.0, roll(x, 2, 0)), jnp.where(row >= ROWS - 2, 0.0, roll(x, -2, 0))
             left, right = roll(x, 1, 1), roll(x, -1, 1)
             near1 = up1 + dn1
             q = 8.0 * hyper_visc * x - 2.0 * hyper_visc * near1
@@ -499,8 +505,32 @@
                 out = out + coriolis * v
             if c == 3:
                 out = out - coriolis * u
-            fix = unpack(corr_ref[tile(t // PER), :], t)
-            new_ref[tile(t), :] = sea * (out + jnp.where(border, fix, 0.0))
+            new_ref[tile(t), :] = sea * out
+
+
+def border_kernel(pack_ref, delta_ref, mask_ref, state_in, state_ref, done_ref):
+    lay = Layout(state_ref.shape[0] // ROWS)
+    row, lane = iota(0), iota(1)
+    border = (lane < SLOT // 2) | (lane >= LANES - SLOT // 2)
+    sea = mask_ref[...].astype(F32)
+    sea = jnp.where(border, sea, 0.0)
+    done_ref[...] = sea
+    in_slot = lax.rem(lane, SLOT)
+    half = in_slot < SLOT // 2
+    near = (in_slot == 3) | (in_slot == 4)
+    far = (in_slot >= 2) & (in_slot <= 5)
+    sign = jnp.where(in_slot == 3, -0.5 * time_step, jnp.where(in_slot == 4, 0.5 * time_step, 0.0))
+    for p in range(lay.packs):
+        d = delta_ref[tile(p), :]
+        dv = jnp.where(row == 0, 0.0, roll(d, 1, 0)) + jnp.where(row == ROWS - 1, 0.0, roll(d, -1, 0))
+        second = jnp.where(half, roll(d, -2, 1), roll(d, 2, 1))
+        fix = (
+            jnp.where(far, -hyper_visc * second, 0.0)
+            + jnp.where(near, across(hyper_visc * (8.0 * d - 2.0 * dv)), 0.0)
+            + sign * spread(pack_ref[tile(p), :], 3) * across(d)
+        )
+        for t in range(p * PER, (p + 1) * PER):
+            state_ref[tile(t), :] = state_ref[tile(t), :] + sea * unpack(fix, t)
 
 
 def call(kernel, outs, *args, scratch=(), specs=None, out_specs=None, aliases=None, flops=0):
@@ -542,9 +572,10 @@
     )
     first = lax.ppermute(pack, axes, g_one)
     second = lax.ppermute(pack, axes, g_two)
-    rows_one, rows_two = call(rows_kernel, [(2 * lay.tiles, LANES)] * 2, m)
-    rows_one = lax.ppermute(rows_one, axes, b_one)
-    rows_two = lax.ppermute(rows_two, axes, b_two)
+    flow_one, flow_two = call(flow_kernel, [(2 * lay.flow, LANES)] * 2, m)
+    flow_one = lax.ppermute(flow_one, axes, b_one)
+    flow_two = lax.ppermute(flow_two, axes, b_two)
+    part, inner_done = call(inner_kernel, [state.shape, one_tile], m, land_mask, flops=LONG)
     message = (lay.message, LANES)
     own, near, delta, one, two = call(
         edge_kernel,
@@ -554,23 +585,16 @@
         flat,
         first,
         second,
+        inner_done,
         flops=10 * LONG,
     )
     one = lax.ppermute(one, axes, b_one)
     two = lax.ppermute(two, axes, b_two)
-    (cross,) = call(cross_kernel, [one_tile], m, rows_one, rows_two)
-    part, done = call(
-        step_kernel,
-        [state.shape, one_tile],
-        m,
-        pack,
-        delta,
-        rows_one,
-        rows_two,
-        land_mask,
-        scratch=[(lay.tiles * EXT, LANES), packed],
-        flops=LONG,
-    )
+    (cross,) = call(cross_kernel, [one_tile], m, flow_one, flow_two)
+    part, done = call(border_kernel, [state.shape, one_tile], pack, delta, land_mask, part, aliases={3: 0}, flops=LONG)
+    rest_one, rest_two = call(rest_kernel, [(lay.rest, LANES)] * 2, m, delta, cross)
+    rest_one = lax.ppermute(rest_one, axes, b_one)
+    rest_two = lax.ppermute(rest_two, axes, b_two)
     basis, sent = call(
         functools.partial(moment_kernel, levels=lay.levels),
         [(ITERS * ROWS, LANES), (nb * ng, LANES)],
@@ -589,13 +613,14 @@
         [state.shape, state.shape, one_tile],
         got,
         basis,
-        one,
-        two,
+        m,
+        rest_one,
+        rest_two,
         land_mask,
         part,
         scratch=[one_tile, pltpu.SemaphoreType.DMA((2,))],
         out_specs=[VMEM, HBM, HBM],
-        aliases={5: 0},
+        aliases={6: 0},
     )
     return new_state.reshape(ocean_state.shape), surface
 

time: 26.8 us -> 26.6 us (level)
  waiting for transfers between devices: 2.56 us -> 0.56 us
  starting transfers between devices: 6.96 us -> 8.62 us
  blocking collectives: 11.3 us -> 10.5 us
  Pallas kernels: 5.05 us -> 5.56 us
  local copies, waits for them, and re-layouts: 0.01 us -> 0.47 us
    ppermute x2 -> x4, starting transfers between devices: 0.14 us -> 1.81 us  [the longest x1 1.24 us: on_device(): rest_two = lax.ppermute(rest_two, axes, b_two)]
    ppermute x1, waiting for transfers between devices: 1.75 us -> 0.29 us  [on_device(): first = lax.ppermute(pack, axes, g_one)]
    ppermute x1, starting transfers between devices: 2.09 us -> 1.24 us  [on_device(): two = lax.ppermute(two, axes, b_two)]
    ppermute x1, starting transfers between devices: 0.06 us -> 0.91 us  [on_device(): one = lax.ppermute(one, axes, b_one)]
    all_to_all x1, blocking collectives: 11.3 us -> 10.5 us  [on_device(): got = lax.all_to_all(sent, axes, 0, 0, tiled=True)]
    ppermute x2 -> x4, waiting for transfers between devices: 0.8 us -> 0.01 us  [the longest x1 0.01 us: on_device(): rest_one = lax.ppermute(rest_one, axes, b_one)]
    pallas_call x7 -> x9, Pallas kernels: 5.05 us -> 5.56 us  [call(): pl.pallas_call(kernel, out_shape=[jax.ShapeDtypeStruct(s, F32) for s in o...]
    unnamed x2, local copies, waits for them, and re-layouts: 0.01 us -> 0.47 us
  transfers between devices with their start and end apart: 6 -> 8, of which waited for: 2 -> 2; matrix products, arithmetic and copies ran while one was open for 0% -> 0% of each run, Pallas kernels for 7% -> 11%
where the time goes in v6:
time: 26.6 us; the launch traced here: 26.4 us
  blocking collectives  10.5 us (39%)
  starting transfers between devices  8.62 us (32%)
  Pallas kernels  5.56 us (21%)
  between operations  0.71 us (3%)
  waiting for transfers between devices  0.56 us (2%)
  local copies, waits for them, and re-layouts  0.47 us (2%)
    all_to_all x1, blocking collectives, on_device(): got = lax.all_to_all(sent, axes, 0, 0, tiled=True)  10.5 us
    pallas_call x9, Pallas kernels, call(): pl.pallas_call(kernel, out_shape=[jax.ShapeDtypeStruct(s, F32) for s in o...  5.56 us
    ppermute x1, starting transfers between devices, on_device(): first = lax.ppermute(pack, axes, g_one)  4.15 us
    ppermute x1, starting transfers between devices, on_device(): two = lax.ppermute(two, axes, b_two)  1.24 us
    ppermute x1, starting transfers between devices, on_device(): rest_two = lax.ppermute(rest_two, axes, b_two)  1.24 us
    ppermute x1, starting transfers between devices, on_device(): one = lax.ppermute(one, axes, b_one)  0.91 us
  transfers between devices with their start and end apart: 8, of which 2 were waited for; matrix products, arithmetic and copies ran while one was open for 0% of the time, Pallas kernels for 11%

profile of v6, /device:TPU:0, one launch (start us, length us, event | category | flops | bytes accessed | tf_op | source)
XLA Modules:
  0.0 26.4 jit_solution(8073337474578575505)
XLA Ops:
  0.6 1.5 %shard_map.59 = (f32[1152,128]{1,0:T(8,128)S(1)}, f32[80,128]{1,0:T(8,128)S(1)}, f32[48,128]{1,0:T(8,128)S(1)}) custom-call(f32[1152,128]{1,0:T(8,128)} %bitcast.8, s32[8,128]{1,0:T(8,128)} %mask_ref.5, f32[8,128]{1,0:T(8,128)} %height_hbm.1, f32[8,128]{1,0:T(8,128)} %damp_hbm.1), custom_call_target="tpu_custom_call" | custom-call | tf_op jit(solution)/shard_map/pallas_call | solution.py:537
  2.1 0.5 %collective-permute-start.1 = (f32[80,128]{1,0:T(8,128)S(1)}, f32[80,128]{1,0:T(8,128)S(1)}, u32[]{:S(2)}, u32[]{:S(2)}) collective-permute-start(f32[80,128]{1,0:T(8,128)S(1)} %get-tuple-element.23.pack_ref), channel_id=1, source_target_pairs={{0,4},{1,2},{2,1},{3,7},{4,0},{5,6},{6,5},{7,3},{8,12},{9,10},{10,... | collective-permute-start | bytes 122888 | tf_op jit(solution)/shard_map/ppermute | solution.py:574
  2.7 4.1 %collective-permute-start = (f32[80,128]{1,0:T(8,128)S(1)}, f32[80,128]{1,0:T(8,128)S(1)}, u32[]{:S(2)}, u32[]{:S(2)}) collective-permute-start(f32[80,128]{1,0:T(8,128)S(1)} %get-tuple-element.23.pack_ref), channel_id=1, source_target_pairs={{0,1},{1,0},{2,3},{3,2},{4,5},{5,4},{6,7},{7,6},{8,9},{9,8},{10,11... | collective-permute-start | bytes 122888 | tf_op jit(solution)/shard_map/ppermute | solution.py:573
  6.8 0.0 copy-start
  6.9 0.1 collective-permute-start.2
  6.9 0.1 collective-permute-start.3
  7.0 0.5 %copy-done = s32[8,128]{1,0:T(8,128)S(1)} copy-done((s32[8,128]{1,0:T(8,128)S(1)}, s32[8,128]{1,0:T(8,128)}, u32[]{:S(2)}) %copy-start) | copy-done | bytes 4120
  7.5 1.0 %shard_map.60 = (f32[1152,128]{1,0:T(8,128)S(1)}, f32[8,128]{1,0:T(8,128)S(1)}) custom-call(f32[1152,128]{1,0:T(8,128)S(1)} %get-tuple-element.22.m_ref, s32[8,128]{1,0:T(8,128)S(1)} %copy-done), custom_call_target="tpu_custom_call" | custom-call | flops 1000000000 | tf_op jit(solution)/shard_map/pallas_call | solution.py:537
  8.5 0.0 collective-permute-done.1.second_ref
  8.5 0.3 %collective-permute-done.first_ref = f32[80,128]{1,0:T(8,128)S(1)} collective-permute-done((f32[80,128]{1,0:T(8,128)S(1)}, f32[80,128]{1,0:T(8,128)S(1)}, u32[]{:S(2)}, u32[]{:S(2)}) %collective-permute-start) | collective-permute-done | bytes 40992 | tf_op jit(solution)/shard_map/ppermute | solution.py:573
  8.8 0.4 %shard_map.61 = (f32[56,128]{1,0:T(8,128)S(1)}, f32[32,128]{1,0:T(8,128)S(1)}, f32[72,128]{1,0:T(8,128)S(1)}, f32[72,128]{1,0:T(8,128)S(1)}, f32[72,128]{1,0:T(8,128)S(1)}) custom-call(f32[1152,128]{1,0:T(8,128)S(1)} %get-tuple-element.22.m_ref, f32[80,128]{1,0:T(8,128)S(1)} %get-tuple-element.23.pack_ref, f32[48,128]{1,0:T(8,128)S(1)} %get-tuple-element.24.flat_ref, ...), custom_call_target="tpu_custom_call" | custom-call | flops 10000000000 | tf_op jit(solution)/shard_map/pallas_call | solution.py:537
  9.2 0.9 %collective-permute-start.4 = (f32[72,128]{1,0:T(8,128)S(1)}, f32[72,128]{1,0:T(8,128)S(1)}, u32[]{:S(2)}, u32[]{:S(2)}) collective-permute-start(f32[72,128]{1,0:T(8,128)S(1)} %get-tuple-element.30), channel_id=1, source_target_pairs={{0,4},{1,5},{2,6},{3,7},{4,0},{5,1},{6,2},{7,3},{8,12},{9,13},{10,... | collective-permute-start | bytes 110600 | tf_op jit(solution)/shard_map/ppermute | solution.py:591
  10.1 1.2 %collective-permute-start.5 = (f32[72,128]{1,0:T(8,128)S(1)}, f32[72,128]{1,0:T(8,128)S(1)}, u32[]{:S(2)}, u32[]{:S(2)}) collective-permute-start(f32[72,128]{1,0:T(8,128)S(1)} %get-tuple-element.31), channel_id=1, source_target_pairs={{0,1},{1,0},{2,3},{3,2},{4,8},{5,9},{6,10},{7,11},{8,4},{9,5},{10,... | collective-permute-start | bytes 110600 | tf_op jit(solution)/shard_map/ppermute | solution.py:592
  11.3 0.0 collective-permute-done.2.one_ref
  11.3 0.0 collective-permute-done.3.two_ref
  11.3 0.1 shard_map.63.cross_ref.after_ref
  11.4 0.1 shard_map.66
  11.5 0.4 %collective-permute-start.6 = (f32[304,128]{1,0:T(8,128)S(1)}, f32[304,128]{1,0:T(8,128)S(1)}, u32[]{:S(2)}, u32[]{:S(2)}) collective-permute-start(f32[304,128]{1,0:T(8,128)S(1)} %get-tuple-element.37), channel_id=1, source_target_pairs={{0,4},{1,5},{2,6},{3,7},{4,0},{5,1},{6,2},{7,3},{8,12},{9,13},{10,... | collective-permute-start | bytes 466952 | tf_op jit(solution)/shard_map/ppermute | solution.py:596
  11.9 1.2 %collective-permute-start.7 = (f32[304,128]{1,0:T(8,128)S(1)}, f32[304,128]{1,0:T(8,128)S(1)}, u32[]{:S(2)}, u32[]{:S(2)}) collective-permute-start(f32[304,128]{1,0:T(8,128)S(1)} %get-tuple-element.38), channel_id=1, source_target_pairs={{0,1},{1,0},{2,3},{3,2},{4,8},{5,9},{6,10},{7,11},{8,4},{9,5},{10,... | collective-permute-start | bytes 466952 | tf_op jit(solution)/shard_map/ppermute | solution.py:597
  13.2 0.6 %shard_map.64 = (f32[1152,128]{1,0:T(8,128)S(1)}, f32[8,128]{1,0:T(8,128)S(1)}) custom-call(f32[80,128]{1,0:T(8,128)S(1)} %get-tuple-element.23.pack_ref, f32[72,128]{1,0:T(8,128)S(1)} %get-tuple-element.32.delta_ref, s32[8,128]{1,0:T(8,128)S(1)} %copy-done, f32[1152,128]{1,0:T(8,128)S(1)} %get-tuple-element.33.state_in), custom_call_target="tpu_custom_call", output_to_operand_aliasing={{0}: (3, {})} | custom-call | flops 1000000000 | tf_op jit(solution)/shard_map/pallas_call | solution.py:537
  13.8 0.0 collective-permute-done.4.one_ref
  13.8 0.2 collective-permute-done.5.two_ref
  14.1 0.7 %shard_map.65 = (f32[24,128]{1,0:T(8,128)S(1)}, f32[32,128]{1,0:T(8,128)S(1)}) custom-call(f32[56,128]{1,0:T(8,128)S(1)} %get-tuple-element.26.own_ref, f32[32,128]{1,0:T(8,128)S(1)} %get-tuple-element.27.near_ref, f32[8,128]{1,0:T(8,128)S(1)} %shard_map.63.cross_ref.after_ref, f32[72,128]{1,0:T(8,128)S(1)} %collective-permute-done.4.one_ref, ...), custom_call_target="tpu_custom_call" | custom-call | flops 1000000000 | tf_op jit(solution)/shard_map/pallas_call | solution.py:537
  14.8 10.5 %all_to_all.11 = f32[32,1,128]{2,1,0:T(1,128)S(1)} all-to-all(f32[32,1,128]{2,1,0:T(1,128)S(1)} %bitcast.7), channel_id=1, replica_groups=mesh['blocks'=8,'group'=4] {'blocks','group'}, dimensions={0} | all-to-all | bytes 32768 | tf_op jit(solution)/shard_map/all_to_all | solution.py:610
  25.3 0.0 collective-permute-done.6.one_ref
  25.3 0.0 collective-permute-done.7.two_ref
  25.3 1.1 %shard_map.67 = (f32[1152,128]{1,0:T(8,128)S(1)}, f32[1152,128]{1,0:T(8,128)}, f32[8,128]{1,0:T(8,128)}) custom-call(f32[32,128]{1,0:T(8,128)S(1)} %bitcast.6, f32[24,128]{1,0:T(8,128)S(1)} %get-tuple-element.36.basis_ref, f32[1152,128]{1,0:T(8,128)S(1)} %get-tuple-element.22.m_ref, ...), custom_call_target="tpu_custom_call", output_to_operand_aliasing={{0}: (6, {})} | custom-call | tf_op jit(solution)/shard_map/pallas_call | solution.py:537
  (1 shorter events, 0.0 us)
Async XLA Ops:
  2.1 6.3 %collective-permute-start.1 = (f32[80,128]{1,0:T(8,128)S(1)}, f32[80,128]{1,0:T(8,128)S(1)}, u32[]{:S(2)}, u32[]{:S(2)}) collective-permute-start(f32[80,128]{1,0:T(8,128)S(1)} %get-tuple-element.23.pack_ref), channel_id=1, source_target_pairs={{0,4},{1,2},{2,1},{3,7},{4,0},{5,6},{6,5},{7,3},{8,12},{9,10},{10,... | collective-permute-start | bytes 122888 | tf_op jit(solution)/shard_map/ppermute | solution.py:574
  2.7 6.1 %collective-permute-start = (f32[80,128]{1,0:T(8,128)S(1)}, f32[80,128]{1,0:T(8,128)S(1)}, u32[]{:S(2)}, u32[]{:S(2)}) collective-permute-start(f32[80,128]{1,0:T(8,128)S(1)} %get-tuple-element.23.pack_ref), channel_id=1, source_target_pairs={{0,1},{1,0},{2,3},{3,2},{4,5},{5,4},{6,7},{7,6},{8,9},{9,8},{10,11... | collective-permute-start | bytes 122888 | tf_op jit(solution)/shard_map/ppermute | solution.py:573
  6.8 0.7 %copy-start = (s32[8,128]{1,0:T(8,128)S(1)}, s32[8,128]{1,0:T(8,128)}, u32[]{:S(2)}) copy-start(s32[8,128]{1,0:T(8,128)} %mask_ref.5) | copy-start | bytes 12292
  6.9 4.5 %collective-permute-start.2 = (f32[80,128]{1,0:T(8,128)S(1)}, f32[80,128]{1,0:T(8,128)S(1)}, u32[]{:S(2)}, u32[]{:S(2)}) collective-permute-start(f32[80,128]{1,0:T(8,128)S(1)} %get-tuple-element.28), channel_id=1, source_target_pairs={{0,4},{1,5},{2,6},{3,7},{4,0},{5,1},{6,2},{7,3},{8,12},{9,13},{10,... | collective-permute-start | bytes 122888 | tf_op jit(solution)/shard_map/ppermute | solution.py:576
  6.9 4.4 %collective-permute-start.3 = (f32[80,128]{1,0:T(8,128)S(1)}, f32[80,128]{1,0:T(8,128)S(1)}, u32[]{:S(2)}, u32[]{:S(2)}) collective-permute-start(f32[80,128]{1,0:T(8,128)S(1)} %get-tuple-element.29), channel_id=1, source_target_pairs={{0,1},{1,0},{2,3},{3,2},{4,8},{5,9},{6,10},{7,11},{8,4},{9,5},{10,... | collective-permute-start | bytes 122888 | tf_op jit(solution)/shard_map/ppermute | solution.py:577
  9.2 4.6 %collective-permute-start.4 = (f32[72,128]{1,0:T(8,128)S(1)}, f32[72,128]{1,0:T(8,128)S(1)}, u32[]{:S(2)}, u32[]{:S(2)}) collective-permute-start(f32[72,128]{1,0:T(8,128)S(1)} %get-tuple-element.30), channel_id=1, source_target_pairs={{0,4},{1,5},{2,6},{3,7},{4,0},{5,1},{6,2},{7,3},{8,12},{9,13},{10,... | collective-permute-start | bytes 110600 | tf_op jit(solution)/shard_map/ppermute | solution.py:591
  10.1 4.0 %collective-permute-start.5 = (f32[72,128]{1,0:T(8,128)S(1)}, f32[72,128]{1,0:T(8,128)S(1)}, u32[]{:S(2)}, u32[]{:S(2)}) collective-permute-start(f32[72,128]{1,0:T(8,128)S(1)} %get-tuple-element.31), channel_id=1, source_target_pairs={{0,1},{1,0},{2,3},{3,2},{4,8},{5,9},{6,10},{7,11},{8,4},{9,5},{10,... | collective-permute-start | bytes 110600 | tf_op jit(solution)/shard_map/ppermute | solution.py:592
  11.5 13.8 %collective-permute-start.6 = (f32[304,128]{1,0:T(8,128)S(1)}, f32[304,128]{1,0:T(8,128)S(1)}, u32[]{:S(2)}, u32[]{:S(2)}) collective-permute-start(f32[304,128]{1,0:T(8,128)S(1)} %get-tuple-element.37), channel_id=1, source_target_pairs={{0,4},{1,5},{2,6},{3,7},{4,0},{5,1},{6,2},{7,3},{8,12},{9,13},{10,... | collective-permute-start | bytes 466952 | tf_op jit(solution)/shard_map/ppermute | solution.py:596
  11.9 13.3 %collective-permute-start.7 = (f32[304,128]{1,0:T(8,128)S(1)}, f32[304,128]{1,0:T(8,128)S(1)}, u32[]{:S(2)}, u32[]{:S(2)}) collective-permute-start(f32[304,128]{1,0:T(8,128)S(1)} %get-tuple-element.38), channel_id=1, source_target_pairs={{0,1},{1,0},{2,3},{3,2},{4,8},{5,9},{6,10},{7,11},{8,4},{9,5},{10,... | collective-permute-start | bytes 466952 | tf_op jit(solution)/shard_map/ppermute | solution.py:597

commit v7 on v6

--- a/solution.py
+++ b/solution.py
@@ -68,10 +68,12 @@
         self.eights = tiles // ROWS
         self.pad = -(-self.packs // ROWS) * ROWS
         self.flow = -(-self.levels // ROWS) * ROWS
+        self.flat = 2 * self.flow
+        self.early = self.flat + FLAT * ROWS
         self.edge = 0
-        self.flat = self.pad
-        self.strip = self.flat + FLAT * ROWS
-        self.message = self.strip + ROWS
+        self.strip = self.pad
+        self.inner = self.strip + ROWS
+        self.message = self.inner + ROWS
         self.delta = 2 * tiles
         self.rest = self.delta + self.pad
 
@@ -183,12 +185,11 @@
     return x
 
 
-def edge_kernel(
-    m_ref, pack_ref, flat_ref, first_ref, second_ref, done_ref, own_ref, near_ref, delta_ref, one_ref, two_ref
-):
-    lay = Layout(m_ref.shape[0] // ROWS)
+def edge_kernel(pack_ref, first_ref, second_ref, done_ref, own_ref, near_ref, delta_ref, one_ref, two_ref):
+    lay = Layout((pack_ref.shape[0] // ROWS - 1) * PER)
     at = Place()
     lane = iota(1)
+    comp = packed_comp((ROWS, LANES))
     in_slot = lax.rem(lane, SLOT)
     half = in_slot < SLOT // 2
     sign = jnp.where(in_slot == SLOT // 2 - 1, 0.5, jnp.where(in_slot == SLOT // 2, -0.5, 0.0))
@@ -198,6 +199,9 @@
         from_left = jnp.where(at.g_even, second, first) * at.left
         from_right = jnp.where(at.g_even, first, second) * at.right
         return jnp.where(low, from_left, from_right)
+
+    def flow(x):
+        return jnp.where(comp == 2, roll(x, SLOT, 1), x)
 
     near_ref[...] = jnp.zeros(near_ref.shape, F32)
     inner = jnp.zeros((ROWS, LANES), F32)
@@ -207,25 +211,22 @@
         delta_ref[tile(p), :] = far - own
         near_ref[p : p + 1, :] = far[0:1]
         near_ref[lay.pad + p : lay.pad + p + 1, :] = far[ROWS - 1 : ROWS]
-        inner = inner + spread(own, 3) * across(far)
-        outer = outer + spread(far, 3) * across(own)
+        inner = inner + flow(own) * across(far)
+        outer = outer + flow(far) * across(own)
     inner, outer = fold(sign * inner), fold(sign * outer)
     strip = beyond(lay.packs, lax.rem(lane, STRIP) < STRIP // 2)
-    for f in range(FLAT):
-        value = flat_ref[tile(f), :]
-        if 2 <= f <= 3:
-            border = (lane == 0) | (lane == LANES - 1)
-            value = value + jnp.where(border, unpack(inner, f), 0.0)
-            mid = STRIP * f + STRIP // 2
-            border = (lane == mid - 1) | (lane == mid)
-            strip = strip + jnp.where(border, roll(unpack(outer, f), mid, 1), 0.0)
-        own_ref[tile(f), :] = value
-    own_ref[tile(FLAT), :] = strip
+    for f in (2, 3):
+        mid = STRIP * f + STRIP // 2
+        border = (lane == mid - 1) | (lane == mid)
+        strip = strip + jnp.where(border, roll(unpack(outer, f), mid, 1), 0.0)
+    own_ref[0:ROWS, :] = strip
+    own_ref[ROWS : 2 * ROWS, :] = inner
 
     def fill(low_ref, high_ref):
         for ref, rows in ((low_ref, slice(0, lay.pad)), (high_ref, slice(lay.pad, 2 * lay.pad))):
             ref[pl.ds(lay.edge, lay.pad), :] = near_ref[rows, :]
-            ref[pl.ds(lay.flat, (FLAT + 1) * ROWS), :] = own_ref[...]
+            ref[pl.ds(lay.strip, ROWS), :] = strip
+            ref[pl.ds(lay.inner, ROWS), :] = inner
 
     pl.when(at.b_even)(lambda: fill(two_ref, one_ref))
     pl.when(jnp.logical_not(at.b_even))(lambda: fill(one_ref, two_ref))
@@ -244,7 +245,7 @@
     return parts
 
 
-def flow_kernel(m_ref, one_ref, two_ref):
+def flow_kernel(m_ref, flat_ref, one_ref, two_ref):
     lay = Layout(m_ref.shape[0] // ROWS)
 
     def fill(low_ref, high_ref):
@@ -252,6 +253,7 @@
             for c in range(2):
                 for n, x in enumerate(level_rows(m_ref, 2 + c, row)):
                     ref[pl.ds(c * lay.flow + n * ROWS, ROWS), :] = x
+            ref[pl.ds(lay.flat, FLAT * ROWS), :] = flat_ref[...]
 
     even = Place().b_even
     pl.when(even)(lambda: fill(two_ref, one_ref))
@@ -300,24 +302,34 @@
     cross_ref[...] = out
 
 
-def moment_kernel(own_ref, near_ref, cross_ref, one_ref, two_ref, done_ref, basis_ref, send_ref, wide_ref, *, levels):
+def moment_kernel(
+    flat_ref, own_ref, near_ref, cross_ref, flow_one_ref, flow_two_ref, one_ref, two_ref, done_ref, basis_ref, send_ref, wide_ref, *, levels
+):
     lay = Layout(levels * COMPS)
     at = Place()
     row, lane = iota(0), iota(1)
     outside = (lane < STRIP // 2) | (lane >= LANES - STRIP // 2)
     rows = 3 * ROWS
 
-    def neighbours(where):
-        return at.from_up(one_ref[where, :], two_ref[where, :]), at.from_down(one_ref[where, :], two_ref[where, :])
-
-    strips = neighbours(pl.ds(lay.strip, ROWS))
-    strips = (strips[0], own_ref[tile(FLAT), :], strips[1])
+    def neighbours(where, first_ref=one_ref, second_ref=two_ref):
+        first, second = first_ref[where, :], second_ref[where, :]
+        return at.from_up(first, second), at.from_down(first, second)
+
+    def around(where, own, *refs):
+        up, down = neighbours(where, *refs)
+        return up, own, down
+
+    strips = around(pl.ds(lay.strip, ROWS), own_ref[0:ROWS, :])
+    inners = around(pl.ds(lay.inner, ROWS), own_ref[ROWS : 2 * ROWS, :])
+    border = (lane == 0) | (lane == LANES - 1)
     for f in range(FLAT):
-        fields = neighbours(pl.ds(lay.flat + f * ROWS, ROWS))
-        fields = (fields[0], own_ref[tile(f), :], fields[1])
+        fields = around(pl.ds(lay.flat + f * ROWS, ROWS), flat_ref[tile(f), :], flow_one_ref, flow_two_ref)
         for k in range(3):
             to = pl.ds(f * rows + k * ROWS, ROWS)
-            wide_ref[to, 0:LANES] = fields[k]
+            value = fields[k]
+            if 2 <= f <= 3:
+                value = value + jnp.where(border, unpack(inners[k], f), 0.0)
+            wide_ref[to, 0:LANES] = value
             side = roll(strips[k], -(STRIP * f + STRIP // 2), 1)
             wide_ref[to, LANES : 2 * LANES] = jnp.where(outside, side, 0.0)
 
@@ -400,9 +412,11 @@
     near = (in_slot == SLOT // 2 - 1) | (in_slot == SLOT // 2)
     sea = mask_ref[...].astype(F32)
     sides = ((at.from_up, 1, 0, 0, 1, 0.5 * time_step), (at.from_down, 0, 1, ROWS - 1, ROWS - 2, -0.5 * time_step))
-    for take, first, second, row, inner, slope in sides:
-        fix = jnp.where(near, across(-2.0 * hyper_visc * take(one_ref[place, :], two_ref[place, :])), 0.0)
-        for s in range(lay.eights):
+    fixes = [across(-2.0 * hyper_visc * side[0](one_ref[place, :], two_ref[place, :])) for side in sides]
+    fixes = [jnp.where(near, x, 0.0) for x in fixes]
+    writes = []
+    for s in range(lay.eights):
+        for (take, first, second, row, inner, slope), fix in zip(sides, fixes):
             x1, x2 = [take(one_ref[w, :], two_ref[w, :]) for w in (tile(n * lay.eights + s) for n in (first, second))]
             flow = m_ref[pl.ds(ROWS * ROWS * s + row, ROWS, stride=ROWS), :]
             u = flow
@@ -420,8 +434,11 @@
             state_ref[to, :] = state_ref[to, :] + sea[row : row + 1] * more
             to = pl.ds(ROWS * ROWS * s + inner, ROWS, stride=ROWS)
             state_ref[to, :] = state_ref[to, :] - (hyper_visc * sea[inner : inner + 1]) * x1
-    write = pltpu.make_async_copy(state_ref, state_hbm, sems.at[0])
-    write.start()
+        if s + 1 in (lay.eights // 2, lay.eights):
+            start = len(writes) * (lay.eights // 2) * ROWS * ROWS
+            part = pl.ds(start, (s + 1) * ROWS * ROWS - start)
+            writes.append(pltpu.make_async_copy(state_ref.at[part], state_hbm.at[part], sems.at[len(writes)]))
+            writes[-1].start()
 
     line = jnp.sum(got_ref[...], axis=0, keepdims=True)
     lane = iota(1, 1)
@@ -457,10 +474,10 @@
     for k in range(1, ITERS):
         out = out + surface[k] * basis_ref[tile(k), :]
     surface_ref[...] = out
-    write_surface = pltpu.make_async_copy(surface_ref, surface_hbm, sems.at[1])
-    write_surface.start()
-    write.wait()
-    write_surface.wait()
+    writes.append(pltpu.make_async_copy(surface_ref, surface_hbm, sems.at[len(writes)]))
+    writes[-1].start()
+    for write in writes:
+        write.wait()
 
 
 def inner_kernel(m_ref, mask_ref, new_ref, done_ref):
@@ -510,27 +527,27 @@
 
 def border_kernel(pack_ref, delta_ref, mask_ref, state_in, state_ref, done_ref):
     lay = Layout(state_ref.shape[0] // ROWS)
-    row, lane = iota(0), iota(1)
+    lane = iota(1)
     border = (lane < SLOT // 2) | (lane >= LANES - SLOT // 2)
     sea = mask_ref[...].astype(F32)
     sea = jnp.where(border, sea, 0.0)
     done_ref[...] = sea
-    in_slot = lax.rem(lane, SLOT)
-    half = in_slot < SLOT // 2
-    near = (in_slot == 3) | (in_slot == 4)
-    far = (in_slot >= 2) & (in_slot <= 5)
-    sign = jnp.where(in_slot == 3, -0.5 * time_step, jnp.where(in_slot == 4, 0.5 * time_step, 0.0))
-    for p in range(lay.packs):
-        d = delta_ref[tile(p), :]
-        dv = jnp.where(row == 0, 0.0, roll(d, 1, 0)) + jnp.where(row == ROWS - 1, 0.0, roll(d, -1, 0))
-        second = jnp.where(half, roll(d, -2, 1), roll(d, 2, 1))
-        fix = (
-            jnp.where(far, -hyper_visc * second, 0.0)
-            + jnp.where(near, across(hyper_visc * (8.0 * d - 2.0 * dv)), 0.0)
-            + sign * spread(pack_ref[tile(p), :], 3) * across(d)
-        )
-        for t in range(p * PER, (p + 1) * PER):
-            state_ref[tile(t), :] = state_ref[tile(t), :] + sea * unpack(fix, t)
+    d = delta_ref[...]
+    row, in_slot = lax.rem(iota(0, d.shape[0]), ROWS), lax.rem(iota(1, d.shape[0]), SLOT)
+    mid = SLOT // 2
+    near = (in_slot == mid - 1) | (in_slot == mid)
+    far = (in_slot >= mid - 2) & (in_slot <= mid + 1)
+    sign = jnp.where(in_slot == mid - 1, -0.5 * time_step, jnp.where(in_slot == mid, 0.5 * time_step, 0.0))
+    dv = jnp.where(row == 0, 0.0, roll(d, 1, 0)) + jnp.where(row == ROWS - 1, 0.0, roll(d, -1, 0))
+    second = jnp.where(in_slot < mid, roll(d, -2, 1), roll(d, 2, 1))
+    fix = (
+        jnp.where(far, -hyper_visc * second, 0.0)
+        + jnp.where(near, across(hyper_visc * (8.0 * d - 2.0 * dv)), 0.0)
+        + sign * spread(pack_ref[0 : d.shape[0], :], 3) * across(d)
+    )
+    for t in range(lay.tiles):
+        p = t // PER
+        state_ref[tile(t), :] = state_ref[tile(t), :] + sea * unpack(fix[p * ROWS : (p + 1) * ROWS], t)
 
 
 def call(kernel, outs, *args, scratch=(), specs=None, out_specs=None, aliases=None, flops=0):
@@ -572,17 +589,15 @@
     )
     first = lax.ppermute(pack, axes, g_one)
     second = lax.ppermute(pack, axes, g_two)
-    flow_one, flow_two = call(flow_kernel, [(2 * lay.flow, LANES)] * 2, m)
+    flow_one, flow_two = call(flow_kernel, [(lay.early, LANES)] * 2, m, flat)
     flow_one = lax.ppermute(flow_one, axes, b_one)
     flow_two = lax.ppermute(flow_two, axes, b_two)
     part, inner_done = call(inner_kernel, [state.shape, one_tile], m, land_mask, flops=LONG)
     message = (lay.message, LANES)
     own, near, delta, one, two = call(
         edge_kernel,
-        [(flats[0] + ROWS, LANES), (2 * lay.pad, LANES), packed, message, message],
-        m,
+        [(2 * ROWS, LANES), (2 * lay.pad, LANES), packed, message, message],
         pack,
-        flat,
         first,
         second,
         inner_done,
@@ -598,9 +613,12 @@
     basis, sent = call(
         functools.partial(moment_kernel, levels=lay.levels),
         [(ITERS * ROWS, LANES), (nb * ng, LANES)],
+        flat,
         own,
         near,
         cross,
+        flow_one,
+        flow_two,
         one,
         two,
         done,
@@ -618,7 +636,7 @@
         rest_two,
         land_mask,
         part,
-        scratch=[one_tile, pltpu.SemaphoreType.DMA((2,))],
+        scratch=[one_tile, pltpu.SemaphoreType.DMA((3,))],
         out_specs=[VMEM, HBM, HBM],
         aliases={6: 0},
     )

time: 26.6 us -> 26.2 us (0.985)
  Pallas kernels: 5.56 us -> 5.21 us
    pallas_call x9, Pallas kernels: 5.56 us -> 5.21 us  [call(): pl.pallas_call(kernel, out_shape=[jax.ShapeDtypeStruct(s, F32) for s in o...]
  transfers between devices with their start and end apart: 8 -> 8, of which waited for: 2 -> 2; matrix products, arithmetic and copies ran while one was open for 0% -> 0% of each run, Pallas kernels for 11% -> 10%
where the time goes in v7:
time: 26.2 us; the launch traced here: 26 us
  blocking collectives  10.4 us (40%)
  starting transfers between devices  8.5 us (32%)
  Pallas kernels  5.21 us (20%)
  between operations  0.7 us (3%)
  waiting for transfers between devices  0.67 us (3%)
  local copies, waits for them, and re-layouts  0.47 us (2%)
    all_to_all x1, blocking collectives, on_device(): got = lax.all_to_all(sent, axes, 0, 0, tiled=True)  10.4 us
    pallas_call x9, Pallas kernels, call(): pl.pallas_call(kernel, out_shape=[jax.ShapeDtypeStruct(s, F32) for s in o...  5.21 us
    ppermute x1, starting transfers between devices, on_device(): first = lax.ppermute(pack, axes, g_one)  4.15 us
    ppermute x1, starting transfers between devices, on_device(): two = lax.ppermute(two, axes, b_two)  1.21 us
    ppermute x1, starting transfers between devices, on_device(): rest_two = lax.ppermute(rest_two, axes, b_two)  1.21 us
    ppermute x1, starting transfers between devices, on_device(): one = lax.ppermute(one, axes, b_one)  0.86 us
  transfers between devices with their start and end apart: 8, of which 2 were waited for; matrix products, arithmetic and copies ran while one was open for 0% of the time, Pallas kernels for 10%

profile of v7, /device:TPU:0, one launch (start us, length us, event | category | flops | bytes accessed | tf_op | source)
XLA Modules:
  0.0 26.0 jit_solution(12817472364001426870)
XLA Ops:
  0.6 1.5 %shard_map.59 = (f32[1152,128]{1,0:T(8,128)S(1)}, f32[80,128]{1,0:T(8,128)S(1)}, f32[48,128]{1,0:T(8,128)S(1)}) custom-call(f32[1152,128]{1,0:T(8,128)} %bitcast.8, s32[8,128]{1,0:T(8,128)} %mask_ref.5, f32[8,128]{1,0:T(8,128)} %height_hbm.1, f32[8,128]{1,0:T(8,128)} %damp_hbm.1), custom_call_target="tpu_custom_call" | custom-call | tf_op jit(solution)/shard_map/pallas_call | solution.py:554
  2.1 0.5 %collective-permute-start.1 = (f32[80,128]{1,0:T(8,128)S(1)}, f32[80,128]{1,0:T(8,128)S(1)}, u32[]{:S(2)}, u32[]{:S(2)}) collective-permute-start(f32[80,128]{1,0:T(8,128)S(1)} %get-tuple-element.23.pack_ref), channel_id=1, source_target_pairs={{0,4},{1,2},{2,1},{3,7},{4,0},{5,6},{6,5},{7,3},{8,12},{9,10},{10,... | collective-permute-start | bytes 122888 | tf_op jit(solution)/shard_map/ppermute | solution.py:591
  2.7 4.1 %collective-permute-start = (f32[80,128]{1,0:T(8,128)S(1)}, f32[80,128]{1,0:T(8,128)S(1)}, u32[]{:S(2)}, u32[]{:S(2)}) collective-permute-start(f32[80,128]{1,0:T(8,128)S(1)} %get-tuple-element.23.pack_ref), channel_id=1, source_target_pairs={{0,1},{1,0},{2,3},{3,2},{4,5},{5,4},{6,7},{7,6},{8,9},{9,8},{10,11... | collective-permute-start | bytes 122888 | tf_op jit(solution)/shard_map/ppermute | solution.py:590
  6.8 0.0 copy-start
  6.9 0.1 collective-permute-start.2
  7.0 0.1 collective-permute-start.3
  7.0 0.5 %copy-done = s32[8,128]{1,0:T(8,128)S(1)} copy-done((s32[8,128]{1,0:T(8,128)S(1)}, s32[8,128]{1,0:T(8,128)}, u32[]{:S(2)}) %copy-start) | copy-done | bytes 4120
  7.5 1.0 %shard_map.60 = (f32[1152,128]{1,0:T(8,128)S(1)}, f32[8,128]{1,0:T(8,128)S(1)}) custom-call(f32[1152,128]{1,0:T(8,128)S(1)} %get-tuple-element.24.m_ref, s32[8,128]{1,0:T(8,128)S(1)} %copy-done), custom_call_target="tpu_custom_call" | custom-call | flops 1000000000 | tf_op jit(solution)/shard_map/pallas_call | solution.py:554
  8.5 0.0 collective-permute-done.1.second_ref
  8.5 0.3 %collective-permute-done.first_ref = f32[80,128]{1,0:T(8,128)S(1)} collective-permute-done((f32[80,128]{1,0:T(8,128)S(1)}, f32[80,128]{1,0:T(8,128)S(1)}, u32[]{:S(2)}, u32[]{:S(2)}) %collective-permute-start) | collective-permute-done | bytes 40992 | tf_op jit(solution)/shard_map/ppermute | solution.py:590
  8.8 0.4 %shard_map.61 = (f32[16,128]{1,0:T(8,128)S(1)}, f32[32,128]{1,0:T(8,128)S(1)}, f32[72,128]{1,0:T(8,128)S(1)}, f32[32,128]{1,0:T(8,128)S(1)}, f32[32,128]{1,0:T(8,128)S(1)}) custom-call(f32[80,128]{1,0:T(8,128)S(1)} %get-tuple-element.23.pack_ref, f32[80,128]{1,0:T(8,128)S(1)} %collective-permute-done.first_ref, ...), custom_call_target="tpu_custom_call" | custom-call | flops 10000000000 | tf_op jit(solution)/shard_map/pallas_call | solution.py:554
  9.2 0.9 %collective-permute-start.4 = (f32[32,128]{1,0:T(8,128)S(1)}, f32[32,128]{1,0:T(8,128)S(1)}, u32[]{:S(2)}, u32[]{:S(2)}) collective-permute-start(f32[32,128]{1,0:T(8,128)S(1)} %get-tuple-element.30), channel_id=1, source_target_pairs={{0,4},{1,5},{2,6},{3,7},{4,0},{5,1},{6,2},{7,3},{8,12},{9,13},{10,... | collective-permute-start | bytes 49160 | tf_op jit(solution)/shard_map/ppermute | solution.py:606
  10.0 1.2 %collective-permute-start.5 = (f32[32,128]{1,0:T(8,128)S(1)}, f32[32,128]{1,0:T(8,128)S(1)}, u32[]{:S(2)}, u32[]{:S(2)}) collective-permute-start(f32[32,128]{1,0:T(8,128)S(1)} %get-tuple-element.31), channel_id=1, source_target_pairs={{0,1},{1,0},{2,3},{3,2},{4,8},{5,9},{6,10},{7,11},{8,4},{9,5},{10,... | collective-permute-start | bytes 49160 | tf_op jit(solution)/shard_map/ppermute | solution.py:607
  11.2 0.0 collective-permute-done.2.one_ref.flow_one_ref
  11.2 0.0 collective-permute-done.3.two_ref.flow_two_ref
  11.3 0.1 shard_map.63.cross_ref.after_ref
  11.3 0.1 shard_map.66
  11.4 0.4 %collective-permute-start.6 = (f32[304,128]{1,0:T(8,128)S(1)}, f32[304,128]{1,0:T(8,128)S(1)}, u32[]{:S(2)}, u32[]{:S(2)}) collective-permute-start(f32[304,128]{1,0:T(8,128)S(1)} %get-tuple-element.37), channel_id=1, source_target_pairs={{0,4},{1,5},{2,6},{3,7},{4,0},{5,1},{6,2},{7,3},{8,12},{9,13},{10,... | collective-permute-start | bytes 466952 | tf_op jit(solution)/shard_map/ppermute | solution.py:611
  11.9 1.2 %collective-permute-start.7 = (f32[304,128]{1,0:T(8,128)S(1)}, f32[304,128]{1,0:T(8,128)S(1)}, u32[]{:S(2)}, u32[]{:S(2)}) collective-permute-start(f32[304,128]{1,0:T(8,128)S(1)} %get-tuple-element.38), channel_id=1, source_target_pairs={{0,1},{1,0},{2,3},{3,2},{4,8},{5,9},{6,10},{7,11},{8,4},{9,5},{10,... | collective-permute-start | bytes 466952 | tf_op jit(solution)/shard_map/ppermute | solution.py:612
  13.1 0.4 %shard_map.64 = (f32[1152,128]{1,0:T(8,128)S(1)}, f32[8,128]{1,0:T(8,128)S(1)}) custom-call(f32[80,128]{1,0:T(8,128)S(1)} %get-tuple-element.23.pack_ref, f32[72,128]{1,0:T(8,128)S(1)} %get-tuple-element.32.delta_ref, s32[8,128]{1,0:T(8,128)S(1)} %copy-done, f32[1152,128]{1,0:T(8,128)S(1)} %get-tuple-element.33.state_in), custom_call_target="tpu_custom_call", output_to_operand_aliasing={{0}: (3, {})} | custom-call | flops 1000000000 | tf_op jit(solution)/shard_map/pallas_call | solution.py:554
  13.4 0.0 collective-permute-done.4.one_ref
  13.4 0.3 %collective-permute-done.5.two_ref = f32[32,128]{1,0:T(8,128)S(1)} collective-permute-done((f32[32,128]{1,0:T(8,128)S(1)}, f32[32,128]{1,0:T(8,128)S(1)}, u32[]{:S(2)}, u32[]{:S(2)}) %collective-permute-start.5) | collective-permute-done | bytes 16416 | tf_op jit(solution)/shard_map/ppermute | solution.py:607
  13.8 0.7 %shard_map.65 = (f32[24,128]{1,0:T(8,128)S(1)}, f32[32,128]{1,0:T(8,128)S(1)}) custom-call(f32[48,128]{1,0:T(8,128)S(1)} %get-tuple-element.22.flat_ref, f32[16,128]{1,0:T(8,128)S(1)} %get-tuple-element.26.own_ref, f32[32,128]{1,0:T(8,128)S(1)} %get-tuple-element.27.near_ref, f32[8,128]{1,0:T(8,128)S(1)} %shard_map.63.cross_ref.after_ref, ...), custom_call_target="tpu_custom_call" | custom-call | flops 1000000000 | tf_op jit(solution)/shard_map/pallas_call | solution.py:554
  14.4 10.4 %all_to_all.11 = f32[32,1,128]{2,1,0:T(1,128)S(1)} all-to-all(f32[32,1,128]{2,1,0:T(1,128)S(1)} %bitcast.7), channel_id=1, replica_groups=mesh['blocks'=8,'group'=4] {'blocks','group'}, dimensions={0} | all-to-all | bytes 32768 | tf_op jit(solution)/shard_map/all_to_all | solution.py:628
  24.9 0.0 collective-permute-done.6.one_ref
  24.9 0.0 collective-permute-done.7.two_ref
  24.9 1.1 %shard_map.67 = (f32[1152,128]{1,0:T(8,128)S(1)}, f32[1152,128]{1,0:T(8,128)}, f32[8,128]{1,0:T(8,128)}) custom-call(f32[32,128]{1,0:T(8,128)S(1)} %bitcast.6, f32[24,128]{1,0:T(8,128)S(1)} %get-tuple-element.36.basis_ref, f32[1152,128]{1,0:T(8,128)S(1)} %get-tuple-element.24.m_ref, ...), custom_call_target="tpu_custom_call", output_to_operand_aliasing={{0}: (6, {})} | custom-call | tf_op jit(solution)/shard_map/pallas_call | solution.py:554
  (1 shorter events, 0.0 us)
Async XLA Ops:
  2.1 6.3 %collective-permute-start.1 = (f32[80,128]{1,0:T(8,128)S(1)}, f32[80,128]{1,0:T(8,128)S(1)}, u32[]{:S(2)}, u32[]{:S(2)}) collective-permute-start(f32[80,128]{1,0:T(8,128)S(1)} %get-tuple-element.23.pack_ref), channel_id=1, source_target_pairs={{0,4},{1,2},{2,1},{3,7},{4,0},{5,6},{6,5},{7,3},{8,12},{9,10},{10,... | collective-permute-start | bytes 122888 | tf_op jit(solution)/shard_map/ppermute | solution.py:591
  2.7 6.1 %collective-permute-start = (f32[80,128]{1,0:T(8,128)S(1)}, f32[80,128]{1,0:T(8,128)S(1)}, u32[]{:S(2)}, u32[]{:S(2)}) collective-permute-start(f32[80,128]{1,0:T(8,128)S(1)} %get-tuple-element.23.pack_ref), channel_id=1, source_target_pairs={{0,1},{1,0},{2,3},{3,2},{4,5},{5,4},{6,7},{7,6},{8,9},{9,8},{10,11... | collective-permute-start | bytes 122888 | tf_op jit(solution)/shard_map/ppermute | solution.py:590
  6.8 0.7 %copy-start = (s32[8,128]{1,0:T(8,128)S(1)}, s32[8,128]{1,0:T(8,128)}, u32[]{:S(2)}) copy-start(s32[8,128]{1,0:T(8,128)} %mask_ref.5) | copy-start | bytes 12292
  6.9 4.4 %collective-permute-start.2 = (f32[128,128]{1,0:T(8,128)S(1)}, f32[128,128]{1,0:T(8,128)S(1)}, u32[]{:S(2)}, u32[]{:S(2)}) collective-permute-start(f32[128,128]{1,0:T(8,128)S(1)} %get-tuple-element.28), channel_id=1, source_target_pairs={{0,4},{1,5},{2,6},{3,7},{4,0},{5,1},{6,2},{7,3},{8,12},{9,13},{10,... | collective-permute-start | bytes 196616 | tf_op jit(solution)/shard_map/ppermute | solution.py:593
  7.0 4.3 %collective-permute-start.3 = (f32[128,128]{1,0:T(8,128)S(1)}, f32[128,128]{1,0:T(8,128)S(1)}, u32[]{:S(2)}, u32[]{:S(2)}) collective-permute-start(f32[128,128]{1,0:T(8,128)S(1)} %get-tuple-element.29), channel_id=1, source_target_pairs={{0,1},{1,0},{2,3},{3,2},{4,8},{5,9},{6,10},{7,11},{8,4},{9,5},{10,... | collective-permute-start | bytes 196616 | tf_op jit(solution)/shard_map/ppermute | solution.py:594
  9.2 4.3 %collective-permute-start.4 = (f32[32,128]{1,0:T(8,128)S(1)}, f32[32,128]{1,0:T(8,128)S(1)}, u32[]{:S(2)}, u32[]{:S(2)}) collective-permute-start(f32[32,128]{1,0:T(8,128)S(1)} %get-tuple-element.30), channel_id=1, source_target_pairs={{0,4},{1,5},{2,6},{3,7},{4,0},{5,1},{6,2},{7,3},{8,12},{9,13},{10,... | collective-permute-start | bytes 49160 | tf_op jit(solution)/shard_map/ppermute | solution.py:606
  10.0 3.7 %collective-permute-start.5 = (f32[32,128]{1,0:T(8,128)S(1)}, f32[32,128]{1,0:T(8,128)S(1)}, u32[]{:S(2)}, u32[]{:S(2)}) collective-permute-start(f32[32,128]{1,0:T(8,128)S(1)} %get-tuple-element.31), channel_id=1, source_target_pairs={{0,1},{1,0},{2,3},{3,2},{4,8},{5,9},{6,10},{7,11},{8,4},{9,5},{10,... | collective-permute-start | bytes 49160 | tf_op jit(solution)/shard_map/ppermute | solution.py:607
  11.4 13.4 %collective-permute-start.6 = (f32[304,128]{1,0:T(8,128)S(1)}, f32[304,128]{1,0:T(8,128)S(1)}, u32[]{:S(2)}, u32[]{:S(2)}) collective-permute-start(f32[304,128]{1,0:T(8,128)S(1)} %get-tuple-element.37), channel_id=1, source_target_pairs={{0,4},{1,5},{2,6},{3,7},{4,0},{5,1},{6,2},{7,3},{8,12},{9,13},{10,... | collective-permute-start | bytes 466952 | tf_op jit(solution)/shard_map/ppermute | solution.py:611
  11.9 13.0 %collective-permute-start.7 = (f32[304,128]{1,0:T(8,128)S(1)}, f32[304,128]{1,0:T(8,128)S(1)}, u32[]{:S(2)}, u32[]{:S(2)}) collective-permute-start(f32[304,128]{1,0:T(8,128)S(1)} %get-tuple-element.38), channel_id=1, source_target_pairs={{0,1},{1,0},{2,3},{3,2},{4,8},{5,9},{6,10},{7,11},{8,4},{9,5},{10,... | collective-permute-start | bytes 466952 | tf_op jit(solution)/shard_map/ppermute | solution.py:612

commit v8 on v7

--- a/solution.py
+++ b/solution.py
@@ -24,6 +24,7 @@
 STRIP = 16
 LONG = 10**9
 SHIFT = 4.5
+PAIRS = [(i, j) for i in range(ITERS) for j in range(i, ITERS + 1)]
 F32 = jnp.float32
 VMEM = pl.BlockSpec(memory_space=pltpu.VMEM)
 HBM = pl.BlockSpec(memory_space=pltpu.HBM)
@@ -236,12 +237,10 @@
     lay = Layout(m_ref.shape[0] // ROWS)
     step = COMPS * ROWS
     parts = []
-    for start in range(0, lay.levels, ROWS):
-        count = min(ROWS, lay.levels - start)
-        x = m_ref[pl.ds(start * step + comp * ROWS + row, count, stride=step), :]
-        if count < ROWS:
-            x = jnp.concatenate([x, jnp.zeros((ROWS - count, LANES), F32)], axis=0)
-        parts.append(x)
+    for first in range(0, lay.levels, ROWS):
+        start = min(first, lay.levels - ROWS)
+        x = m_ref[pl.ds(start * step + comp * ROWS + row, ROWS, stride=step), :]
+        parts.append(jnp.where(iota(0) < first - start, 0.0, x))
     return parts
 
 
@@ -389,13 +388,22 @@
         x = v[-1]
         v.append(own_diagonal * x - sea * (both(x, 1, 0) + both(x, 1, 1)))
     v = [x[ROWS : 2 * ROWS, 0:LANES] for x in v]
+
+    def over_rows(x, y):
+        return jnp.sum(x * y, axis=0, keepdims=True)
+
+    norm, slope = [jnp.sum(over_rows(v[0], x), axis=1, keepdims=True) for x in v[:2]]
+    theta = jnp.where(norm > 0.0, slope / jnp.where(norm > 0.0, norm, 1.0), 0.0)
+    q = [v[0]] + [v[k] - theta * v[k - 1] for k in range(1, ITERS + 1)]
     for k in range(ITERS):
-        basis_ref[tile(k), :] = v[k]
-    line = jnp.zeros((ROWS, LANES), F32)
-    for k in range(2 * ITERS):
-        part = jnp.sum(v[k // 2] * v[k - k // 2], axis=0, keepdims=True)
-        line = jnp.where(row == k, part, line)
+        basis_ref[tile(k), :] = q[k]
+    basis_ref[tile(ITERS), :] = jnp.broadcast_to(theta, (ROWS, LANES))
+    row, lane = iota(0, 2 * ROWS), iota(1, 2 * ROWS)
+    line = jnp.zeros((2 * ROWS, LANES), F32)
+    for k, (i, j) in enumerate(PAIRS):
+        line = jnp.where(row == k, over_rows(q[i], q[j]), line)
     line = jnp.sum(line, axis=1, keepdims=True)
+    line = jnp.where(row == len(PAIRS), theta, line)
     line = jnp.sum(jnp.where(row == lane, line, 0.0), axis=0, keepdims=True)
     send_ref[...] = jnp.broadcast_to(line, send_ref.shape)
 
@@ -440,39 +448,53 @@
             writes.append(pltpu.make_async_copy(state_ref.at[part], state_hbm.at[part], sems.at[len(writes)]))
             writes[-1].start()
 
-    line = jnp.sum(got_ref[...], axis=0, keepdims=True)
-    lane = iota(1, 1)
-    moment = [jnp.sum(jnp.where(lane == k, line, 0.0), axis=1, keepdims=True) for k in range(2 * ITERS)]
+    got = got_ref[...]
+    gram = {pair: jnp.broadcast_to(got[:, k : k + 1], got.shape) for k, pair in enumerate(PAIRS)}
+    theta = jnp.broadcast_to(got[:, len(PAIRS) : len(PAIRS) + 1], got.shape)
+
+    def local(a, theta):
+        out = [a[-1]]
+        for x in a[-2::-1]:
+            out.insert(0, x + theta * out[0])
+        return out
 
     def dot(a, b):
         total = None
-        for k in range(len(a) + len(b) - 1):
-            weight = sum(a[n] * b[k - n] for n in range(len(a)) if 0 <= k - n < len(b))
-            total = weight * moment[k] if total is None else total + weight * moment[k]
-        return total
+        for i, x in enumerate(local(a, theta)):
+            part = None
+            for j, y in enumerate(local(b, theta)):
+                term = y * gram[min(i, j), max(i, j)]
+                part = term if part is None else part + term
+            total = x * part if total is None else total + x * part
+        return jnp.sum(total, axis=0, keepdims=True)
 
     def add(a, scale, b):
-        out = list(a) + [0.0] * (len(b) - len(a))
+        out = list(a) + [jnp.zeros_like(one)] * (len(b) - len(a))
         return [x + scale * b[n] if n < len(b) else x for n, x in enumerate(out)]
 
     def image(a):
-        return [SHIFT * (a[n] if n < len(a) else 0.0) + (a[n - 1] if n else 0.0) for n in range(len(a) + 1)]
-
-    one = jnp.ones((1, 1), F32)
+        return [SHIFT * a[0]] + [SHIFT * a[n] + a[n - 1] for n in range(1, len(a))] + [a[-1]]
+
+    one = jnp.ones((1, LANES), F32)
     residual, direction, surface = [one], [one], []
     norm = dot(residual, residual)
     for iteration in range(ITERS):
         applied = image(direction)
         alpha = norm / dot(direction, applied)
+        if iteration:
+            alpha = jnp.where(norm > 0.0, alpha, 0.0)
         surface = add(surface, alpha, direction)
         if iteration + 1 < ITERS:
             residual = add(residual, -alpha, applied)
             following = dot(residual, residual)
-            direction = add(residual, following / norm, direction)
+            ratio = following / norm
+            if iteration:
+                ratio = jnp.where(norm > 0.0, ratio, 0.0)
+            direction = add(residual, ratio, direction)
             norm = following
-    out = surface[0] * basis_ref[tile(0), :]
-    for k in range(1, ITERS):
-        out = out + surface[k] * basis_ref[tile(k), :]
+    out = jnp.zeros((ROWS, LANES), F32)
+    for k, x in enumerate(local(surface, basis_ref[tile(ITERS), :])):
+        out = out + x * basis_ref[tile(k), :]
     surface_ref[...] = out
     writes.append(pltpu.make_async_copy(surface_ref, surface_hbm, sems.at[len(writes)]))
     writes[-1].start()
@@ -612,7 +634,7 @@
     rest_two = lax.ppermute(rest_two, axes, b_two)
     basis, sent = call(
         functools.partial(moment_kernel, levels=lay.levels),
-        [(ITERS * ROWS, LANES), (nb * ng, LANES)],
+        [((ITERS + 1) * ROWS, LANES), (nb * ng, LANES)],
         flat,
         own,
         near,

time: 26.2 us -> 26.2 us (level)
  transfers between devices with their start and end apart: 8 -> 8, of which waited for: 2 -> 3; matrix products, arithmetic and copies ran while one was open for 0% -> 0% of each run, Pallas kernels for 10% -> 10%
where the time goes in v8:
time: 26.2 us; the launch traced here: 26 us
  blocking collectives  10.4 us (40%)
  starting transfers between devices  8.49 us (32%)
  Pallas kernels  5.22 us (20%)
  between operations  0.7 us (3%)
  waiting for transfers between devices  0.68 us (3%)
  local copies, waits for them, and re-layouts  0.46 us (2%)
    all_to_all x1, blocking collectives, on_device(): got = lax.all_to_all(sent, axes, 0, 0, tiled=True)  10.4 us
    pallas_call x9, Pallas kernels, call(): pl.pallas_call(kernel, out_shape=[jax.ShapeDtypeStruct(s, F32) for s in o...  5.22 us
    ppermute x1, starting transfers between devices, on_device(): first = lax.ppermute(pack, axes, g_one)  4.15 us
    ppermute x1, starting transfers between devices, on_device(): rest_two = lax.ppermute(rest_two, axes, b_two)  1.2 us
    ppermute x1, starting transfers between devices, on_device(): two = lax.ppermute(two, axes, b_two)  1.2 us
    ppermute x1, starting transfers between devices, on_device(): one = lax.ppermute(one, axes, b_one)  0.87 us
  transfers between devices with their start and end apart: 8, of which 3 were waited for; matrix products, arithmetic and copies ran while one was open for 0% of the time, Pallas kernels for 10%

profile of v8, /device:TPU:0, one launch (start us, length us, event | category | flops | bytes accessed | tf_op | source)
XLA Modules:
  0.0 26.0 jit_solution(7044993955468711626)
XLA Ops:
  0.6 1.5 %shard_map.59 = (f32[1152,128]{1,0:T(8,128)S(1)}, f32[80,128]{1,0:T(8,128)S(1)}, f32[48,128]{1,0:T(8,128)S(1)}) custom-call(f32[1152,128]{1,0:T(8,128)} %bitcast.8, s32[8,128]{1,0:T(8,128)} %mask_ref.5, f32[8,128]{1,0:T(8,128)} %height_hbm.1, f32[8,128]{1,0:T(8,128)} %damp_hbm.1), custom_call_target="tpu_custom_call" | custom-call | tf_op jit(solution)/shard_map/pallas_call | solution.py:576
  2.1 0.5 %collective-permute-start.1 = (f32[80,128]{1,0:T(8,128)S(1)}, f32[80,128]{1,0:T(8,128)S(1)}, u32[]{:S(2)}, u32[]{:S(2)}) collective-permute-start(f32[80,128]{1,0:T(8,128)S(1)} %get-tuple-element.23.pack_ref), channel_id=1, source_target_pairs={{0,4},{1,2},{2,1},{3,7},{4,0},{5,6},{6,5},{7,3},{8,12},{9,10},{10,... | collective-permute-start | bytes 122888 | tf_op jit(solution)/shard_map/ppermute | solution.py:613
  2.7 4.1 %collective-permute-start = (f32[80,128]{1,0:T(8,128)S(1)}, f32[80,128]{1,0:T(8,128)S(1)}, u32[]{:S(2)}, u32[]{:S(2)}) collective-permute-start(f32[80,128]{1,0:T(8,128)S(1)} %get-tuple-element.23.pack_ref), channel_id=1, source_target_pairs={{0,1},{1,0},{2,3},{3,2},{4,5},{5,4},{6,7},{7,6},{8,9},{9,8},{10,11... | collective-permute-start | bytes 122888 | tf_op jit(solution)/shard_map/ppermute | solution.py:612
  6.8 0.0 copy-start
  6.8 0.1 shard_map.62
  6.9 0.1 collective-permute-start.2
  7.0 0.1 collective-permute-start.3
  7.0 0.5 %copy-done = s32[8,128]{1,0:T(8,128)S(1)} copy-done((s32[8,128]{1,0:T(8,128)S(1)}, s32[8,128]{1,0:T(8,128)}, u32[]{:S(2)}) %copy-start) | copy-done | bytes 4120
  7.5 1.0 %shard_map.60 = (f32[1152,128]{1,0:T(8,128)S(1)}, f32[8,128]{1,0:T(8,128)S(1)}) custom-call(f32[1152,128]{1,0:T(8,128)S(1)} %get-tuple-element.24.m_ref, s32[8,128]{1,0:T(8,128)S(1)} %copy-done), custom_call_target="tpu_custom_call" | custom-call | flops 1000000000 | tf_op jit(solution)/shard_map/pallas_call | solution.py:576
  8.5 0.0 collective-permute-done.1.second_ref
  8.5 0.3 %collective-permute-done.first_ref = f32[80,128]{1,0:T(8,128)S(1)} collective-permute-done((f32[80,128]{1,0:T(8,128)S(1)}, f32[80,128]{1,0:T(8,128)S(1)}, u32[]{:S(2)}, u32[]{:S(2)}) %collective-permute-start) | collective-permute-done | bytes 40992 | tf_op jit(solution)/shard_map/ppermute | solution.py:612
  8.8 0.4 %shard_map.61 = (f32[16,128]{1,0:T(8,128)S(1)}, f32[32,128]{1,0:T(8,128)S(1)}, f32[72,128]{1,0:T(8,128)S(1)}, f32[32,128]{1,0:T(8,128)S(1)}, f32[32,128]{1,0:T(8,128)S(1)}) custom-call(f32[80,128]{1,0:T(8,128)S(1)} %get-tuple-element.23.pack_ref, f32[80,128]{1,0:T(8,128)S(1)} %collective-permute-done.first_ref, ...), custom_call_target="tpu_custom_call" | custom-call | flops 10000000000 | tf_op jit(solution)/shard_map/pallas_call | solution.py:576
  9.2 0.9 %collective-permute-start.4 = (f32[32,128]{1,0:T(8,128)S(1)}, f32[32,128]{1,0:T(8,128)S(1)}, u32[]{:S(2)}, u32[]{:S(2)}) collective-permute-start(f32[32,128]{1,0:T(8,128)S(1)} %get-tuple-element.30), channel_id=1, source_target_pairs={{0,4},{1,5},{2,6},{3,7},{4,0},{5,1},{6,2},{7,3},{8,12},{9,13},{10,... | collective-permute-start | bytes 49160 | tf_op jit(solution)/shard_map/ppermute | solution.py:628
  10.0 1.2 %collective-permute-start.5 = (f32[32,128]{1,0:T(8,128)S(1)}, f32[32,128]{1,0:T(8,128)S(1)}, u32[]{:S(2)}, u32[]{:S(2)}) collective-permute-start(f32[32,128]{1,0:T(8,128)S(1)} %get-tuple-element.31), channel_id=1, source_target_pairs={{0,1},{1,0},{2,3},{3,2},{4,8},{5,9},{6,10},{7,11},{8,4},{9,5},{10,... | collective-permute-start | bytes 49160 | tf_op jit(solution)/shard_map/ppermute | solution.py:629
  11.2 0.0 collective-permute-done.2.one_ref.flow_one_ref
  11.2 0.1 collective-permute-done.3.two_ref.flow_two_ref
  11.3 0.1 shard_map.63.cross_ref.after_ref
  11.4 0.1 shard_map.66
  11.4 0.4 %collective-permute-start.6 = (f32[304,128]{1,0:T(8,128)S(1)}, f32[304,128]{1,0:T(8,128)S(1)}, u32[]{:S(2)}, u32[]{:S(2)}) collective-permute-start(f32[304,128]{1,0:T(8,128)S(1)} %get-tuple-element.37), channel_id=1, source_target_pairs={{0,4},{1,5},{2,6},{3,7},{4,0},{5,1},{6,2},{7,3},{8,12},{9,13},{10,... | collective-permute-start | bytes 466952 | tf_op jit(solution)/shard_map/ppermute | solution.py:633
  11.9 1.2 %collective-permute-start.7 = (f32[304,128]{1,0:T(8,128)S(1)}, f32[304,128]{1,0:T(8,128)S(1)}, u32[]{:S(2)}, u32[]{:S(2)}) collective-permute-start(f32[304,128]{1,0:T(8,128)S(1)} %get-tuple-element.38), channel_id=1, source_target_pairs={{0,1},{1,0},{2,3},{3,2},{4,8},{5,9},{6,10},{7,11},{8,4},{9,5},{10,... | collective-permute-start | bytes 466952 | tf_op jit(solution)/shard_map/ppermute | solution.py:634
  13.1 0.4 %shard_map.64 = (f32[1152,128]{1,0:T(8,128)S(1)}, f32[8,128]{1,0:T(8,128)S(1)}) custom-call(f32[80,128]{1,0:T(8,128)S(1)} %get-tuple-element.23.pack_ref, f32[72,128]{1,0:T(8,128)S(1)} %get-tuple-element.32.delta_ref, s32[8,128]{1,0:T(8,128)S(1)} %copy-done, f32[1152,128]{1,0:T(8,128)S(1)} %get-tuple-element.33.state_in), custom_call_target="tpu_custom_call", output_to_operand_aliasing={{0}: (3, {})} | custom-call | flops 1000000000 | tf_op jit(solution)/shard_map/pallas_call | solution.py:576
  13.4 0.0 collective-permute-done.4.one_ref
  13.4 0.3 %collective-permute-done.5.two_ref = f32[32,128]{1,0:T(8,128)S(1)} collective-permute-done((f32[32,128]{1,0:T(8,128)S(1)}, f32[32,128]{1,0:T(8,128)S(1)}, u32[]{:S(2)}, u32[]{:S(2)}) %collective-permute-start.5) | collective-permute-done | bytes 16416 | tf_op jit(solution)/shard_map/ppermute | solution.py:629
  13.8 0.7 %shard_map.65 = (f32[32,128]{1,0:T(8,128)S(1)}, f32[32,128]{1,0:T(8,128)S(1)}) custom-call(f32[48,128]{1,0:T(8,128)S(1)} %get-tuple-element.22.flat_ref, f32[16,128]{1,0:T(8,128)S(1)} %get-tuple-element.26.own_ref, f32[32,128]{1,0:T(8,128)S(1)} %get-tuple-element.27.near_ref, f32[8,128]{1,0:T(8,128)S(1)} %shard_map.63.cross_ref.after_ref, ...), custom_call_target="tpu_custom_call" | custom-call | flops 1000000000 | tf_op jit(solution)/shard_map/pallas_call | solution.py:576
  14.5 10.4 %all_to_all.11 = f32[32,1,128]{2,1,0:T(1,128)S(1)} all-to-all(f32[32,1,128]{2,1,0:T(1,128)S(1)} %bitcast.7), channel_id=1, replica_groups=mesh['blocks'=8,'group'=4] {'blocks','group'}, dimensions={0} | all-to-all | bytes 32768 | tf_op jit(solution)/shard_map/all_to_all | solution.py:650
  24.9 0.0 collective-permute-done.6.one_ref
  24.9 0.0 collective-permute-done.7.two_ref
  24.9 1.1 %shard_map.67 = (f32[1152,128]{1,0:T(8,128)S(1)}, f32[1152,128]{1,0:T(8,128)}, f32[8,128]{1,0:T(8,128)}) custom-call(f32[32,128]{1,0:T(8,128)S(1)} %bitcast.6, f32[32,128]{1,0:T(8,128)S(1)} %get-tuple-element.36.basis_ref, f32[1152,128]{1,0:T(8,128)S(1)} %get-tuple-element.24.m_ref, ...), custom_call_target="tpu_custom_call", output_to_operand_aliasing={{0}: (6, {})} | custom-call | tf_op jit(solution)/shard_map/pallas_call | solution.py:576
Async XLA Ops:
  2.1 6.3 %collective-permute-start.1 = (f32[80,128]{1,0:T(8,128)S(1)}, f32[80,128]{1,0:T(8,128)S(1)}, u32[]{:S(2)}, u32[]{:S(2)}) collective-permute-start(f32[80,128]{1,0:T(8,128)S(1)} %get-tuple-element.23.pack_ref), channel_id=1, source_target_pairs={{0,4},{1,2},{2,1},{3,7},{4,0},{5,6},{6,5},{7,3},{8,12},{9,10},{10,... | collective-permute-start | bytes 122888 | tf_op jit(solution)/shard_map/ppermute | solution.py:613
  2.7 6.1 %collective-permute-start = (f32[80,128]{1,0:T(8,128)S(1)}, f32[80,128]{1,0:T(8,128)S(1)}, u32[]{:S(2)}, u32[]{:S(2)}) collective-permute-start(f32[80,128]{1,0:T(8,128)S(1)} %get-tuple-element.23.pack_ref), channel_id=1, source_target_pairs={{0,1},{1,0},{2,3},{3,2},{4,5},{5,4},{6,7},{7,6},{8,9},{9,8},{10,11... | collective-permute-start | bytes 122888 | tf_op jit(solution)/shard_map/ppermute | solution.py:612
  6.8 0.7 %copy-start = (s32[8,128]{1,0:T(8,128)S(1)}, s32[8,128]{1,0:T(8,128)}, u32[]{:S(2)}) copy-start(s32[8,128]{1,0:T(8,128)} %mask_ref.5) | copy-start | bytes 12292
  6.9 4.4 %collective-permute-start.2 = (f32[128,128]{1,0:T(8,128)S(1)}, f32[128,128]{1,0:T(8,128)S(1)}, u32[]{:S(2)}, u32[]{:S(2)}) collective-permute-start(f32[128,128]{1,0:T(8,128)S(1)} %get-tuple-element.28), channel_id=1, source_target_pairs={{0,4},{1,5},{2,6},{3,7},{4,0},{5,1},{6,2},{7,3},{8,12},{9,13},{10,... | collective-permute-start | bytes 196616 | tf_op jit(solution)/shard_map/ppermute | solution.py:615
  7.0 4.3 %collective-permute-start.3 = (f32[128,128]{1,0:T(8,128)S(1)}, f32[128,128]{1,0:T(8,128)S(1)}, u32[]{:S(2)}, u32[]{:S(2)}) collective-permute-start(f32[128,128]{1,0:T(8,128)S(1)} %get-tuple-element.29), channel_id=1, source_target_pairs={{0,1},{1,0},{2,3},{3,2},{4,8},{5,9},{6,10},{7,11},{8,4},{9,5},{10,... | collective-permute-start | bytes 196616 | tf_op jit(solution)/shard_map/ppermute | solution.py:616
  9.2 4.3 %collective-permute-start.4 = (f32[32,128]{1,0:T(8,128)S(1)}, f32[32,128]{1,0:T(8,128)S(1)}, u32[]{:S(2)}, u32[]{:S(2)}) collective-permute-start(f32[32,128]{1,0:T(8,128)S(1)} %get-tuple-element.30), channel_id=1, source_target_pairs={{0,4},{1,5},{2,6},{3,7},{4,0},{5,1},{6,2},{7,3},{8,12},{9,13},{10,... | collective-permute-start | bytes 49160 | tf_op jit(solution)/shard_map/ppermute | solution.py:628
  10.0 3.7 %collective-permute-start.5 = (f32[32,128]{1,0:T(8,128)S(1)}, f32[32,128]{1,0:T(8,128)S(1)}, u32[]{:S(2)}, u32[]{:S(2)}) collective-permute-start(f32[32,128]{1,0:T(8,128)S(1)} %get-tuple-element.31), channel_id=1, source_target_pairs={{0,1},{1,0},{2,3},{3,2},{4,8},{5,9},{6,10},{7,11},{8,4},{9,5},{10,... | collective-permute-start | bytes 49160 | tf_op jit(solution)/shard_map/ppermute | solution.py:629
  11.4 13.4 %collective-permute-start.6 = (f32[304,128]{1,0:T(8,128)S(1)}, f32[304,128]{1,0:T(8,128)S(1)}, u32[]{:S(2)}, u32[]{:S(2)}) collective-permute-start(f32[304,128]{1,0:T(8,128)S(1)} %get-tuple-element.37), channel_id=1, source_target_pairs={{0,4},{1,5},{2,6},{3,7},{4,0},{5,1},{6,2},{7,3},{8,12},{9,13},{10,... | collective-permute-start | bytes 466952 | tf_op jit(solution)/shard_map/ppermute | solution.py:633
  11.9 13.0 %collective-permute-start.7 = (f32[304,128]{1,0:T(8,128)S(1)}, f32[304,128]{1,0:T(8,128)S(1)}, u32[]{:S(2)}, u32[]{:S(2)}) collective-permute-start(f32[304,128]{1,0:T(8,128)S(1)} %get-tuple-element.38), channel_id=1, source_target_pairs={{0,1},{1,0},{2,3},{3,2},{4,8},{5,9},{6,10},{7,11},{8,4},{9,5},{10,... | collective-permute-start | bytes 466952 | tf_op jit(solution)/shard_map/ppermute | solution.py:634

commit v9 on v8

--- a/solution.py
+++ b/solution.py
@@ -409,7 +409,7 @@
 
 
 def solve_kernel(
-    got_ref, basis_ref, m_ref, one_ref, two_ref, mask_ref, state_in, state_ref, state_hbm, surface_hbm, surface_ref, sems
+    got_ref, basis_ref, m_ref, one_ref, two_ref, mask_ref, part_ref, state_hbm, surface_hbm, state_ref, surface_ref, sems
 ):
     lay = Layout(state_ref.shape[0] // ROWS)
     at = Place()
@@ -424,6 +424,8 @@
     fixes = [jnp.where(near, x, 0.0) for x in fixes]
     writes = []
     for s in range(lay.eights):
+        group = pl.ds(ROWS * ROWS * s, ROWS * ROWS)
+        state_ref[group, :] = part_ref[group, :]
         for (take, first, second, row, inner, slope), fix in zip(sides, fixes):
             x1, x2 = [take(one_ref[w, :], two_ref[w, :]) for w in (tile(n * lay.eights + s) for n in (first, second))]
             flow = m_ref[pl.ds(ROWS * ROWS * s + row, ROWS, stride=ROWS), :]
@@ -547,7 +549,7 @@
             new_ref[tile(t), :] = sea * out
 
 
-def border_kernel(pack_ref, delta_ref, mask_ref, state_in, state_ref, done_ref):
+def border_kernel(pack_ref, delta_ref, mask_ref, part_ref, state_ref, done_ref):
     lay = Layout(state_ref.shape[0] // ROWS)
     lane = iota(1)
     border = (lane < SLOT // 2) | (lane >= LANES - SLOT // 2)
@@ -569,17 +571,16 @@
     )
     for t in range(lay.tiles):
         p = t // PER
-        state_ref[tile(t), :] = state_ref[tile(t), :] + sea * unpack(fix[p * ROWS : (p + 1) * ROWS], t)
-
-
-def call(kernel, outs, *args, scratch=(), specs=None, out_specs=None, aliases=None, flops=0):
+        state_ref[tile(t), :] = part_ref[tile(t), :] + sea * unpack(fix[p * ROWS : (p + 1) * ROWS], t)
+
+
+def call(kernel, outs, *args, scratch=(), specs=None, out_specs=None, flops=0):
     return pl.pallas_call(
         kernel,
         out_shape=[jax.ShapeDtypeStruct(s, F32) for s in outs],
         in_specs=specs or [VMEM] * len(args),
         out_specs=out_specs or [VMEM] * len(outs),
         scratch_shapes=[pltpu.VMEM(s, F32) if isinstance(s, tuple) else s for s in scratch],
-        input_output_aliases=aliases or {},
         compiler_params=pltpu.CompilerParams(vmem_limit_bytes=8 * 1024 * 1024),
         cost_estimate=pl.CostEstimate(flops=flops, bytes_accessed=0, transcendentals=0),
     )(*args)
@@ -628,7 +629,7 @@
     one = lax.ppermute(one, axes, b_one)
     two = lax.ppermute(two, axes, b_two)
     (cross,) = call(cross_kernel, [one_tile], m, flow_one, flow_two)
-    part, done = call(border_kernel, [state.shape, one_tile], pack, delta, land_mask, part, aliases={3: 0}, flops=LONG)
+    part, done = call(border_kernel, [state.shape, one_tile], pack, delta, land_mask, part, flops=LONG)
     rest_one, rest_two = call(rest_kernel, [(lay.rest, LANES)] * 2, m, delta, cross)
     rest_one = lax.ppermute(rest_one, axes, b_one)
     rest_two = lax.ppermute(rest_two, axes, b_two)
@@ -648,9 +649,9 @@
         flops=LONG,
     )
     got = lax.all_to_all(sent, axes, 0, 0, tiled=True)
-    _, new_state, surface = call(
+    new_state, surface = call(
         solve_kernel,
-        [state.shape, state.shape, one_tile],
+        [state.shape, one_tile],
         got,
         basis,
         m,
@@ -658,9 +659,8 @@
         rest_two,
         land_mask,
         part,
-        scratch=[one_tile, pltpu.SemaphoreType.DMA((3,))],
-        out_specs=[VMEM, HBM, HBM],
-        aliases={6: 0},
+        scratch=[state.shape, one_tile, pltpu.SemaphoreType.DMA((3,))],
+        out_specs=[HBM, HBM],
     )
     return new_state.reshape(ocean_state.shape), surface
 

time: 26.2 us -> 26.2 us (level)
  no operation moved by 1% of the time
where the time goes in v9:
time: 26.2 us; the launch traced here: 26 us
  blocking collectives  10.4 us (40%)
  starting transfers between devices  8.49 us (32%)
  Pallas kernels  5.25 us (20%)
  between operations  0.7 us (3%)
  waiting for transfers between devices  0.69 us (3%)
  local copies, waits for them, and re-layouts  0.46 us (2%)
    all_to_all x1, blocking collectives, on_device(): got = lax.all_to_all(sent, axes, 0, 0, tiled=True)  10.4 us
    pallas_call x9, Pallas kernels, call(): pl.pallas_call(kernel, out_shape=[jax.ShapeDtypeStruct(s, F32) for s in o...  5.25 us
    ppermute x1, starting transfers between devices, on_device(): first = lax.ppermute(pack, axes, g_one)  4.15 us
    ppermute x1, starting transfers between devices, on_device(): two = lax.ppermute(two, axes, b_two)  1.19 us
    ppermute x1, starting transfers between devices, on_device(): rest_two = lax.ppermute(rest_two, axes, b_two)  1.19 us
    ppermute x1, starting transfers between devices, on_device(): one = lax.ppermute(one, axes, b_one)  0.87 us
  transfers between devices with their start and end apart: 8, of which 3 were waited for; matrix products, arithmetic and copies ran while one was open for 0% of the time, Pallas kernels for 10%

profile of v9, /device:TPU:0, one launch (start us, length us, event | category | flops | bytes accessed | tf_op | source)
XLA Modules:
  0.0 26.0 jit_solution(14838762466213057314)
XLA Ops:
  0.6 1.5 %shard_map.59 = (f32[1152,128]{1,0:T(8,128)S(1)}, f32[80,128]{1,0:T(8,128)S(1)}, f32[48,128]{1,0:T(8,128)S(1)}) custom-call(f32[1152,128]{1,0:T(8,128)} %bitcast.8, s32[8,128]{1,0:T(8,128)} %mask_ref.5, f32[8,128]{1,0:T(8,128)} %height_hbm.1, f32[8,128]{1,0:T(8,128)} %damp_hbm.1), custom_call_target="tpu_custom_call" | custom-call | tf_op jit(solution)/shard_map/pallas_call | solution.py:578
  2.1 0.5 %collective-permute-start.1 = (f32[80,128]{1,0:T(8,128)S(1)}, f32[80,128]{1,0:T(8,128)S(1)}, u32[]{:S(2)}, u32[]{:S(2)}) collective-permute-start(f32[80,128]{1,0:T(8,128)S(1)} %get-tuple-element.23.pack_ref), channel_id=1, source_target_pairs={{0,4},{1,2},{2,1},{3,7},{4,0},{5,6},{6,5},{7,3},{8,12},{9,10},{10,... | collective-permute-start | bytes 122888 | tf_op jit(solution)/shard_map/ppermute | solution.py:614
  2.7 4.1 %collective-permute-start = (f32[80,128]{1,0:T(8,128)S(1)}, f32[80,128]{1,0:T(8,128)S(1)}, u32[]{:S(2)}, u32[]{:S(2)}) collective-permute-start(f32[80,128]{1,0:T(8,128)S(1)} %get-tuple-element.23.pack_ref), channel_id=1, source_target_pairs={{0,1},{1,0},{2,3},{3,2},{4,5},{5,4},{6,7},{7,6},{8,9},{9,8},{10,11... | collective-permute-start | bytes 122888 | tf_op jit(solution)/shard_map/ppermute | solution.py:613
  6.8 0.0 copy-start
  6.8 0.1 shard_map.62
  6.9 0.1 collective-permute-start.2
  7.0 0.1 collective-permute-start.3
  7.0 0.5 %copy-done = s32[8,128]{1,0:T(8,128)S(1)} copy-done((s32[8,128]{1,0:T(8,128)S(1)}, s32[8,128]{1,0:T(8,128)}, u32[]{:S(2)}) %copy-start) | copy-done | bytes 4120
  7.5 1.0 %shard_map.60 = (f32[1152,128]{1,0:T(8,128)S(1)}, f32[8,128]{1,0:T(8,128)S(1)}) custom-call(f32[1152,128]{1,0:T(8,128)S(1)} %get-tuple-element.24.m_ref, s32[8,128]{1,0:T(8,128)S(1)} %copy-done), custom_call_target="tpu_custom_call" | custom-call | flops 1000000000 | tf_op jit(solution)/shard_map/pallas_call | solution.py:578
  8.5 0.0 collective-permute-done.1.second_ref
  8.5 0.3 %collective-permute-done.first_ref = f32[80,128]{1,0:T(8,128)S(1)} collective-permute-done((f32[80,128]{1,0:T(8,128)S(1)}, f32[80,128]{1,0:T(8,128)S(1)}, u32[]{:S(2)}, u32[]{:S(2)}) %collective-permute-start) | collective-permute-done | bytes 40992 | tf_op jit(solution)/shard_map/ppermute | solution.py:613
  8.8 0.4 %shard_map.61 = (f32[16,128]{1,0:T(8,128)S(1)}, f32[32,128]{1,0:T(8,128)S(1)}, f32[72,128]{1,0:T(8,128)S(1)}, f32[32,128]{1,0:T(8,128)S(1)}, f32[32,128]{1,0:T(8,128)S(1)}) custom-call(f32[80,128]{1,0:T(8,128)S(1)} %get-tuple-element.23.pack_ref, f32[80,128]{1,0:T(8,128)S(1)} %collective-permute-done.first_ref, ...), custom_call_target="tpu_custom_call" | custom-call | flops 10000000000 | tf_op jit(solution)/shard_map/pallas_call | solution.py:578
  9.2 0.9 %collective-permute-start.4 = (f32[32,128]{1,0:T(8,128)S(1)}, f32[32,128]{1,0:T(8,128)S(1)}, u32[]{:S(2)}, u32[]{:S(2)}) collective-permute-start(f32[32,128]{1,0:T(8,128)S(1)} %get-tuple-element.30), channel_id=1, source_target_pairs={{0,4},{1,5},{2,6},{3,7},{4,0},{5,1},{6,2},{7,3},{8,12},{9,13},{10,... | collective-permute-start | bytes 49160 | tf_op jit(solution)/shard_map/ppermute | solution.py:629
  10.0 1.2 %collective-permute-start.5 = (f32[32,128]{1,0:T(8,128)S(1)}, f32[32,128]{1,0:T(8,128)S(1)}, u32[]{:S(2)}, u32[]{:S(2)}) collective-permute-start(f32[32,128]{1,0:T(8,128)S(1)} %get-tuple-element.31), channel_id=1, source_target_pairs={{0,1},{1,0},{2,3},{3,2},{4,8},{5,9},{6,10},{7,11},{8,4},{9,5},{10,... | collective-permute-start | bytes 49160 | tf_op jit(solution)/shard_map/ppermute | solution.py:630
  11.2 0.0 collective-permute-done.2.one_ref.flow_one_ref
  11.2 0.1 collective-permute-done.3.two_ref.flow_two_ref
  11.3 0.1 shard_map.63.cross_ref.after_ref
  11.4 0.1 shard_map.66
  11.4 0.4 %collective-permute-start.6 = (f32[304,128]{1,0:T(8,128)S(1)}, f32[304,128]{1,0:T(8,128)S(1)}, u32[]{:S(2)}, u32[]{:S(2)}) collective-permute-start(f32[304,128]{1,0:T(8,128)S(1)} %get-tuple-element.37), channel_id=1, source_target_pairs={{0,4},{1,5},{2,6},{3,7},{4,0},{5,1},{6,2},{7,3},{8,12},{9,13},{10,... | collective-permute-start | bytes 466952 | tf_op jit(solution)/shard_map/ppermute | solution.py:634
  11.9 1.2 %collective-permute-start.7 = (f32[304,128]{1,0:T(8,128)S(1)}, f32[304,128]{1,0:T(8,128)S(1)}, u32[]{:S(2)}, u32[]{:S(2)}) collective-permute-start(f32[304,128]{1,0:T(8,128)S(1)} %get-tuple-element.38), channel_id=1, source_target_pairs={{0,1},{1,0},{2,3},{3,2},{4,8},{5,9},{6,10},{7,11},{8,4},{9,5},{10,... | collective-permute-start | bytes 466952 | tf_op jit(solution)/shard_map/ppermute | solution.py:635
  13.1 0.4 %shard_map.64 = (f32[1152,128]{1,0:T(8,128)S(1)}, f32[8,128]{1,0:T(8,128)S(1)}) custom-call(f32[80,128]{1,0:T(8,128)S(1)} %get-tuple-element.23.pack_ref, f32[72,128]{1,0:T(8,128)S(1)} %get-tuple-element.32.delta_ref, s32[8,128]{1,0:T(8,128)S(1)} %copy-done, f32[1152,128]{1,0:T(8,128)S(1)} %get-tuple-element.33.part_ref), custom_call_target="tpu_custom_call" | custom-call | flops 1000000000 | tf_op jit(solution)/shard_map/pallas_call | solution.py:578
  13.4 0.0 collective-permute-done.4.one_ref
  13.4 0.3 %collective-permute-done.5.two_ref = f32[32,128]{1,0:T(8,128)S(1)} collective-permute-done((f32[32,128]{1,0:T(8,128)S(1)}, f32[32,128]{1,0:T(8,128)S(1)}, u32[]{:S(2)}, u32[]{:S(2)}) %collective-permute-start.5) | collective-permute-done | bytes 16416 | tf_op jit(solution)/shard_map/ppermute | solution.py:630
  13.8 0.7 %shard_map.65 = (f32[32,128]{1,0:T(8,128)S(1)}, f32[32,128]{1,0:T(8,128)S(1)}) custom-call(f32[48,128]{1,0:T(8,128)S(1)} %get-tuple-element.22.flat_ref, f32[16,128]{1,0:T(8,128)S(1)} %get-tuple-element.26.own_ref, f32[32,128]{1,0:T(8,128)S(1)} %get-tuple-element.27.near_ref, f32[8,128]{1,0:T(8,128)S(1)} %shard_map.63.cross_ref.after_ref, ...), custom_call_target="tpu_custom_call" | custom-call | flops 1000000000 | tf_op jit(solution)/shard_map/pallas_call | solution.py:578
  14.5 10.4 %all_to_all.11 = f32[32,1,128]{2,1,0:T(1,128)S(1)} all-to-all(f32[32,1,128]{2,1,0:T(1,128)S(1)} %bitcast.7), channel_id=1, replica_groups=mesh['blocks'=8,'group'=4] {'blocks','group'}, dimensions={0} | all-to-all | bytes 32768 | tf_op jit(solution)/shard_map/all_to_all | solution.py:651
  24.9 0.0 collective-permute-done.6.one_ref
  24.9 0.0 collective-permute-done.7.two_ref
  24.9 1.1 %shard_map.67 = (f32[1152,128]{1,0:T(8,128)}, f32[8,128]{1,0:T(8,128)}) custom-call(f32[32,128]{1,0:T(8,128)S(1)} %bitcast.6, f32[32,128]{1,0:T(8,128)S(1)} %get-tuple-element.36.basis_ref, f32[1152,128]{1,0:T(8,128)S(1)} %get-tuple-element.24.m_ref, f32[304,128]{1,0:T(8,128)S(1)} %collective-permute-done.6.one_ref, ...), custom_call_target="tpu_custom_call" | custom-call | tf_op jit(solution)/shard_map/pallas_call | solution.py:578
Async XLA Ops:
  2.1 6.3 %collective-permute-start.1 = (f32[80,128]{1,0:T(8,128)S(1)}, f32[80,128]{1,0:T(8,128)S(1)}, u32[]{:S(2)}, u32[]{:S(2)}) collective-permute-start(f32[80,128]{1,0:T(8,128)S(1)} %get-tuple-element.23.pack_ref), channel_id=1, source_target_pairs={{0,4},{1,2},{2,1},{3,7},{4,0},{5,6},{6,5},{7,3},{8,12},{9,10},{10,... | collective-permute-start | bytes 122888 | tf_op jit(solution)/shard_map/ppermute | solution.py:614
  2.7 6.1 %collective-permute-start = (f32[80,128]{1,0:T(8,128)S(1)}, f32[80,128]{1,0:T(8,128)S(1)}, u32[]{:S(2)}, u32[]{:S(2)}) collective-permute-start(f32[80,128]{1,0:T(8,128)S(1)} %get-tuple-element.23.pack_ref), channel_id=1, source_target_pairs={{0,1},{1,0},{2,3},{3,2},{4,5},{5,4},{6,7},{7,6},{8,9},{9,8},{10,11... | collective-permute-start | bytes 122888 | tf_op jit(solution)/shard_map/ppermute | solution.py:613
  6.8 0.7 %copy-start = (s32[8,128]{1,0:T(8,128)S(1)}, s32[8,128]{1,0:T(8,128)}, u32[]{:S(2)}) copy-start(s32[8,128]{1,0:T(8,128)} %mask_ref.5) | copy-start | bytes 12292
  6.9 4.4 %collective-permute-start.2 = (f32[128,128]{1,0:T(8,128)S(1)}, f32[128,128]{1,0:T(8,128)S(1)}, u32[]{:S(2)}, u32[]{:S(2)}) collective-permute-start(f32[128,128]{1,0:T(8,128)S(1)} %get-tuple-element.28), channel_id=1, source_target_pairs={{0,4},{1,5},{2,6},{3,7},{4,0},{5,1},{6,2},{7,3},{8,12},{9,13},{10,... | collective-permute-start | bytes 196616 | tf_op jit(solution)/shard_map/ppermute | solution.py:616
  7.0 4.3 %collective-permute-start.3 = (f32[128,128]{1,0:T(8,128)S(1)}, f32[128,128]{1,0:T(8,128)S(1)}, u32[]{:S(2)}, u32[]{:S(2)}) collective-permute-start(f32[128,128]{1,0:T(8,128)S(1)} %get-tuple-element.29), channel_id=1, source_target_pairs={{0,1},{1,0},{2,3},{3,2},{4,8},{5,9},{6,10},{7,11},{8,4},{9,5},{10,... | collective-permute-start | bytes 196616 | tf_op jit(solution)/shard_map/ppermute | solution.py:617
  9.2 4.3 %collective-permute-start.4 = (f32[32,128]{1,0:T(8,128)S(1)}, f32[32,128]{1,0:T(8,128)S(1)}, u32[]{:S(2)}, u32[]{:S(2)}) collective-permute-start(f32[32,128]{1,0:T(8,128)S(1)} %get-tuple-element.30), channel_id=1, source_target_pairs={{0,4},{1,5},{2,6},{3,7},{4,0},{5,1},{6,2},{7,3},{8,12},{9,13},{10,... | collective-permute-start | bytes 49160 | tf_op jit(solution)/shard_map/ppermute | solution.py:629
  10.0 3.7 %collective-permute-start.5 = (f32[32,128]{1,0:T(8,128)S(1)}, f32[32,128]{1,0:T(8,128)S(1)}, u32[]{:S(2)}, u32[]{:S(2)}) collective-permute-start(f32[32,128]{1,0:T(8,128)S(1)} %get-tuple-element.31), channel_id=1, source_target_pairs={{0,1},{1,0},{2,3},{3,2},{4,8},{5,9},{6,10},{7,11},{8,4},{9,5},{10,... | collective-permute-start | bytes 49160 | tf_op jit(solution)/shard_map/ppermute | solution.py:630
  11.4 13.4 %collective-permute-start.6 = (f32[304,128]{1,0:T(8,128)S(1)}, f32[304,128]{1,0:T(8,128)S(1)}, u32[]{:S(2)}, u32[]{:S(2)}) collective-permute-start(f32[304,128]{1,0:T(8,128)S(1)} %get-tuple-element.37), channel_id=1, source_target_pairs={{0,4},{1,5},{2,6},{3,7},{4,0},{5,1},{6,2},{7,3},{8,12},{9,13},{10,... | collective-permute-start | bytes 466952 | tf_op jit(solution)/shard_map/ppermute | solution.py:634
  11.9 13.0 %collective-permute-start.7 = (f32[304,128]{1,0:T(8,128)S(1)}, f32[304,128]{1,0:T(8,128)S(1)}, u32[]{:S(2)}, u32[]{:S(2)}) collective-permute-start(f32[304,128]{1,0:T(8,128)S(1)} %get-tuple-element.38), channel_id=1, source_target_pairs={{0,1},{1,0},{2,3},{3,2},{4,8},{5,9},{6,10},{7,11},{8,4},{9,5},{10,... | collective-permute-start | bytes 466952 | tf_op jit(solution)/shard_map/ppermute | solution.py:635

commit v10 on v9

--- a/solution.py
+++ b/solution.py
@@ -393,7 +393,7 @@
         return jnp.sum(x * y, axis=0, keepdims=True)
 
     norm, slope = [jnp.sum(over_rows(v[0], x), axis=1, keepdims=True) for x in v[:2]]
-    theta = jnp.where(norm > 0.0, slope / jnp.where(norm > 0.0, norm, 1.0), 0.0)
+    theta = jnp.where(norm > 0.0, jnp.clip(slope / jnp.where(norm > 0.0, norm, 1.0), -SHIFT, SHIFT), 0.0)
     q = [v[0]] + [v[k] - theta * v[k - 1] for k in range(1, ITERS + 1)]
     for k in range(ITERS):
         basis_ref[tile(k), :] = q[k]

time: 26.2 us -> 26.2 us (level)
  no operation moved by 1% of the time
where the time goes in v10:
time: 26.2 us; the launch traced here: 26 us
  blocking collectives  10.4 us (40%)
  starting transfers between devices  8.49 us (32%)
  Pallas kernels  5.25 us (20%)
  between operations  0.7 us (3%)
  waiting for transfers between devices  0.69 us (3%)
  local copies, waits for them, and re-layouts  0.46 us (2%)
    all_to_all x1, blocking collectives, on_device(): got = lax.all_to_all(sent, axes, 0, 0, tiled=True)  10.4 us
    pallas_call x9, Pallas kernels, call(): pl.pallas_call(kernel, out_shape=[jax.ShapeDtypeStruct(s, F32) for s in o...  5.25 us
    ppermute x1, starting transfers between devices, on_device(): first = lax.ppermute(pack, axes, g_one)  4.15 us
    ppermute x1, starting transfers between devices, on_device(): two = lax.ppermute(two, axes, b_two)  1.19 us
    ppermute x1, starting transfers between devices, on_device(): rest_two = lax.ppermute(rest_two, axes, b_two)  1.19 us
    ppermute x1, starting transfers between devices, on_device(): one = lax.ppermute(one, axes, b_one)  0.87 us
  transfers between devices with their start and end apart: 8, of which 3 were waited for; matrix products, arithmetic and copies ran while one was open for 0% of the time, Pallas kernels for 10%

profile of v10, /device:TPU:0, one launch (start us, length us, event | category | flops | bytes accessed | tf_op | source)
XLA Modules:
  0.0 26.0 jit_solution(13188378646710218149)
XLA Ops:
  0.6 1.5 %shard_map.59 = (f32[1152,128]{1,0:T(8,128)S(1)}, f32[80,128]{1,0:T(8,128)S(1)}, f32[48,128]{1,0:T(8,128)S(1)}) custom-call(f32[1152,128]{1,0:T(8,128)} %bitcast.8, s32[8,128]{1,0:T(8,128)} %mask_ref.5, f32[8,128]{1,0:T(8,128)} %height_hbm.1, f32[8,128]{1,0:T(8,128)} %damp_hbm.1), custom_call_target="tpu_custom_call" | custom-call | tf_op jit(solution)/shard_map/pallas_call | solution.py:578
  2.1 0.5 %collective-permute-start.1 = (f32[80,128]{1,0:T(8,128)S(1)}, f32[80,128]{1,0:T(8,128)S(1)}, u32[]{:S(2)}, u32[]{:S(2)}) collective-permute-start(f32[80,128]{1,0:T(8,128)S(1)} %get-tuple-element.23.pack_ref), channel_id=1, source_target_pairs={{0,4},{1,2},{2,1},{3,7},{4,0},{5,6},{6,5},{7,3},{8,12},{9,10},{10,... | collective-permute-start | bytes 122888 | tf_op jit(solution)/shard_map/ppermute | solution.py:614
  2.7 4.1 %collective-permute-start = (f32[80,128]{1,0:T(8,128)S(1)}, f32[80,128]{1,0:T(8,128)S(1)}, u32[]{:S(2)}, u32[]{:S(2)}) collective-permute-start(f32[80,128]{1,0:T(8,128)S(1)} %get-tuple-element.23.pack_ref), channel_id=1, source_target_pairs={{0,1},{1,0},{2,3},{3,2},{4,5},{5,4},{6,7},{7,6},{8,9},{9,8},{10,11... | collective-permute-start | bytes 122888 | tf_op jit(solution)/shard_map/ppermute | solution.py:613
  6.8 0.0 copy-start
  6.8 0.1 shard_map.62
  6.9 0.1 collective-permute-start.2
  7.0 0.1 collective-permute-start.3
  7.0 0.5 %copy-done = s32[8,128]{1,0:T(8,128)S(1)} copy-done((s32[8,128]{1,0:T(8,128)S(1)}, s32[8,128]{1,0:T(8,128)}, u32[]{:S(2)}) %copy-start) | copy-done | bytes 4120
  7.5 1.0 %shard_map.60 = (f32[1152,128]{1,0:T(8,128)S(1)}, f32[8,128]{1,0:T(8,128)S(1)}) custom-call(f32[1152,128]{1,0:T(8,128)S(1)} %get-tuple-element.24.m_ref, s32[8,128]{1,0:T(8,128)S(1)} %copy-done), custom_call_target="tpu_custom_call" | custom-call | flops 1000000000 | tf_op jit(solution)/shard_map/pallas_call | solution.py:578
  8.5 0.0 collective-permute-done.1.second_ref
  8.5 0.3 %collective-permute-done.first_ref = f32[80,128]{1,0:T(8,128)S(1)} collective-permute-done((f32[80,128]{1,0:T(8,128)S(1)}, f32[80,128]{1,0:T(8,128)S(1)}, u32[]{:S(2)}, u32[]{:S(2)}) %collective-permute-start) | collective-permute-done | bytes 40992 | tf_op jit(solution)/shard_map/ppermute | solution.py:613
  8.8 0.4 %shard_map.61 = (f32[16,128]{1,0:T(8,128)S(1)}, f32[32,128]{1,0:T(8,128)S(1)}, f32[72,128]{1,0:T(8,128)S(1)}, f32[32,128]{1,0:T(8,128)S(1)}, f32[32,128]{1,0:T(8,128)S(1)}) custom-call(f32[80,128]{1,0:T(8,128)S(1)} %get-tuple-element.23.pack_ref, f32[80,128]{1,0:T(8,128)S(1)} %collective-permute-done.first_ref, ...), custom_call_target="tpu_custom_call" | custom-call | flops 10000000000 | tf_op jit(solution)/shard_map/pallas_call | solution.py:578
  9.2 0.9 %collective-permute-start.4 = (f32[32,128]{1,0:T(8,128)S(1)}, f32[32,128]{1,0:T(8,128)S(1)}, u32[]{:S(2)}, u32[]{:S(2)}) collective-permute-start(f32[32,128]{1,0:T(8,128)S(1)} %get-tuple-element.30), channel_id=1, source_target_pairs={{0,4},{1,5},{2,6},{3,7},{4,0},{5,1},{6,2},{7,3},{8,12},{9,13},{10,... | collective-permute-start | bytes 49160 | tf_op jit(solution)/shard_map/ppermute | solution.py:629
  10.0 1.2 %collective-permute-start.5 = (f32[32,128]{1,0:T(8,128)S(1)}, f32[32,128]{1,0:T(8,128)S(1)}, u32[]{:S(2)}, u32[]{:S(2)}) collective-permute-start(f32[32,128]{1,0:T(8,128)S(1)} %get-tuple-element.31), channel_id=1, source_target_pairs={{0,1},{1,0},{2,3},{3,2},{4,8},{5,9},{6,10},{7,11},{8,4},{9,5},{10,... | collective-permute-start | bytes 49160 | tf_op jit(solution)/shard_map/ppermute | solution.py:630
  11.2 0.0 collective-permute-done.2.one_ref.flow_one_ref
  11.2 0.1 collective-permute-done.3.two_ref.flow_two_ref
  11.3 0.1 shard_map.63.cross_ref.after_ref
  11.4 0.1 shard_map.66
  11.4 0.4 %collective-permute-start.6 = (f32[304,128]{1,0:T(8,128)S(1)}, f32[304,128]{1,0:T(8,128)S(1)}, u32[]{:S(2)}, u32[]{:S(2)}) collective-permute-start(f32[304,128]{1,0:T(8,128)S(1)} %get-tuple-element.37), channel_id=1, source_target_pairs={{0,4},{1,5},{2,6},{3,7},{4,0},{5,1},{6,2},{7,3},{8,12},{9,13},{10,... | collective-permute-start | bytes 466952 | tf_op jit(solution)/shard_map/ppermute | solution.py:634
  11.9 1.2 %collective-permute-start.7 = (f32[304,128]{1,0:T(8,128)S(1)}, f32[304,128]{1,0:T(8,128)S(1)}, u32[]{:S(2)}, u32[]{:S(2)}) collective-permute-start(f32[304,128]{1,0:T(8,128)S(1)} %get-tuple-element.38), channel_id=1, source_target_pairs={{0,1},{1,0},{2,3},{3,2},{4,8},{5,9},{6,10},{7,11},{8,4},{9,5},{10,... | collective-permute-start | bytes 466952 | tf_op jit(solution)/shard_map/ppermute | solution.py:635
  13.1 0.4 %shard_map.64 = (f32[1152,128]{1,0:T(8,128)S(1)}, f32[8,128]{1,0:T(8,128)S(1)}) custom-call(f32[80,128]{1,0:T(8,128)S(1)} %get-tuple-element.23.pack_ref, f32[72,128]{1,0:T(8,128)S(1)} %get-tuple-element.32.delta_ref, s32[8,128]{1,0:T(8,128)S(1)} %copy-done, f32[1152,128]{1,0:T(8,128)S(1)} %get-tuple-element.33.part_ref), custom_call_target="tpu_custom_call" | custom-call | flops 1000000000 | tf_op jit(solution)/shard_map/pallas_call | solution.py:578
  13.4 0.0 collective-permute-done.4.one_ref
  13.4 0.3 %collective-permute-done.5.two_ref = f32[32,128]{1,0:T(8,128)S(1)} collective-permute-done((f32[32,128]{1,0:T(8,128)S(1)}, f32[32,128]{1,0:T(8,128)S(1)}, u32[]{:S(2)}, u32[]{:S(2)}) %collective-permute-start.5) | collective-permute-done | bytes 16416 | tf_op jit(solution)/shard_map/ppermute | solution.py:630
  13.8 0.7 %shard_map.65 = (f32[32,128]{1,0:T(8,128)S(1)}, f32[32,128]{1,0:T(8,128)S(1)}) custom-call(f32[48,128]{1,0:T(8,128)S(1)} %get-tuple-element.22.flat_ref, f32[16,128]{1,0:T(8,128)S(1)} %get-tuple-element.26.own_ref, f32[32,128]{1,0:T(8,128)S(1)} %get-tuple-element.27.near_ref, f32[8,128]{1,0:T(8,128)S(1)} %shard_map.63.cross_ref.after_ref, ...), custom_call_target="tpu_custom_call" | custom-call | flops 1000000000 | tf_op jit(solution)/shard_map/pallas_call | solution.py:578
  14.5 10.4 %all_to_all.11 = f32[32,1,128]{2,1,0:T(1,128)S(1)} all-to-all(f32[32,1,128]{2,1,0:T(1,128)S(1)} %bitcast.7), channel_id=1, replica_groups=mesh['blocks'=8,'group'=4] {'blocks','group'}, dimensions={0} | all-to-all | bytes 32768 | tf_op jit(solution)/shard_map/all_to_all | solution.py:651
  24.9 0.0 collective-permute-done.6.one_ref
  24.9 0.0 collective-permute-done.7.two_ref
  24.9 1.1 %shard_map.67 = (f32[1152,128]{1,0:T(8,128)}, f32[8,128]{1,0:T(8,128)}) custom-call(f32[32,128]{1,0:T(8,128)S(1)} %bitcast.6, f32[32,128]{1,0:T(8,128)S(1)} %get-tuple-element.36.basis_ref, f32[1152,128]{1,0:T(8,128)S(1)} %get-tuple-element.24.m_ref, f32[304,128]{1,0:T(8,128)S(1)} %collective-permute-done.6.one_ref, ...), custom_call_target="tpu_custom_call" | custom-call | tf_op jit(solution)/shard_map/pallas_call | solution.py:578
Async XLA Ops:
  2.1 6.3 %collective-permute-start.1 = (f32[80,128]{1,0:T(8,128)S(1)}, f32[80,128]{1,0:T(8,128)S(1)}, u32[]{:S(2)}, u32[]{:S(2)}) collective-permute-start(f32[80,128]{1,0:T(8,128)S(1)} %get-tuple-element.23.pack_ref), channel_id=1, source_target_pairs={{0,4},{1,2},{2,1},{3,7},{4,0},{5,6},{6,5},{7,3},{8,12},{9,10},{10,... | collective-permute-start | bytes 122888 | tf_op jit(solution)/shard_map/ppermute | solution.py:614
  2.7 6.1 %collective-permute-start = (f32[80,128]{1,0:T(8,128)S(1)}, f32[80,128]{1,0:T(8,128)S(1)}, u32[]{:S(2)}, u32[]{:S(2)}) collective-permute-start(f32[80,128]{1,0:T(8,128)S(1)} %get-tuple-element.23.pack_ref), channel_id=1, source_target_pairs={{0,1},{1,0},{2,3},{3,2},{4,5},{5,4},{6,7},{7,6},{8,9},{9,8},{10,11... | collective-permute-start | bytes 122888 | tf_op jit(solution)/shard_map/ppermute | solution.py:613
  6.8 0.7 %copy-start = (s32[8,128]{1,0:T(8,128)S(1)}, s32[8,128]{1,0:T(8,128)}, u32[]{:S(2)}) copy-start(s32[8,128]{1,0:T(8,128)} %mask_ref.5) | copy-start | bytes 12292
  6.9 4.4 %collective-permute-start.2 = (f32[128,128]{1,0:T(8,128)S(1)}, f32[128,128]{1,0:T(8,128)S(1)}, u32[]{:S(2)}, u32[]{:S(2)}) collective-permute-start(f32[128,128]{1,0:T(8,128)S(1)} %get-tuple-element.28), channel_id=1, source_target_pairs={{0,4},{1,5},{2,6},{3,7},{4,0},{5,1},{6,2},{7,3},{8,12},{9,13},{10,... | collective-permute-start | bytes 196616 | tf_op jit(solution)/shard_map/ppermute | solution.py:616
  7.0 4.3 %collective-permute-start.3 = (f32[128,128]{1,0:T(8,128)S(1)}, f32[128,128]{1,0:T(8,128)S(1)}, u32[]{:S(2)}, u32[]{:S(2)}) collective-permute-start(f32[128,128]{1,0:T(8,128)S(1)} %get-tuple-element.29), channel_id=1, source_target_pairs={{0,1},{1,0},{2,3},{3,2},{4,8},{5,9},{6,10},{7,11},{8,4},{9,5},{10,... | collective-permute-start | bytes 196616 | tf_op jit(solution)/shard_map/ppermute | solution.py:617
  9.2 4.3 %collective-permute-start.4 = (f32[32,128]{1,0:T(8,128)S(1)}, f32[32,128]{1,0:T(8,128)S(1)}, u32[]{:S(2)}, u32[]{:S(2)}) collective-permute-start(f32[32,128]{1,0:T(8,128)S(1)} %get-tuple-element.30), channel_id=1, source_target_pairs={{0,4},{1,5},{2,6},{3,7},{4,0},{5,1},{6,2},{7,3},{8,12},{9,13},{10,... | collective-permute-start | bytes 49160 | tf_op jit(solution)/shard_map/ppermute | solution.py:629
  10.0 3.7 %collective-permute-start.5 = (f32[32,128]{1,0:T(8,128)S(1)}, f32[32,128]{1,0:T(8,128)S(1)}, u32[]{:S(2)}, u32[]{:S(2)}) collective-permute-start(f32[32,128]{1,0:T(8,128)S(1)} %get-tuple-element.31), channel_id=1, source_target_pairs={{0,1},{1,0},{2,3},{3,2},{4,8},{5,9},{6,10},{7,11},{8,4},{9,5},{10,... | collective-permute-start | bytes 49160 | tf_op jit(solution)/shard_map/ppermute | solution.py:630
  11.4 13.4 %collective-permute-start.6 = (f32[304,128]{1,0:T(8,128)S(1)}, f32[304,128]{1,0:T(8,128)S(1)}, u32[]{:S(2)}, u32[]{:S(2)}) collective-permute-start(f32[304,128]{1,0:T(8,128)S(1)} %get-tuple-element.37), channel_id=1, source_target_pairs={{0,4},{1,5},{2,6},{3,7},{4,0},{5,1},{6,2},{7,3},{8,12},{9,13},{10,... | collective-permute-start | bytes 466952 | tf_op jit(solution)/shard_map/ppermute | solution.py:634
  11.9 13.0 %collective-permute-start.7 = (f32[304,128]{1,0:T(8,128)S(1)}, f32[304,128]{1,0:T(8,128)S(1)}, u32[]{:S(2)}, u32[]{:S(2)}) collective-permute-start(f32[304,128]{1,0:T(8,128)S(1)} %get-tuple-element.38), channel_id=1, source_target_pairs={{0,1},{1,0},{2,3},{3,2},{4,8},{5,9},{6,10},{7,11},{8,4},{9,5},{10,... | collective-permute-start | bytes 466952 | tf_op jit(solution)/shard_map/ppermute | solution.py:635

commit v11 on v10

--- a/solution.py
+++ b/solution.py
@@ -223,14 +223,12 @@
     own_ref[0:ROWS, :] = strip
     own_ref[ROWS : 2 * ROWS, :] = inner
 
-    def fill(low_ref, high_ref):
-        for ref, rows in ((low_ref, slice(0, lay.pad)), (high_ref, slice(lay.pad, 2 * lay.pad))):
-            ref[pl.ds(lay.edge, lay.pad), :] = near_ref[rows, :]
-            ref[pl.ds(lay.strip, ROWS), :] = strip
-            ref[pl.ds(lay.inner, ROWS), :] = inner
-
-    pl.when(at.b_even)(lambda: fill(two_ref, one_ref))
-    pl.when(jnp.logical_not(at.b_even))(lambda: fill(one_ref, two_ref))
+    low, high = near_ref[0 : lay.pad, :], near_ref[lay.pad :, :]
+    one_ref[pl.ds(lay.edge, lay.pad), :] = jnp.where(at.b_even, high, low)
+    two_ref[pl.ds(lay.edge, lay.pad), :] = jnp.where(at.b_even, low, high)
+    for ref in (one_ref, two_ref):
+        ref[pl.ds(lay.strip, ROWS), :] = strip
+        ref[pl.ds(lay.inner, ROWS), :] = inner
 
 
 def level_rows(m_ref, comp, row):
@@ -384,10 +382,13 @@
     divergence = 0.5 * (roll(east, -1, 0) - roll(east, 1, 0) + roll(north, -1, 1) - roll(north, 1, 1))
     v = [forcing - gravity * sea * divergence]
     own_diagonal = diagonal - SHIFT
-    for _ in range(ITERS):
+    for _ in range(ITERS - 1):
         x = v[-1]
         v.append(own_diagonal * x - sea * (both(x, 1, 0) + both(x, 1, 1)))
-    v = [x[ROWS : 2 * ROWS, 0:LANES] for x in v]
+    x, middle = v[-1], slice(ROWS, 2 * ROWS)
+    beside = both(x[:, 0:LANES], 1, 0)[middle] + both(x[middle], 1, 1)[:, 0:LANES]
+    v = [x[middle, 0:LANES] for x in v]
+    v.append(own_diagonal[middle, 0:LANES] * v[-1] - sea[middle, 0:LANES] * beside)
 
     def over_rows(x, y):
         return jnp.sum(x * y, axis=0, keepdims=True)
@@ -593,6 +594,8 @@
     lay = Layout(state.shape[0] // ROWS)
     g_one, g_two = swap_pairs(shape, "group")
     b_one, b_two = swap_pairs(shape, "blocks")
+    ends = (0, nb - 1)
+    f_two = [(i, j if i // ng not in ends else (nb - 1 - i // ng) * ng + i % ng) for i, j in b_two]
     one_tile = (ROWS, LANES)
     packed = (lay.packs * ROWS, LANES)
     flats = (FLAT * ROWS, LANES)
@@ -614,7 +617,7 @@
     second = lax.ppermute(pack, axes, g_two)
     flow_one, flow_two = call(flow_kernel, [(lay.early, LANES)] * 2, m, flat)
     flow_one = lax.ppermute(flow_one, axes, b_one)
-    flow_two = lax.ppermute(flow_two, axes, b_two)
+    flow_two = lax.ppermute(flow_two, axes, f_two)
     part, inner_done = call(inner_kernel, [state.shape, one_tile], m, land_mask, flops=LONG)
     message = (lay.message, LANES)
     own, near, delta, one, two = call(

time: 26.2 us -> 26.2 us (level)
  blocking collectives: 10.4 us -> 9.49 us
  waiting for transfers between devices: 0.69 us -> 1.51 us
  starting transfers between devices: 8.49 us -> 9.03 us
  local copies, waits for them, and re-layouts: 0.46 us -> 0.01 us
    ppermute x1, starting transfers between devices: 0.07 us -> 2.55 us  [on_device(): flow_two = lax.ppermute(flow_two, axes, f_two)]
    all_to_all x1, blocking collectives: 10.4 us -> 9.49 us  [on_device(): got = lax.all_to_all(sent, axes, 0, 0, tiled=True)]
    ppermute x1, starting transfers between devices: 1.19 us -> 0.32 us  [on_device(): two = lax.ppermute(two, axes, b_two)]
    ppermute x1, starting transfers between devices: 0.87 us -> 0.01 us  [on_device(): one = lax.ppermute(one, axes, b_one)]
    ppermute x1, waiting for transfers between devices: 0.33 us -> 1.02 us  [on_device(): two = lax.ppermute(two, axes, b_two)]
    unnamed x2, local copies, waits for them, and re-layouts: 0.46 us -> 0.01 us
    ppermute x1, waiting for transfers between devices: 0.06 us -> 0.47 us  [on_device(): flow_two = lax.ppermute(flow_two, axes, f_two)]
    ppermute x1, waiting for transfers between devices: 0.29 us -> 0.01 us  [on_device(): first = lax.ppermute(pack, axes, g_one)]
  transfers between devices with their start and end apart: 8 -> 8, of which waited for: 3 -> 2; matrix products, arithmetic and copies ran while one was open for 0% -> 0% of each run, Pallas kernels for 10% -> 10%
where the time goes in v11:
time: 26.2 us; the launch traced here: 26 us
  blocking collectives  9.49 us (36%)
  starting transfers between devices  9.03 us (34%)
  Pallas kernels  5.25 us (20%)
  waiting for transfers between devices  1.51 us (6%)
  between operations  0.7 us (3%)
    all_to_all x1, blocking collectives, on_device(): got = lax.all_to_all(sent, axes, 0, 0, tiled=True)  9.49 us
    pallas_call x9, Pallas kernels, call(): pl.pallas_call(kernel, out_shape=[jax.ShapeDtypeStruct(s, F32) for s in o...  5.25 us
    ppermute x1, starting transfers between devices, on_device(): first = lax.ppermute(pack, axes, g_one)  4.15 us
    ppermute x1, starting transfers between devices, on_device(): flow_two = lax.ppermute(flow_two, axes, f_two)  2.55 us
    ppermute x1, starting transfers between devices, on_device(): rest_two = lax.ppermute(rest_two, axes, b_two)  1.25 us
    ppermute x1, waiting for transfers between devices, on_device(): two = lax.ppermute(two, axes, b_two)  1.02 us
  transfers between devices with their start and end apart: 8, of which 2 were waited for; matrix products, arithmetic and copies ran while one was open for 0% of the time, Pallas kernels for 10%

profile of v11, /device:TPU:0, one launch (start us, length us, event | category | flops | bytes accessed | tf_op | source)
XLA Modules:
  0.0 26.0 jit_solution(3370065659554086415)
XLA Ops:
  0.6 1.5 %shard_map.59 = (f32[1152,128]{1,0:T(8,128)S(1)}, f32[80,128]{1,0:T(8,128)S(1)}, f32[48,128]{1,0:T(8,128)S(1)}) custom-call(f32[1152,128]{1,0:T(8,128)} %bitcast.8, s32[8,128]{1,0:T(8,128)} %mask_ref.5, f32[8,128]{1,0:T(8,128)} %height_hbm.1, f32[8,128]{1,0:T(8,128)} %damp_hbm.1), custom_call_target="tpu_custom_call" | custom-call | tf_op jit(solution)/shard_map/pallas_call | solution.py:579
  2.1 0.5 %collective-permute-start.1 = (f32[80,128]{1,0:T(8,128)S(1)}, f32[80,128]{1,0:T(8,128)S(1)}, u32[]{:S(2)}, u32[]{:S(2)}) collective-permute-start(f32[80,128]{1,0:T(8,128)S(1)} %get-tuple-element.23.pack_ref), channel_id=1, source_target_pairs={{0,4},{1,2},{2,1},{3,7},{4,0},{5,6},{6,5},{7,3},{8,12},{9,10},{10,... | collective-permute-start | bytes 122888 | tf_op jit(solution)/shard_map/ppermute | solution.py:617
  2.7 4.1 %collective-permute-start = (f32[80,128]{1,0:T(8,128)S(1)}, f32[80,128]{1,0:T(8,128)S(1)}, u32[]{:S(2)}, u32[]{:S(2)}) collective-permute-start(f32[80,128]{1,0:T(8,128)S(1)} %get-tuple-element.23.pack_ref), channel_id=1, source_target_pairs={{0,1},{1,0},{2,3},{3,2},{4,5},{5,4},{6,7},{7,6},{8,9},{9,8},{10,11... | collective-permute-start | bytes 122888 | tf_op jit(solution)/shard_map/ppermute | solution.py:616
  6.8 0.0 copy-start
  6.8 0.1 shard_map.62
  6.9 0.1 collective-permute-start.2
  7.0 2.5 %collective-permute-start.3 = (f32[128,128]{1,0:T(8,128)S(1)}, f32[128,128]{1,0:T(8,128)S(1)}, u32[]{:S(2)}, u32[]{:S(2)}) collective-permute-start(f32[128,128]{1,0:T(8,128)S(1)} %get-tuple-element.29), channel_id=1, source_target_pairs={{0,28},{1,29},{2,30},{3,31},{4,8},{5,9},{6,10},{7,11},{8,4},{9,5},... | collective-permute-start | bytes 196616 | tf_op jit(solution)/shard_map/ppermute | solution.py:620
  9.5 0.0 copy-done
  9.5 1.0 %shard_map.60 = (f32[1152,128]{1,0:T(8,128)S(1)}, f32[8,128]{1,0:T(8,128)S(1)}) custom-call(f32[1152,128]{1,0:T(8,128)S(1)} %get-tuple-element.24.m_ref, s32[8,128]{1,0:T(8,128)S(1)} %copy-done), custom_call_target="tpu_custom_call" | custom-call | flops 1000000000 | tf_op jit(solution)/shard_map/pallas_call | solution.py:579
  10.5 0.0 collective-permute-done.1.second_ref
  10.5 0.0 collective-permute-done.first_ref
  10.5 0.4 %shard_map.61 = (f32[16,128]{1,0:T(8,128)S(1)}, f32[32,128]{1,0:T(8,128)S(1)}, f32[72,128]{1,0:T(8,128)S(1)}, f32[32,128]{1,0:T(8,128)S(1)}, f32[32,128]{1,0:T(8,128)S(1)}) custom-call(f32[80,128]{1,0:T(8,128)S(1)} %get-tuple-element.23.pack_ref, f32[80,128]{1,0:T(8,128)S(1)} %collective-permute-done.first_ref, ...), custom_call_target="tpu_custom_call" | custom-call | flops 10000000000 | tf_op jit(solution)/shard_map/pallas_call | solution.py:579
  10.9 0.0 collective-permute-start.4
  10.9 0.3 %collective-permute-start.5 = (f32[32,128]{1,0:T(8,128)S(1)}, f32[32,128]{1,0:T(8,128)S(1)}, u32[]{:S(2)}, u32[]{:S(2)}) collective-permute-start(f32[32,128]{1,0:T(8,128)S(1)} %get-tuple-element.31), channel_id=1, source_target_pairs={{0,1},{1,0},{2,3},{3,2},{4,8},{5,9},{6,10},{7,11},{8,4},{9,5},{10,... | collective-permute-start | bytes 49160 | tf_op jit(solution)/shard_map/ppermute | solution.py:633
  11.2 0.0 collective-permute-done.2.one_ref.flow_one_ref
  11.2 0.5 %collective-permute-done.3.two_ref.flow_two_ref = f32[128,128]{1,0:T(8,128)S(1)} collective-permute-done((f32[128,128]{1,0:T(8,128)S(1)}, f32[128,128]{1,0:T(8,128)S(1)}, u32[]{:S(2)}, u32[]{:S(2)}) %collective-permute-start.3) | collective-permute-done | bytes 65568 | tf_op jit(solution)/shard_map/ppermute | solution.py:620
  11.7 0.1 shard_map.63.cross_ref.after_ref
  11.8 0.1 shard_map.66
  11.9 0.2 collective-permute-start.6
  12.0 1.3 %collective-permute-start.7 = (f32[304,128]{1,0:T(8,128)S(1)}, f32[304,128]{1,0:T(8,128)S(1)}, u32[]{:S(2)}, u32[]{:S(2)}) collective-permute-start(f32[304,128]{1,0:T(8,128)S(1)} %get-tuple-element.38), channel_id=1, source_target_pairs={{0,1},{1,0},{2,3},{3,2},{4,8},{5,9},{6,10},{7,11},{8,4},{9,5},{10,... | collective-permute-start | bytes 466952 | tf_op jit(solution)/shard_map/ppermute | solution.py:638
  13.3 0.4 %shard_map.64 = (f32[1152,128]{1,0:T(8,128)S(1)}, f32[8,128]{1,0:T(8,128)S(1)}) custom-call(f32[80,128]{1,0:T(8,128)S(1)} %get-tuple-element.23.pack_ref, f32[72,128]{1,0:T(8,128)S(1)} %get-tuple-element.32.delta_ref, s32[8,128]{1,0:T(8,128)S(1)} %copy-done, f32[1152,128]{1,0:T(8,128)S(1)} %get-tuple-element.33.part_ref), custom_call_target="tpu_custom_call" | custom-call | flops 1000000000 | tf_op jit(solution)/shard_map/pallas_call | solution.py:579
  13.6 0.0 collective-permute-done.4.one_ref
  13.7 1.0 %collective-permute-done.5.two_ref = f32[32,128]{1,0:T(8,128)S(1)} collective-permute-done((f32[32,128]{1,0:T(8,128)S(1)}, f32[32,128]{1,0:T(8,128)S(1)}, u32[]{:S(2)}, u32[]{:S(2)}) %collective-permute-start.5) | collective-permute-done | bytes 16416 | tf_op jit(solution)/shard_map/ppermute | solution.py:633
  14.7 0.7 %shard_map.65 = (f32[32,128]{1,0:T(8,128)S(1)}, f32[32,128]{1,0:T(8,128)S(1)}) custom-call(f32[48,128]{1,0:T(8,128)S(1)} %get-tuple-element.22.flat_ref, f32[16,128]{1,0:T(8,128)S(1)} %get-tuple-element.26.own_ref, f32[32,128]{1,0:T(8,128)S(1)} %get-tuple-element.27.near_ref, f32[8,128]{1,0:T(8,128)S(1)} %shard_map.63.cross_ref.after_ref, ...), custom_call_target="tpu_custom_call" | custom-call | flops 1000000000 | tf_op jit(solution)/shard_map/pallas_call | solution.py:579
  15.4 9.5 %all_to_all.11 = f32[32,1,128]{2,1,0:T(1,128)S(1)} all-to-all(f32[32,1,128]{2,1,0:T(1,128)S(1)} %bitcast.7), channel_id=1, replica_groups=mesh['blocks'=8,'group'=4] {'blocks','group'}, dimensions={0} | all-to-all | bytes 32768 | tf_op jit(solution)/shard_map/all_to_all | solution.py:654
  24.9 0.0 collective-permute-done.6.one_ref
  24.9 0.0 collective-permute-done.7.two_ref
  24.9 1.1 %shard_map.67 = (f32[1152,128]{1,0:T(8,128)}, f32[8,128]{1,0:T(8,128)}) custom-call(f32[32,128]{1,0:T(8,128)S(1)} %bitcast.6, f32[32,128]{1,0:T(8,128)S(1)} %get-tuple-element.36.basis_ref, f32[1152,128]{1,0:T(8,128)S(1)} %get-tuple-element.24.m_ref, f32[304,128]{1,0:T(8,128)S(1)} %collective-permute-done.6.one_ref, ...), custom_call_target="tpu_custom_call" | custom-call | tf_op jit(solution)/shard_map/pallas_call | solution.py:579
Async XLA Ops:
  2.1 8.4 %collective-permute-start.1 = (f32[80,128]{1,0:T(8,128)S(1)}, f32[80,128]{1,0:T(8,128)S(1)}, u32[]{:S(2)}, u32[]{:S(2)}) collective-permute-start(f32[80,128]{1,0:T(8,128)S(1)} %get-tuple-element.23.pack_ref), channel_id=1, source_target_pairs={{0,4},{1,2},{2,1},{3,7},{4,0},{5,6},{6,5},{7,3},{8,12},{9,10},{10,... | collective-permute-start | bytes 122888 | tf_op jit(solution)/shard_map/ppermute | solution.py:617
  2.7 7.8 %collective-permute-start = (f32[80,128]{1,0:T(8,128)S(1)}, f32[80,128]{1,0:T(8,128)S(1)}, u32[]{:S(2)}, u32[]{:S(2)}) collective-permute-start(f32[80,128]{1,0:T(8,128)S(1)} %get-tuple-element.23.pack_ref), channel_id=1, source_target_pairs={{0,1},{1,0},{2,3},{3,2},{4,5},{5,4},{6,7},{7,6},{8,9},{9,8},{10,11... | collective-permute-start | bytes 122888 | tf_op jit(solution)/shard_map/ppermute | solution.py:616
  6.8 2.7 %copy-start = (s32[8,128]{1,0:T(8,128)S(1)}, s32[8,128]{1,0:T(8,128)}, u32[]{:S(2)}) copy-start(s32[8,128]{1,0:T(8,128)} %mask_ref.5) | copy-start | bytes 12292
  6.9 4.3 %collective-permute-start.2 = (f32[128,128]{1,0:T(8,128)S(1)}, f32[128,128]{1,0:T(8,128)S(1)}, u32[]{:S(2)}, u32[]{:S(2)}) collective-permute-start(f32[128,128]{1,0:T(8,128)S(1)} %get-tuple-element.28), channel_id=1, source_target_pairs={{0,4},{1,5},{2,6},{3,7},{4,0},{5,1},{6,2},{7,3},{8,12},{9,13},{10,... | collective-permute-start | bytes 196616 | tf_op jit(solution)/shard_map/ppermute | solution.py:619
  7.0 4.7 %collective-permute-start.3 = (f32[128,128]{1,0:T(8,128)S(1)}, f32[128,128]{1,0:T(8,128)S(1)}, u32[]{:S(2)}, u32[]{:S(2)}) collective-permute-start(f32[128,128]{1,0:T(8,128)S(1)} %get-tuple-element.29), channel_id=1, source_target_pairs={{0,28},{1,29},{2,30},{3,31},{4,8},{5,9},{6,10},{7,11},{8,4},{9,5},... | collective-permute-start | bytes 196616 | tf_op jit(solution)/shard_map/ppermute | solution.py:620
  10.9 2.7 %collective-permute-start.4 = (f32[32,128]{1,0:T(8,128)S(1)}, f32[32,128]{1,0:T(8,128)S(1)}, u32[]{:S(2)}, u32[]{:S(2)}) collective-permute-start(f32[32,128]{1,0:T(8,128)S(1)} %get-tuple-element.30), channel_id=1, source_target_pairs={{0,4},{1,5},{2,6},{3,7},{4,0},{5,1},{6,2},{7,3},{8,12},{9,13},{10,... | collective-permute-start | bytes 49160 | tf_op jit(solution)/shard_map/ppermute | solution.py:632
  10.9 3.8 %collective-permute-start.5 = (f32[32,128]{1,0:T(8,128)S(1)}, f32[32,128]{1,0:T(8,128)S(1)}, u32[]{:S(2)}, u32[]{:S(2)}) collective-permute-start(f32[32,128]{1,0:T(8,128)S(1)} %get-tuple-element.31), channel_id=1, source_target_pairs={{0,1},{1,0},{2,3},{3,2},{4,8},{5,9},{6,10},{7,11},{8,4},{9,5},{10,... | collective-permute-start | bytes 49160 | tf_op jit(solution)/shard_map/ppermute | solution.py:633
  11.9 13.0 %collective-permute-start.6 = (f32[304,128]{1,0:T(8,128)S(1)}, f32[304,128]{1,0:T(8,128)S(1)}, u32[]{:S(2)}, u32[]{:S(2)}) collective-permute-start(f32[304,128]{1,0:T(8,128)S(1)} %get-tuple-element.37), channel_id=1, source_target_pairs={{0,4},{1,5},{2,6},{3,7},{4,0},{5,1},{6,2},{7,3},{8,12},{9,13},{10,... | collective-permute-start | bytes 466952 | tf_op jit(solution)/shard_map/ppermute | solution.py:637
  12.0 12.8 %collective-permute-start.7 = (f32[304,128]{1,0:T(8,128)S(1)}, f32[304,128]{1,0:T(8,128)S(1)}, u32[]{:S(2)}, u32[]{:S(2)}) collective-permute-start(f32[304,128]{1,0:T(8,128)S(1)} %get-tuple-element.38), channel_id=1, source_target_pairs={{0,1},{1,0},{2,3},{3,2},{4,8},{5,9},{6,10},{7,11},{8,4},{9,5},{10,... | collective-permute-start | bytes 466952 | tf_op jit(solution)/shard_map/ppermute | solution.py:638
